TPU v7x, 512 devices: a whole 4x8x8 slice. The times are simulated.
512 devices in a mesh: wide: 64 (over z, x, core), narrow: 8 (over y).
Axes of the slice: x: 4, y: 8, z: 8, core: 2. Of those that a mesh axis runs over, the one named last changes fastest.
Arguments:
- fields: float32 [2, 64, 2048, 1024], P(None, 'narrow', 'wide'), may hold values from -6 to 6
- field_bins: int32 [2, 64, 2048, 1024], P(None, 'narrow', 'wide'), may hold values from 0 to 255
- colour_table: bfloat16 [2, 3, 256], replicated, may hold values from 0.049804688 to 1
- opacity_table: bfloat16 [2, 256], replicated, may hold values from 0.00049972534 to 0.0099487305
- view_dir: int32 [2048], P('wide'), may hold values from 0 to 1
Outputs:
- frame: float32 [4, 2048, 1024], P(None, None, 'narrow')
Inputs may be any that keep to these rules, and one draw needn't show every extreme that they name: `view_dir`: 0: the column's rays travel toward increasing depth index; 1: toward decreasing depth index.
All inputs are finite; a program needn't handle non-finite values.
Results may differ from a plain program's by a relative error of at most 0.0003.
Values sent between devices are 32-bit elements; how exact they have to be, the bound alone decides.
No kernel may reach another device: no remote copies, remote signals or barrier semaphores. Data moves between devices by JAX's collectives and lax.ppermute only.
A program may use at most 64 MiB of HBM per device.

v0:
```python
import math

import jax
import jax.numpy as jnp
from jax import lax
from jax.sharding import PartitionSpec as P


def extended(cells, sides, width):
    for axis, dim in sides:
        count = lax.axis_size(axis)
        ends = count - 1
        head = lax.slice_in_dim(cells, 0, width, axis=dim)
        tail = lax.slice_in_dim(cells, cells.shape[dim] - width, cells.shape[dim], axis=dim)
        cells = jnp.concatenate(
            [
                lax.ppermute(tail, axis, [(i, (i + 1) % count) for i in range(ends)]),
                cells,
                lax.ppermute(head, axis, [((i + 1) % count, i) for i in range(ends)]),
            ],
            axis=dim,
        )
    return cells


def partner(block, axis, distance):
    count = lax.axis_size(axis)
    route = []
    for low in range(count):
        high = low | 1 << distance
        if high != low and high < count:
            route += [(low, high), (high, low)]
    return lax.ppermute(block, axis, route)


def gradient_terms(padded):
    grad_depth = 0.5 * (padded[:, 2:, 1:-1, 1:-1] - padded[:, :-2, 1:-1, 1:-1])
    grad_column = 0.5 * (padded[:, 1:-1, 2:, 1:-1] - padded[:, 1:-1, :-2, 1:-1])
    grad_row = 0.5 * (padded[:, 1:-1, 1:-1, 2:] - padded[:, 1:-1, 1:-1, :-2])
    square = grad_depth * grad_depth + grad_column * grad_column + grad_row * grad_row
    shading = 0.3 + 0.7 * jnp.abs(grad_depth) / jnp.sqrt(square + 1.0)
    return (shading, 0.25 + jnp.sqrt(square))


def make_sample(shading, opacity_gain, looked_up):
    opacity = looked_up[:, 3] * opacity_gain
    colour = opacity[0] * shading[0] * looked_up[0, :3] + opacity[1] * shading[1] * looked_up[1, :3]
    combined = 1.0 - (1.0 - opacity[0]) * (1.0 - opacity[1])
    return jnp.concatenate([colour, combined[None]], axis=0)


def blend_over(nearer, behind):
    return nearer + (1.0 - nearer[3:4]) * behind


def lookup(table_rows, bins_now):
    columns, row_count = bins_now.shape
    group = math.gcd(columns, 8)
    blocks = bins_now.reshape(columns // group, group * row_count)
    bin_index = lax.broadcasted_iota(jnp.int32, (table_rows.shape[1], 1), 0)

    def one_block(block_bins):
        one_hot = (block_bins.reshape(1, -1) == bin_index).astype(jnp.bfloat16)
        return jnp.dot(table_rows, one_hot, preferred_element_type=jnp.float32)

    looked = lax.map(one_block, blocks)
    return jnp.transpose(looked, (1, 0, 2)).reshape(4, columns, row_count)


def on_device(fields, field_bins, colour_table, opacity_table, view_dir):
    ghosted = extended(fields, (("wide", 2), ("narrow", 1)), 1)
    padded = jnp.pad(ghosted, ((0, 0), (0, 0), (0, 0), (1, 1)))
    shading, opacity_gain = gradient_terms(padded)
    tables = jnp.concatenate([colour_table, opacity_table[:, None, :]], axis=1)
    backward = view_dir == 1
    flip_mask = backward[None, None, :, None]
    shading = jnp.where(flip_mask, jnp.flip(shading, 1), shading)
    opacity_gain = jnp.where(flip_mask, jnp.flip(opacity_gain, 1), opacity_gain)
    bins_used = jnp.where(flip_mask, jnp.flip(field_bins, 1), field_bins)
    depth_count, columns, row_count = (fields.shape[1], fields.shape[2], fields.shape[3])

    def march_step(running, order_step):
        shade_now = lax.dynamic_index_in_dim(shading, order_step, 1, keepdims=False)
        gain_now = lax.dynamic_index_in_dim(opacity_gain, order_step, 1, keepdims=False)
        bins_now = lax.dynamic_index_in_dim(bins_used, order_step, 1, keepdims=False)
        looked_up = jnp.stack([lookup(tables[0], bins_now[0]), lookup(tables[1], bins_now[1])])
        return (blend_over(running, make_sample(shade_now, gain_now, looked_up)), None)

    start = jnp.zeros((4, columns, row_count), jnp.float32)
    brick_image, unused = lax.scan(march_step, start, jnp.arange(depth_count, dtype=jnp.int32))
    narrow_count = lax.axis_size("narrow")
    band_rows = row_count // narrow_count
    position = lax.axis_index("narrow")
    current = brick_image.reshape(4, columns, narrow_count, band_rows)
    column_back = backward[None, :, None, None]
    levels = narrow_count.bit_length() - 1
    for level in range(levels):
        band_count = current.shape[2]
        halves = current.reshape(4, columns, band_count // 2, 2, band_rows)
        own_bit = position // 2**level % 2
        kept_half = lax.dynamic_index_in_dim(halves, own_bit, 3, keepdims=False)
        sent_half = lax.dynamic_index_in_dim(halves, 1 - own_bit, 3, keepdims=False)
        got_half = partner(sent_half, "narrow", level)
        in_front = (own_bit == 0) != column_back
        nearer = jnp.where(in_front, kept_half, got_half)
        behind = jnp.where(in_front, got_half, kept_half)
        current = blend_over(nearer, behind)
    finished = current[:, :, 0]
    return lax.all_gather(finished, "wide", axis=1, tiled=True)


def solution(mesh):
    in_specs = (
        P(None, "narrow", "wide", None),
        P(None, "narrow", "wide", None),
        P(),
        P(),
        P("wide"),
    )
    out_specs = P(None, None, "narrow")
    return jax.shard_map(
        on_device, mesh=mesh, in_specs=in_specs, out_specs=out_specs, check_vma=False
    )
```

profile of v0, /device:TPU:1, one launch (start us, length us, event | category | flops | bytes accessed | tf_op | source)
XLA Modules:
  0.0 328.2 jit_solution(666253449698779306)
XLA Ops:
  6.5 1.4 fusion.33
  8.0 4.5 %collective-permute-start = (f32[2,8,1,1024]{3,2,1,0:T(1,128)S(1)}, f32[2,8,1,1024]{3,2,1,0:T(1,128)S(1)}, u32[]{:S(2)}, u32[]{:S(2)}) collective-permute-start(f32[2,8,1,1024]{3,2,1,0:T(1,128)S(1)} %get-tuple-element.184), channel_id=1, source_target_pairs={{0,8},{8,16},{16,24},{24,32},{32,40},{40,48},{48,56},{56,64},{64,7... | collective-permute-start | bytes 196616 | tf_op jit(solution)/shard_map/ppermute | solution.py:17
  12.5 5.6 %collective-permute-start.1 = (f32[2,8,1,1024]{3,2,1,0:T(1,128)S(1)}, f32[2,8,1,1024]{3,2,1,0:T(1,128)S(1)}, u32[]{:S(2)}, u32[]{:S(2)}) collective-permute-start(f32[2,8,1,1024]{3,2,1,0:T(1,128)S(1)} %get-tuple-element.185), channel_id=1, source_target_pairs={{8,0},{16,8},{24,16},{32,24},{40,32},{48,40},{56,48},{64,56},{72,6... | collective-permute-start | bytes 196616 | tf_op jit(solution)/shard_map/ppermute | solution.py:19
  22.7 4.0 %collective-permute-start.3 = (f32[2,1,34,1024]{3,2,1,0:T(8,128)S(1)}, f32[2,1,34,1024]{3,2,1,0:T(8,128)S(1)}, u32[]{:S(2)}, u32[]{:S(2)}) collective-permute-start(f32[2,1,34,1024]{3,2,1,0:T(8,128)S(1)} %get-tuple-element.183), channel_id=1, source_target_pairs={{0,1},{1,2},{2,3},{3,4},{4,5},{5,6},{6,7},{8,9},{9,10},{10,11},{11... | collective-permute-start | bytes 835592 | tf_op jit(solution)/shard_map/ppermute | solution.py:17
  26.7 1.6 reverse_select_fusion
  28.3 4.4 %collective-permute-done.2 = f32[2,1,34,1024]{3,2,1,0:T(8,128)S(1)} collective-permute-done((f32[2,1,34,1024]{3,2,1,0:T(8,128)S(1)}, f32[2,1,34,1024]{3,2,1,0:T(8,128)S(1)}, u32[]{:S(2)}, u32[]{:S(2)}) %collective-permute-start.2) | collective-permute-done | bytes 278560 | tf_op jit(solution)/shard_map/ppermute | solution.py:19
  32.7 1.4 collective-permute-done.3
  34.1 2.3 select_maximum_fusion
  36.4 2.4 rsqrt_multiply_fusion
  39.3 2.6 add_select_fusion
  41.9 152.9 %while.37 = (s32[]{:T(128)}, f32[4,32,1024]{2,1,0:T(8,128)S(1)}, s32[8]{0:T(128)S(1)}, s32[2,8,32,1024]{3,2,1,0:T(8,128)}, bf16[2,4,256]{2,1,0:T(4,128)(2,1)S(1)...) while((s32[]{:T(128)}, f32[4,32,1024]{2,1,0:T(8,128)S(1)}, ...), condition=%wide.region_5.6_spmd.clone, body=%wide.region_0.5_spmd.clone.sunk | while | flops 39059460 | bytes 13709776 | solution.py:90
  45.8 5.6 %while.38 = (s32[]{:T(128)}, f32[4,4,8192]{2,1,0:T(4,128)S(1)}, s32[4,8192]{1,0:T(4,128)S(1)}, bf16[4,256]{1,0:T(4,128)(2,1)S(1)}, s32[]{:T(128)}) while((s32[]{:T(128)}, f32[4,4,8192]{2,1,0:T(4,128)S(1)}, s32[4,8192]{1,0:T(4,128)S(1)}, bf16[4,256]{1,0:T(4,128)(2,1)S(1)}, s32[]{:T(128)}) %tuple.80), condition=%wide.region_4.4_spmd.clone, body=%wide.region_3.3_spmd.clone.sunk | while | flops 18874368 | bytes 231493 | solution.py:66
  45.8 1.4 fusion.51
  47.2 1.4 fusion.51
  48.6 1.4 fusion.51
  50.0 1.4 fusion.51
  52.3 5.6 %while.39 = (s32[]{:T(128)}, f32[4,4,8192]{2,1,0:T(4,128)S(1)}, s32[4,8192]{1,0:T(4,128)S(1)}, bf16[4,256]{1,0:T(4,128)(2,1)S(1)}, s32[]{:T(128)}) while((s32[]{:T(128)}, f32[4,4,8192]{2,1,0:T(4,128)S(1)}, s32[4,8192]{1,0:T(4,128)S(1)}, bf16[4,256]{1,0:T(4,128)(2,1)S(1)}, s32[]{:T(128)}) %tuple.83), condition=%wide.region_2.2_spmd.clone, body=%wide.region_1.1_spmd.clone.sunk | while | flops 18874368 | bytes 231493 | solution.py:66
  52.4 1.4 fusion.53
  53.8 1.4 fusion.53
  55.2 1.4 fusion.53
  56.6 1.4 fusion.53
  64.9 5.6 %while.38 = (s32[]{:T(128)}, f32[4,4,8192]{2,1,0:T(4,128)S(1)}, s32[4,8192]{1,0:T(4,128)S(1)}, bf16[4,256]{1,0:T(4,128)(2,1)S(1)}, s32[]{:T(128)}) while((s32[]{:T(128)}, f32[4,4,8192]{2,1,0:T(4,128)S(1)}, s32[4,8192]{1,0:T(4,128)S(1)}, bf16[4,256]{1,0:T(4,128)(2,1)S(1)}, s32[]{:T(128)}) %tuple.80), condition=%wide.region_4.4_spmd.clone, body=%wide.region_3.3_spmd.clone.sunk | while | flops 18874368 | bytes 231493 | solution.py:66
  64.9 1.4 fusion.51
  66.4 1.4 fusion.51
  67.8 1.4 fusion.51
  69.2 1.4 fusion.51
  71.4 5.6 %while.39 = (s32[]{:T(128)}, f32[4,4,8192]{2,1,0:T(4,128)S(1)}, s32[4,8192]{1,0:T(4,128)S(1)}, bf16[4,256]{1,0:T(4,128)(2,1)S(1)}, s32[]{:T(128)}) while((s32[]{:T(128)}, f32[4,4,8192]{2,1,0:T(4,128)S(1)}, s32[4,8192]{1,0:T(4,128)S(1)}, bf16[4,256]{1,0:T(4,128)(2,1)S(1)}, s32[]{:T(128)}) %tuple.83), condition=%wide.region_2.2_spmd.clone, body=%wide.region_1.1_spmd.clone.sunk | while | flops 18874368 | bytes 231493 | solution.py:66
  71.5 1.4 fusion.53
  72.9 1.4 fusion.53
  74.3 1.4 fusion.53
  75.7 1.4 fusion.53
  84.0 5.6 %while.38 = (s32[]{:T(128)}, f32[4,4,8192]{2,1,0:T(4,128)S(1)}, s32[4,8192]{1,0:T(4,128)S(1)}, bf16[4,256]{1,0:T(4,128)(2,1)S(1)}, s32[]{:T(128)}) while((s32[]{:T(128)}, f32[4,4,8192]{2,1,0:T(4,128)S(1)}, s32[4,8192]{1,0:T(4,128)S(1)}, bf16[4,256]{1,0:T(4,128)(2,1)S(1)}, s32[]{:T(128)}) %tuple.80), condition=%wide.region_4.4_spmd.clone, body=%wide.region_3.3_spmd.clone.sunk | while | flops 18874368 | bytes 231493 | solution.py:66
  84.1 1.4 fusion.51
  85.5 1.4 fusion.51
  86.9 1.4 fusion.51
  88.3 1.4 fusion.51
  90.5 5.6 %while.39 = (s32[]{:T(128)}, f32[4,4,8192]{2,1,0:T(4,128)S(1)}, s32[4,8192]{1,0:T(4,128)S(1)}, bf16[4,256]{1,0:T(4,128)(2,1)S(1)}, s32[]{:T(128)}) while((s32[]{:T(128)}, f32[4,4,8192]{2,1,0:T(4,128)S(1)}, s32[4,8192]{1,0:T(4,128)S(1)}, bf16[4,256]{1,0:T(4,128)(2,1)S(1)}, s32[]{:T(128)}) %tuple.83), condition=%wide.region_2.2_spmd.clone, body=%wide.region_1.1_spmd.clone.sunk | while | flops 18874368 | bytes 231493 | solution.py:66
  90.6 1.4 fusion.53
  92.0 1.4 fusion.53
  93.4 1.4 fusion.53
  94.8 1.4 fusion.53
  103.1 5.6 %while.38 = (s32[]{:T(128)}, f32[4,4,8192]{2,1,0:T(4,128)S(1)}, s32[4,8192]{1,0:T(4,128)S(1)}, bf16[4,256]{1,0:T(4,128)(2,1)S(1)}, s32[]{:T(128)}) while((s32[]{:T(128)}, f32[4,4,8192]{2,1,0:T(4,128)S(1)}, s32[4,8192]{1,0:T(4,128)S(1)}, bf16[4,256]{1,0:T(4,128)(2,1)S(1)}, s32[]{:T(128)}) %tuple.80), condition=%wide.region_4.4_spmd.clone, body=%wide.region_3.3_spmd.clone.sunk | while | flops 18874368 | bytes 231493 | solution.py:66
  103.2 1.4 fusion.51
  104.6 1.4 fusion.51
  106.0 1.4 fusion.51
  107.4 1.4 fusion.51
  109.7 5.6 %while.39 = (s32[]{:T(128)}, f32[4,4,8192]{2,1,0:T(4,128)S(1)}, s32[4,8192]{1,0:T(4,128)S(1)}, bf16[4,256]{1,0:T(4,128)(2,1)S(1)}, s32[]{:T(128)}) while((s32[]{:T(128)}, f32[4,4,8192]{2,1,0:T(4,128)S(1)}, s32[4,8192]{1,0:T(4,128)S(1)}, bf16[4,256]{1,0:T(4,128)(2,1)S(1)}, s32[]{:T(128)}) %tuple.83), condition=%wide.region_2.2_spmd.clone, body=%wide.region_1.1_spmd.clone.sunk | while | flops 18874368 | bytes 231493 | solution.py:66
  109.7 1.4 fusion.53
  122.2 5.6 %while.38 = (s32[]{:T(128)}, f32[4,4,8192]{2,1,0:T(4,128)S(1)}, s32[4,8192]{1,0:T(4,128)S(1)}, bf16[4,256]{1,0:T(4,128)(2,1)S(1)}, s32[]{:T(128)}) while((s32[]{:T(128)}, f32[4,4,8192]{2,1,0:T(4,128)S(1)}, s32[4,8192]{1,0:T(4,128)S(1)}, bf16[4,256]{1,0:T(4,128)(2,1)S(1)}, s32[]{:T(128)}) %tuple.80), condition=%wide.region_4.4_spmd.clone, body=%wide.region_3.3_spmd.clone.sunk | while | flops 18874368 | bytes 231493 | solution.py:66
  128.8 5.6 %while.39 = (s32[]{:T(128)}, f32[4,4,8192]{2,1,0:T(4,128)S(1)}, s32[4,8192]{1,0:T(4,128)S(1)}, bf16[4,256]{1,0:T(4,128)(2,1)S(1)}, s32[]{:T(128)}) while((s32[]{:T(128)}, f32[4,4,8192]{2,1,0:T(4,128)S(1)}, s32[4,8192]{1,0:T(4,128)S(1)}, bf16[4,256]{1,0:T(4,128)(2,1)S(1)}, s32[]{:T(128)}) %tuple.83), condition=%wide.region_2.2_spmd.clone, body=%wide.region_1.1_spmd.clone.sunk | while | flops 18874368 | bytes 231493 | solution.py:66
  141.4 5.6 %while.38 = (s32[]{:T(128)}, f32[4,4,8192]{2,1,0:T(4,128)S(1)}, s32[4,8192]{1,0:T(4,128)S(1)}, bf16[4,256]{1,0:T(4,128)(2,1)S(1)}, s32[]{:T(128)}) while((s32[]{:T(128)}, f32[4,4,8192]{2,1,0:T(4,128)S(1)}, s32[4,8192]{1,0:T(4,128)S(1)}, bf16[4,256]{1,0:T(4,128)(2,1)S(1)}, s32[]{:T(128)}) %tuple.80), condition=%wide.region_4.4_spmd.clone, body=%wide.region_3.3_spmd.clone.sunk | while | flops 18874368 | bytes 231493 | solution.py:66
  147.9 5.6 %while.39 = (s32[]{:T(128)}, f32[4,4,8192]{2,1,0:T(4,128)S(1)}, s32[4,8192]{1,0:T(4,128)S(1)}, bf16[4,256]{1,0:T(4,128)(2,1)S(1)}, s32[]{:T(128)}) while((s32[]{:T(128)}, f32[4,4,8192]{2,1,0:T(4,128)S(1)}, s32[4,8192]{1,0:T(4,128)S(1)}, bf16[4,256]{1,0:T(4,128)(2,1)S(1)}, s32[]{:T(128)}) %tuple.83), condition=%wide.region_2.2_spmd.clone, body=%wide.region_1.1_spmd.clone.sunk | while | flops 18874368 | bytes 231493 | solution.py:66
  160.5 5.6 %while.38 = (s32[]{:T(128)}, f32[4,4,8192]{2,1,0:T(4,128)S(1)}, s32[4,8192]{1,0:T(4,128)S(1)}, bf16[4,256]{1,0:T(4,128)(2,1)S(1)}, s32[]{:T(128)}) while((s32[]{:T(128)}, f32[4,4,8192]{2,1,0:T(4,128)S(1)}, s32[4,8192]{1,0:T(4,128)S(1)}, bf16[4,256]{1,0:T(4,128)(2,1)S(1)}, s32[]{:T(128)}) %tuple.80), condition=%wide.region_4.4_spmd.clone, body=%wide.region_3.3_spmd.clone.sunk | while | flops 18874368 | bytes 231493 | solution.py:66
  167.0 5.6 %while.39 = (s32[]{:T(128)}, f32[4,4,8192]{2,1,0:T(4,128)S(1)}, s32[4,8192]{1,0:T(4,128)S(1)}, bf16[4,256]{1,0:T(4,128)(2,1)S(1)}, s32[]{:T(128)}) while((s32[]{:T(128)}, f32[4,4,8192]{2,1,0:T(4,128)S(1)}, s32[4,8192]{1,0:T(4,128)S(1)}, bf16[4,256]{1,0:T(4,128)(2,1)S(1)}, s32[]{:T(128)}) %tuple.83), condition=%wide.region_2.2_spmd.clone, body=%wide.region_1.1_spmd.clone.sunk | while | flops 18874368 | bytes 231493 | solution.py:66
  179.6 5.6 %while.38 = (s32[]{:T(128)}, f32[4,4,8192]{2,1,0:T(4,128)S(1)}, s32[4,8192]{1,0:T(4,128)S(1)}, bf16[4,256]{1,0:T(4,128)(2,1)S(1)}, s32[]{:T(128)}) while((s32[]{:T(128)}, f32[4,4,8192]{2,1,0:T(4,128)S(1)}, s32[4,8192]{1,0:T(4,128)S(1)}, bf16[4,256]{1,0:T(4,128)(2,1)S(1)}, s32[]{:T(128)}) %tuple.80), condition=%wide.region_4.4_spmd.clone, body=%wide.region_3.3_spmd.clone.sunk | while | flops 18874368 | bytes 231493 | solution.py:66
  186.1 5.6 %while.39 = (s32[]{:T(128)}, f32[4,4,8192]{2,1,0:T(4,128)S(1)}, s32[4,8192]{1,0:T(4,128)S(1)}, bf16[4,256]{1,0:T(4,128)(2,1)S(1)}, s32[]{:T(128)}) while((s32[]{:T(128)}, f32[4,4,8192]{2,1,0:T(4,128)S(1)}, s32[4,8192]{1,0:T(4,128)S(1)}, bf16[4,256]{1,0:T(4,128)(2,1)S(1)}, s32[]{:T(128)}) %tuple.83), condition=%wide.region_2.2_spmd.clone, body=%wide.region_1.1_spmd.clone.sunk | while | flops 18874368 | bytes 231493 | solution.py:66
  195.8 4.1 %collective-permute-start.4 = (f32[4,32,4,128]{3,1,2,0:T(8,128)S(1)}, f32[4,32,4,128]{3,1,2,0:T(8,128)S(1)}, u32[]{:S(2)}, u32[]{:S(2)}) collective-permute-start(f32[4,32,4,128]{3,1,2,0:T(8,128)S(1)} %bitcast.114), channel_id=1, source_target_pairs={{0,1},{1,0},{2,3},{3,2},{4,5},{5,4},{6,7},{7,6},{8,9},{9,8},{10,11... | collective-permute-start | bytes 786440 | tf_op jit(solution)/shard_map/ppermute | solution.py:33
  199.9 6.2 %collective-permute-done.4 = f32[4,32,4,128]{3,1,2,0:T(8,128)S(1)} collective-permute-done((f32[4,32,4,128]{3,1,2,0:T(8,128)S(1)}, f32[4,32,4,128]{3,1,2,0:T(8,128)S(1)}, u32[]{:S(2)}, u32[]{:S(2)}) %collective-permute-start.4) | collective-permute-done | bytes 262176 | tf_op jit(solution)/shard_map/ppermute | solution.py:33
  206.4 2.7 collective-permute-start.5
  209.1 7.3 %collective-permute-done.5 = f32[4,32,2,128]{3,1,2,0:T(8,128)S(1)} collective-permute-done((f32[4,32,2,128]{3,1,2,0:T(8,128)S(1)}, f32[4,32,2,128]{3,1,2,0:T(8,128)S(1)}, u32[]{:S(2)}, u32[]{:S(2)}) %collective-permute-start.5) | collective-permute-done | bytes 131104 | tf_op jit(solution)/shard_map/ppermute | solution.py:33
  216.7 5.3 %collective-permute-start.6 = (f32[4,32,1,128]{3,1,2,0:T(8,128)S(1)}, f32[4,32,1,128]{3,1,2,0:T(8,128)S(1)}, u32[]{:S(2)}, u32[]{:S(2)}) collective-permute-start(f32[4,32,1,128]{3,1,2,0:T(8,128)S(1)} %constant_dynamic-slice_fusion.4), channel_id=1, source_target_pairs={{0,4},{4,0},{1,5},{5,1},{2,6},{6,2},{3,7},{7,3},{8,12},{12,8},{9,1... | collective-permute-start | bytes 196616 | tf_op jit(solution)/shard_map/ppermute | solution.py:33
  222.0 5.4 %collective-permute-done.6 = f32[4,32,1,128]{3,1,2,0:T(8,128)S(1)} collective-permute-done((f32[4,32,1,128]{3,1,2,0:T(8,128)S(1)}, f32[4,32,1,128]{3,1,2,0:T(8,128)S(1)}, u32[]{:S(2)}, u32[]{:S(2)}) %collective-permute-start.6) | collective-permute-done | bytes 65568 | tf_op jit(solution)/shard_map/ppermute | solution.py:33
  228.2 88.7 %all-gather.3.cloned.1.call-done = f32[4,2048,1,128]{3,1,2,0:T(8,128)} async-done(((f32[4,32,1,128]{3,1,2,0:T(8,128)}), f32[4,2048,1,128]{3,1,2,0:T(8,128)}) %all-gather.3.cloned.1.call-update) | async-done | bytes 4194320 | tf_op jit(solution)/shard_map/all_gather | solution.py:109
  316.9 4.5 %copy.57 = f32[4,2048,128]{2,1,0:T(8,128)} copy(f32[4,2048,128]{2,1,0:T(8,128)} %bitcast.110) | data formatting | bytes 8388608
  (266 shorter events, 102.6 us)
Async XLA Ops:
  6.5 20.2 %copy-start.1 = (s32[2,8,32,1024]{3,2,1,0:T(8,128)S(1)}, s32[2,8,32,1024]{3,2,1,0:T(8,128)}, u32[]{:S(2)}) copy-start(s32[2,8,32,1024]{3,2,1,0:T(8,128)} %param.12) | copy-start | bytes 6291460
  6.5 310.3 %all-gather.3.cloned.1.call-start = ((), (), s32[]{:S(2)}) async-start(), calls=%async_computation | async-start | bytes 4259840 | tf_op jit(solution)/shard_map/all_gather | solution.py:109
  8.0 12.2 %collective-permute-start = (f32[2,8,1,1024]{3,2,1,0:T(1,128)S(1)}, f32[2,8,1,1024]{3,2,1,0:T(1,128)S(1)}, u32[]{:S(2)}, u32[]{:S(2)}) collective-permute-start(f32[2,8,1,1024]{3,2,1,0:T(1,128)S(1)} %get-tuple-element.184), channel_id=1, source_target_pairs={{0,8},{8,16},{16,24},{24,32},{32,40},{40,48},{48,56},{56,64},{64,7... | collective-permute-start | bytes 196616 | tf_op jit(solution)/shard_map/ppermute | solution.py:17
  12.5 7.7 %collective-permute-start.1 = (f32[2,8,1,1024]{3,2,1,0:T(1,128)S(1)}, f32[2,8,1,1024]{3,2,1,0:T(1,128)S(1)}, u32[]{:S(2)}, u32[]{:S(2)}) collective-permute-start(f32[2,8,1,1024]{3,2,1,0:T(1,128)S(1)} %get-tuple-element.185), channel_id=1, source_target_pairs={{8,0},{16,8},{24,16},{32,24},{40,32},{48,40},{56,48},{64,56},{72,6... | collective-permute-start | bytes 196616 | tf_op jit(solution)/shard_map/ppermute | solution.py:19
  21.4 11.3 %collective-permute-start.2 = (f32[2,1,34,1024]{3,2,1,0:T(8,128)S(1)}, f32[2,1,34,1024]{3,2,1,0:T(8,128)S(1)}, u32[]{:S(2)}, u32[]{:S(2)}) collective-permute-start(f32[2,1,34,1024]{3,2,1,0:T(8,128)S(1)} %get-tuple-element.182), channel_id=1, source_target_pairs={{1,0},{2,1},{3,2},{4,3},{5,4},{6,5},{7,6},{9,8},{10,9},{11,10},{12... | collective-permute-start | bytes 835592 | tf_op jit(solution)/shard_map/ppermute | solution.py:19
  22.7 11.4 %collective-permute-start.3 = (f32[2,1,34,1024]{3,2,1,0:T(8,128)S(1)}, f32[2,1,34,1024]{3,2,1,0:T(8,128)S(1)}, u32[]{:S(2)}, u32[]{:S(2)}) collective-permute-start(f32[2,1,34,1024]{3,2,1,0:T(8,128)S(1)} %get-tuple-element.183), channel_id=1, source_target_pairs={{0,1},{1,2},{2,3},{3,4},{4,5},{5,6},{6,7},{8,9},{9,10},{10,11},{11... | collective-permute-start | bytes 835592 | tf_op jit(solution)/shard_map/ppermute | solution.py:17
  26.7 7.4 %copy-start = (f32[2,8,32,1024]{3,2,1,0:T(8,128)S(1)}, f32[2,8,32,1024]{3,2,1,0:T(8,128)}, u32[]{:S(2)}) copy-start(f32[2,8,32,1024]{3,2,1,0:T(8,128)} %param.11) | copy-start | bytes 6291460
  195.8 10.3 %collective-permute-start.4 = (f32[4,32,4,128]{3,1,2,0:T(8,128)S(1)}, f32[4,32,4,128]{3,1,2,0:T(8,128)S(1)}, u32[]{:S(2)}, u32[]{:S(2)}) collective-permute-start(f32[4,32,4,128]{3,1,2,0:T(8,128)S(1)} %bitcast.114), channel_id=1, source_target_pairs={{0,1},{1,0},{2,3},{3,2},{4,5},{5,4},{6,7},{7,6},{8,9},{9,8},{10,11... | collective-permute-start | bytes 786440 | tf_op jit(solution)/shard_map/ppermute | solution.py:33
  206.4 10.1 %collective-permute-start.5 = (f32[4,32,2,128]{3,1,2,0:T(8,128)S(1)}, f32[4,32,2,128]{3,1,2,0:T(8,128)S(1)}, u32[]{:S(2)}, u32[]{:S(2)}) collective-permute-start(f32[4,32,2,128]{3,1,2,0:T(8,128)S(1)} %dynamic-slice_bitcast_fusion), channel_id=1, source_target_pairs={{0,2},{2,0},{1,3},{3,1},{4,6},{6,4},{5,7},{7,5},{8,10},{10,8},{9,1... | collective-permute-start | bytes 393224 | tf_op jit(solution)/shard_map/ppermute | solution.py:33
  216.7 10.7 %collective-permute-start.6 = (f32[4,32,1,128]{3,1,2,0:T(8,128)S(1)}, f32[4,32,1,128]{3,1,2,0:T(8,128)S(1)}, u32[]{:S(2)}, u32[]{:S(2)}) collective-permute-start(f32[4,32,1,128]{3,1,2,0:T(8,128)S(1)} %constant_dynamic-slice_fusion.4), channel_id=1, source_target_pairs={{0,4},{4,0},{1,5},{5,1},{2,6},{6,2},{3,7},{7,3},{8,12},{12,8},{9,1... | collective-permute-start | bytes 196616 | tf_op jit(solution)/shard_map/ppermute | solution.py:33
Sparse Core Ops, SparseCore 0:
  228.3 88.5 all-gather.2
where the time goes:
time: 329 us; the launch traced here: 328 us
  waiting for transfers between devices  113 us (34%)
  matrix products  87.7 us (27%)
  local copies, waits for them, and re-layouts  37.7 us (11%)
  other arithmetic  30.5 us (9%)
  starting transfers between devices  27.5 us (8%)
  loops' own time  17.7 us (5%)
  between operations  13.7 us (4%)
    all_gather x1, waiting for transfers between devices, on_device(): return lax.all_gather(finished, 'wide', axis=1, tiled=True)  88.7 us
    dot_general x64, matrix products, one_block(): return jnp.dot(table_rows, one_hot, preferred_element_type=jnp.float32)  87.7 us
    ppermute x3, waiting for transfers between devices, partner(): return lax.ppermute(block, axis, route)  18.9 us
    another operation x1, loops' own time, on_device(): lax.scan(march_step, start, jnp.arange(depth_count, dtype=jnp.int32))  17.1 us
    ppermute x3, starting transfers between devices, partner(): return lax.ppermute(block, axis, route)  12.2 us
    ppermute x2, starting transfers between devices, extended(): lax.ppermute(tail, axis, [(i, (i + 1) % count) for i in range(ends)])  8.52 us
    mul x8, other arithmetic, make_sample(): opacity[0] * shading[0] * looked_up[0, :3]  8.15 us
    slice x8, local copies, waits for them, and re-layouts, march_step(): bins_now[0]  7.94 us
  transfers between devices with their start and end apart: 8, of which 6 were waited for; matrix products, arithmetic and copies ran while one was open for 1% of the time, Pallas kernels for 0%

commit v1 on v0

v1 whole, which is shorter than its diff:
```python
import jax
import jax.numpy as jnp
from jax import lax
from jax.experimental import pallas as pl
from jax.experimental.pallas import tpu as pltpu
from jax.sharding import Mesh, PartitionSpec as P

LOOK = lax.GatherDimensionNumbers(offset_dims=(), collapsed_slice_dims=(1,), start_index_map=(1,), operand_batching_dims=(0,), start_indices_batching_dims=(0,))

def pick(table, lanes):
    return lax.gather(table, lanes[..., None], LOOK, (1, 1), mode=lax.GatherScatterMode.PROMISE_IN_BOUNDS)

def packed_tables(colour, opacity):
    words = []
    for f in range(2):
        c = [(colour[f, k:k+1, :].astype(jnp.float32) * 4096.0).astype(jnp.int32) for k in range(3)]
        o = (opacity[f:f+1, :].astype(jnp.float32) * 262144.0).astype(jnp.int32)
        w0 = c[0] + c[1] * 8192
        w1 = c[2] + o * 8192
        words.append([[jnp.broadcast_to(w[:, h*128:(h+1)*128], (8, 128)) for h in range(2)] for w in (w0, w1)])
    return words

def brick_kernel(fields, zlo, zhi, xlo, xhi, bins, ctab, otab, back, out, ext, tab):
    depth, cols, rows = fields.shape[1:]
    for f in range(2):
        ext[f, 0, 8:8+cols, 128:128+rows] = zlo[f, 0]
        ext[f, depth+1, 8:8+cols, 128:128+rows] = zhi[f, 0]
        for d in range(depth):
            ext[f, d+1, 8:8+cols, 128:128+rows] = fields[f, d]
            ext[f, d+1, 7:8, 128:128+rows] = xlo[f, d]
            ext[f, d+1, 8+cols:9+cols, 128:128+rows] = xhi[f, d]
            zero = jnp.zeros((cols, 128), jnp.float32)
            ext[f, d+1, 8:8+cols, 0:128] = zero
            ext[f, d+1, 8:8+cols, 128+rows:256+rows] = zero
    words = packed_tables(ctab[...], otab[...])
    for f in range(2):
        for w in range(2):
            for h in range(2):
                tab[f, w, h] = words[f][w][h]
    sub = lax.broadcasted_iota(jnp.int32, (8, 128), 0)
    lane = lax.broadcasted_iota(jnp.int32, (8, 128), 1)
    last_sub, first_sub = sub == 7, sub == 0
    last_lane, first_lane = lane == 127, lane == 0

    def tile(step, carry):
        g = step // (rows // 128)
        b = step % (rows // 128)
        c0 = pl.multiple_of(g * 8, 8)
        r0 = pl.multiple_of(b * 128, 128)
        backward = back[pl.ds(c0, 8), :] == 1
        acc = [None] * 3
        through = None
        for d in range(depth):
            part = [None] * 3
            clear = None
            for f in range(2):
                def at(dd, dc, dr):
                    return ext[f, d + 1 + dd, pl.ds(c0 + 8 + dc, 8), pl.ds(r0 + 128 + dr, 128)]
                here = at(0, 0, 0)
                dz = at(1, 0, 0) - at(-1, 0, 0)
                dx = pltpu.roll(jnp.where(first_sub, at(0, 8, 0), here), 7, 0) - pltpu.roll(jnp.where(last_sub, at(0, -8, 0), here), 1, 0)
                dy = pltpu.roll(jnp.where(first_lane, at(0, 0, 128), here), 127, 1) - pltpu.roll(jnp.where(last_lane, at(0, 0, -128), here), 1, 1)
                total = dz * dz + dx * dx + dy * dy
                shade = 0.3 + (0.35 * jnp.abs(dz)) * lax.rsqrt(0.25 * total + 1.0)
                scale = 2.0 ** -18
                gain = 0.25 * scale + (0.5 * scale) * (total * lax.rsqrt(jnp.maximum(total, 1e-30)))
                idx = bins[f, d, pl.ds(c0, 8), pl.ds(r0, 128)]
                low = idx & 127
                upper = idx > 127
                w = [jnp.where(upper, pick(tab[f, k, 1], low), pick(tab[f, k, 0], low)) for k in range(2)]
                look = [(w[0] & 8191).astype(jnp.float32), (w[0] >> 13).astype(jnp.float32), (w[1] & 8191).astype(jnp.float32)]
                alpha = (w[1] >> 13).astype(jnp.float32) * gain
                lit = alpha * shade
                for k in range(3):
                    term = lit * look[k]
                    part[k] = term if part[k] is None else part[k] + term
                clear = (1.0 - alpha) if clear is None else clear * (1.0 - alpha)
            if d == 0:
                acc = part
                through = clear
            else:
                keep = jnp.where(backward, clear, 1.0)
                weight = jnp.where(backward, 1.0, through)
                acc = [a * keep + weight * p for a, p in zip(acc, part)]
                through = through * clear
        for k in range(3):
            out[b, k, pl.ds(c0, 8), :] = acc[k] * (1.0 / 4096.0)
        out[b, 3, pl.ds(c0, 8), :] = 1.0 - through
        return carry
    lax.fori_loop(0, (cols // 8) * (rows // 128), tile, 0)

def brick(fields, zlo, zhi, xlo, xhi, bins, ctab, otab, back):
    _, depth, cols, rows = fields.shape
    return pl.pallas_call(
        brick_kernel,
        out_shape=jax.ShapeDtypeStruct((rows // 128, 4, cols, 128), jnp.float32),
        in_specs=[pl.BlockSpec(memory_space=pltpu.VMEM)] * 9,
        out_specs=pl.BlockSpec(memory_space=pltpu.VMEM),
        scratch_shapes=[pltpu.VMEM((2, depth + 2, cols + 16, rows + 256), jnp.float32), pltpu.VMEM((2, 2, 2, 8, 128), jnp.int32)],
        compiler_params=pltpu.CompilerParams(vmem_limit_bytes=40 * 2**20),
        name="brick",
    )(fields, zlo, zhi, xlo, xhi, bins, ctab, otab, back)


def join_kernel(parts, back, out):
    depth = parts.shape[0]
    for group in range(parts.shape[2] // 8):
        cols = pl.ds(group * 8, 8)
        backward = back[cols, :] == 1
        acc = [parts[0, k, cols, :] for k in range(3)]
        through = 1.0 - parts[0, 3, cols, :]
        for d in range(1, depth):
            clear = 1.0 - parts[d, 3, cols, :]
            keep = jnp.where(backward, clear, 1.0)
            weight = jnp.where(backward, 1.0, through)
            acc = [a * keep + weight * parts[d, k, cols, :] for k, a in enumerate(acc)]
            through = through * clear
        for k in range(3):
            out[k, cols, :] = acc[k]
        out[3, cols, :] = 1.0 - through


def join(parts, back):
    return pl.pallas_call(
        join_kernel,
        out_shape=jax.ShapeDtypeStruct(parts.shape[1:], jnp.float32),
        in_specs=[pl.BlockSpec(memory_space=pltpu.VMEM)] * 2,
        out_specs=pl.BlockSpec(memory_space=pltpu.VMEM),
        name="join",
    )(parts, back)


def place_kernel(spots, *refs):
    pieces, out, sem = refs[:-2], refs[-2], refs[-1]
    x_count = len(pieces) // 2
    copies = []
    for n, piece in enumerate(pieces):
        for z in range(piece.shape[0]):
            spot = out.at[:, z, spots[n % x_count], spots[x_count + n // x_count]]
            copies.append(pltpu.make_async_copy(piece.at[z], spot, sem))
    for copy in copies:
        copy.start()
    for copy in copies:
        copy.wait()


def place(pieces, others, spots):
    x_count = len(pieces)
    z_count, channels, cols, rows = pieces[0].shape
    frame = pl.pallas_call(
        place_kernel,
        out_shape=jax.ShapeDtypeStruct((channels, z_count, x_count, 2, cols, rows), jnp.float32),
        in_specs=[pl.BlockSpec(memory_space=pltpu.SMEM)] + [pl.BlockSpec(memory_space=pl.ANY)] * (2 * x_count),
        out_specs=pl.BlockSpec(memory_space=pl.ANY),
        scratch_shapes=[pltpu.SemaphoreType.DMA],
        name="place",
    )(spots, *pieces, *others)
    return frame.reshape(channels, z_count * x_count * 2 * cols, rows)


def shifted(value, axis, step, wrap=True):
    count = lax.axis_size(axis)
    route = [(i, (i + step) % count) for i in range(count) if wrap or 0 <= i + step < count]
    return lax.ppermute(value, axis, route)


def neighbour(value, step):
    axes = ("z", "x", "c")
    count = 1
    for axis in axes:
        count *= lax.axis_size(axis)
    return lax.ppermute(value, axes, [(i, i + step) for i in range(count) if 0 <= i + step < count])


def on_device(fields, field_bins, colour_table, opacity_table, view_dir):
    depth, cols = fields.shape[1:3]
    zlo = shifted(fields[:, depth - 1 :], "y", 1, wrap=False)
    zhi = shifted(fields[:, :1], "y", -1, wrap=False)
    xlo = neighbour(fields[:, :, cols - 1 :], 1)
    xhi = neighbour(fields[:, :, :1], -1)
    back = jnp.broadcast_to(view_dir[:, None], (cols, 128))
    partial = brick(fields, zlo, zhi, xlo, xhi, field_bins, colour_table, opacity_table, back)
    partial = lax.all_to_all(partial, "y", 0, 0)
    finished = join(partial, back)
    column = lax.all_gather(finished, "z")
    x_count = lax.axis_size("x")
    steps = [0, 1, x_count - 1] + list(range(2, x_count - 1))
    pieces = [column] + [shifted(column, "x", -step) for step in steps[1:]]
    others = [lax.ppermute(piece, "c", [(0, 1), (1, 0)]) for piece in pieces]
    x, c = lax.axis_index("x"), lax.axis_index("c")
    spots = jnp.stack([(x + step) % x_count for step in steps] + [c, 1 - c])
    return place(pieces, others, spots)


def solution(mesh):
    z_count, x_count, c_count = 8, 4, 2
    grid = Mesh(mesh.devices.reshape(z_count, x_count, c_count, -1), ("z", "x", "c", "y"))
    wide = ("z", "x", "c")
    in_specs = (
        P(None, "y", wide, None),
        P(None, "y", wide, None),
        P(),
        P(),
        P(wide),
    )
    return jax.shard_map(on_device, mesh=grid, in_specs=in_specs, out_specs=P(None, None, "y"), check_vma=False)
```

time: 329 us -> 245 us (0.74)
  Pallas kernels: 0 us -> 139 us
  waiting for transfers between devices: 113 us -> 1.53 us
  matrix products: 87.7 us -> 0 us
  blocking collectives: 0 us -> 40.2 us
  other arithmetic: 30.5 us -> 0 us
  local copies, waits for them, and re-layouts: 37.7 us -> 8.39 us
  starting transfers between devices: 27.5 us -> 55.2 us
  loops' own time: 17.7 us -> 0 us
  between operations: 13.7 us -> 0.24 us
    pallas_call x0 -> x3, Pallas kernels: none -> 139 us  [the longest x1 129 us: place(): pl.pallas_call(place_kernel, out_shape=jax.ShapeDtypeStruct((channels, z_...]
    all_gather x1 -> x0, waiting for transfers between devices: 88.7 us -> none  [on_device(): return lax.all_gather(finished, 'wide', axis=1, tiled=True)]
    dot_general x64 -> x0, matrix products: 87.7 us -> none  [one_block(): return jnp.dot(table_rows, one_hot, preferred_element_type=jnp.float32)]
    ppermute x7 -> x11, starting transfers between devices: 27.5 us -> 55.2 us  [the longest x5 22.5 us: shifted(): return lax.ppermute(value, axis, route)]
    ppermute x7 -> x11, waiting for transfers between devices: 24.6 us -> 1.53 us  [the longest x4 0.9 us: on_device(): others = [lax.ppermute(piece, 'c', [(0, 1), (1, 0)]) for piece in pieces]]
    all_to_all x0 -> x1, blocking collectives: none -> 21.1 us  [on_device(): partial = lax.all_to_all(partial, 'y', 0, 0)]
    all_gather x0 -> x1, blocking collectives: none -> 19.1 us  [on_device(): column = lax.all_gather(finished, 'z')]
    another operation x17 -> x0, loops' own time: 17.7 us -> none  [the longest x1 17.1 us: on_device(): lax.scan(march_step, start, jnp.arange(depth_count, dtype=jnp.int32))]
  transfers between devices with their start and end apart: 8 -> 11, of which waited for: 6 -> 2; matrix products, arithmetic and copies ran while one was open for 1% -> 1% of each run, Pallas kernels for 0% -> 0%
where the time goes in v1:
time: 245 us; the launch traced here: 244 us
  Pallas kernels  139 us (57%)
  starting transfers between devices  55.2 us (23%)
  blocking collectives  40.2 us (16%)
  local copies, waits for them, and re-layouts  8.39 us (3%)
    pallas_call x1, Pallas kernels, place(): pl.pallas_call(place_kernel, out_shape=jax.ShapeDtypeStruct((channels, z_...  129 us
    ppermute x5, starting transfers between devices, shifted(): return lax.ppermute(value, axis, route)  22.5 us
    ppermute x4, starting transfers between devices, on_device(): others = [lax.ppermute(piece, 'c', [(0, 1), (1, 0)]) for piece in pieces]  22.1 us
    all_to_all x1, blocking collectives, on_device(): partial = lax.all_to_all(partial, 'y', 0, 0)  21.1 us
    all_gather x1, blocking collectives, on_device(): column = lax.all_gather(finished, 'z')  19.1 us
    ppermute x2, starting transfers between devices, neighbour(): lax.ppermute(value, axes, [(i, i + step) for i in range(count) if 0 <= i...  10.6 us
    pallas_call x1, Pallas kernels, brick(): pl.pallas_call(brick_kernel, out_shape=jax.ShapeDtypeStruct((rows // 128,...  8.34 us
  transfers between devices with their start and end apart: 11, of which 2 were waited for; matrix products, arithmetic and copies ran while one was open for 1% of the time, Pallas kernels for 0%

profile of v1, /device:TPU:1, one launch (start us, length us, event | category | flops | bytes accessed | tf_op | source)
XLA Modules:
  0.0 244.5 jit_solution(1508859865975620951)
XLA Ops:
  0.0 1.1 fusion.1
  1.1 1.3 collective-permute-start.1
  2.4 4.7 %collective-permute-start = (f32[2,1,32,1024]{3,2,1,0:T(8,128)S(1)}, f32[2,1,32,1024]{3,2,1,0:T(8,128)S(1)}, u32[]{:S(2)}, u32[]{:S(2)}) collective-permute-start(f32[2,1,32,1024]{3,2,1,0:T(8,128)S(1)} %get-tuple-element.8), channel_id=1, source_target_pairs={{0,1},{1,2},{2,3},{3,4},{4,5},{5,6},{6,7},{8,9},{9,10},{10,11},{11... | collective-permute-start | bytes 786440 | tf_op jit(solution)/shard_map/ppermute | solution.py:164
  7.1 1.3 fusion
  8.4 8.7 %collective-permute-start.3 = (f32[2,8,1,1024]{3,2,1,0:T(1,128)S(1)}, f32[2,8,1,1024]{3,2,1,0:T(1,128)S(1)}, u32[]{:S(2)}, u32[]{:S(2)}) collective-permute-start(f32[2,8,1,1024]{3,2,1,0:T(1,128)S(1)} %get-tuple-element.5), channel_id=1, source_target_pairs={{8,0},{16,8},{24,16},{32,24},{40,32},{48,40},{56,48},{64,56},{72,6... | collective-permute-start | bytes 196616 | tf_op jit(solution)/shard_map/ppermute | solution.py:172
  17.0 1.9 collective-permute-start.2
  19.0 0.7 copy.7.ctab
  19.7 0.0 collective-permute-done.3.xhi
  19.7 0.6 collective-permute-done.2.xlo
  20.3 0.0 collective-permute-done.1.zhi
  20.3 0.0 collective-permute-done.zlo
  20.3 0.7 broadcast_in_dim.2.back
  21.0 0.0 copy-start
  21.0 1.6 copy-done
  22.6 0.0 copy-start.1
  22.6 1.6 copy-done.1
  24.2 0.0 copy-start.3
  24.2 0.7 copy-done.3
  24.9 0.0 copy-start.2
  24.9 8.3 %brick.1 = f32[8,4,32,128]{3,2,1,0:T(8,128)S(1)} custom-call(f32[2,8,32,1024]{3,2,1,0:T(8,128)S(1)} %copy-done, f32[2,1,32,1024]{3,2,1,0:T(8,128)S(1)} %collective-permute-done.zlo, f32[2,1,32,1024]{3,2,1,0:T(8,128)S(1)} %collective-permute-done.1.zhi, f32[2,8,1,1024]{3,2,1,0:T(1,128)S(1)} %collective-permute-done.2.xlo, ...), custom_call_target="tpu_custom_call" | custom-call | tf_op jit(solution)/shard_map/brick/pallas_call | solution.py:94
  33.2 0.0 copy-done.2
  33.2 21.1 %all_to_all.5.parts = f32[8,4,32,128]{3,2,1,0:T(8,128)} all-to-all(f32[8,4,32,128]{3,2,1,0:T(8,128)S(1)} %brick.1), channel_id=1, replica_groups=mesh['z'=8,'x'=4,'c'=2,'y'=8] {'y'}, dimensions={0} | all-to-all | bytes 1048576 | tf_op jit(solution)/shard_map/all_to_all | solution.py:183
  54.3 1.7 join.1
  56.1 19.1 %all-gather = f32[32,32,128]{2,1,0:T(8,128)S(1)} all-gather(f32[4,32,128]{2,1,0:T(8,128)} %join.1), channel_id=2, replica_groups=mesh['z'=8,'x'=4,'c'=2,'y'=8] {'z'}, dimensions={0}, use_global_device_ids=true | all-gather | bytes 589824 | tf_op jit(solution)/shard_map/all_gather | solution.py:185
  75.1 0.0 copy-start.4
  75.1 7.8 %collective-permute-start.6 = (f32[8,4,32,128]{3,2,1,0:T(8,128)S(1)}, f32[8,4,32,128]{3,2,1,0:T(8,128)S(1)}, u32[]{:S(2)}, u32[]{:S(2)}) collective-permute-start(f32[8,4,32,128]{3,2,1,0:T(8,128)S(1)} %bitcast.8), channel_id=1, source_target_pairs={{0,32},{16,48},{32,0},{48,16},{1,33},{17,49},{33,1},{49,17},{2,34}... | collective-permute-start | bytes 1572872 | tf_op jit(solution)/shard_map/ppermute | solution.py:164
  82.9 6.9 %collective-permute-start.5 = (f32[8,4,32,128]{3,2,1,0:T(8,128)S(1)}, f32[8,4,32,128]{3,2,1,0:T(8,128)S(1)}, u32[]{:S(2)}, u32[]{:S(2)}) collective-permute-start(f32[8,4,32,128]{3,2,1,0:T(8,128)S(1)} %bitcast.9), channel_id=1, source_target_pairs={{0,16},{16,32},{32,48},{48,0},{1,17},{17,33},{33,49},{49,1},{2,18}... | collective-permute-start | bytes 1572872 | tf_op jit(solution)/shard_map/ppermute | solution.py:164
  89.8 1.9 collective-permute-start.4
  91.7 9.6 %collective-permute-start.7 = (f32[8,4,32,128]{3,2,1,0:T(8,128)S(1)}, f32[8,4,32,128]{3,2,1,0:T(8,128)S(1)}, u32[]{:S(2)}, u32[]{:S(2)}) collective-permute-start(f32[8,4,32,128]{3,2,1,0:T(8,128)S(1)} %bitcast.11), channel_id=1, source_target_pairs={{0,8},{8,0},{1,9},{9,1},{2,10},{10,2},{3,11},{11,3},{4,12},{12,4},... | collective-permute-start | bytes 1572872 | tf_op jit(solution)/shard_map/ppermute | solution.py:189
  101.3 0.0 collective-permute-done.6.refs_3_
  101.3 0.0 copy-start.5
  101.3 3.9 %collective-permute-start.10 = (f32[8,4,32,128]{3,2,1,0:T(8,128)S(1)}, f32[8,4,32,128]{3,2,1,0:T(8,128)S(1)}, u32[]{:S(2)}, u32[]{:S(2)}) collective-permute-start(f32[8,4,32,128]{3,2,1,0:T(8,128)S(1)} %collective-permute-done.6.refs_3_), channel_id=1, source_target_pairs={{0,8},{8,0},{1,9},{9,1},{2,10},{10,2},{3,11},{11,3},{4,12},{12,4},... | collective-permute-start | bytes 1572872 | tf_op jit(solution)/shard_map/ppermute | solution.py:189
  105.3 0.0 collective-permute-done.5.refs_2_
  105.3 0.0 copy-start.6
  105.3 4.7 %collective-permute-start.9 = (f32[8,4,32,128]{3,2,1,0:T(8,128)S(1)}, f32[8,4,32,128]{3,2,1,0:T(8,128)}, u32[]{:S(2)}, u32[]{:S(2)}) collective-permute-start(f32[8,4,32,128]{3,2,1,0:T(8,128)S(1)} %collective-permute-done.5.refs_2_), channel_id=1, source_target_pairs={{0,8},{8,0},{1,9},{9,1},{2,10},{10,2},{3,11},{11,3},{4,12},{12,4},... | collective-permute-start | bytes 1572872 | tf_op jit(solution)/shard_map/ppermute | solution.py:189
  110.0 0.0 collective-permute-done.4.refs_1_
  110.1 0.0 copy-start.7
  110.1 3.8 %collective-permute-start.8 = (f32[8,4,32,128]{3,2,1,0:T(8,128)S(1)}, f32[8,4,32,128]{3,2,1,0:T(8,128)}, u32[]{:S(2)}, u32[]{:S(2)}) collective-permute-start(f32[8,4,32,128]{3,2,1,0:T(8,128)S(1)} %collective-permute-done.4.refs_1_), channel_id=1, source_target_pairs={{0,8},{8,0},{1,9},{9,1},{2,10},{10,2},{3,11},{11,3},{4,12},{12,4},... | collective-permute-start | bytes 1572872 | tf_op jit(solution)/shard_map/ppermute | solution.py:189
  114.0 0.7 stack.27.spots
  114.6 0.0 collective-permute-done.7.refs_4_
  114.6 0.0 copy-start.8
  114.7 0.0 collective-permute-done.10.refs_7_
  114.7 0.0 copy-start.9
  114.7 0.0 collective-permute-done.9.refs_6_
  114.7 0.9 collective-permute-done.8.refs_5_
  115.6 0.0 copy-done.4
  115.6 0.0 copy-done.5
  115.6 0.0 copy-done.6
  115.6 0.0 copy-done.7
  115.6 0.0 copy-done.8
  115.6 0.0 copy-done.9
  115.6 128.8 %place.1 = f32[4,8,4,2,32,128]{5,4,3,2,1,0:T(8,128)} custom-call(s32[6]{0:T(128)} %stack.27.spots, f32[8,4,32,128]{3,2,1,0:T(8,128)} %bitcast.12, f32[8,4,32,128]{3,2,1,0:T(8,128)} %copy-done.7, f32[8,4,32,128]{3,2,1,0:T(8,128)} %copy-done.6, f32[8,4,32,128]{3,2,1,0:T(8,128)} %copy-done.5, f32[8,4,32,128]{3,2,1,0:T(8,128)} %copy-done.8, ...), custom_call_target="tpu_custom_call" | custom-call | tf_op jit(solution)/shard_map/place/pallas_call | solution.py:150
Async XLA Ops:
  1.1 19.2 %collective-permute-start.1 = (f32[2,1,32,1024]{3,2,1,0:T(8,128)S(1)}, f32[2,1,32,1024]{3,2,1,0:T(8,128)S(1)}, u32[]{:S(2)}, u32[]{:S(2)}) collective-permute-start(f32[2,1,32,1024]{3,2,1,0:T(8,128)S(1)} %get-tuple-element.7), channel_id=1, source_target_pairs={{1,0},{2,1},{3,2},{4,3},{5,4},{6,5},{7,6},{9,8},{10,9},{11,10},{12... | collective-permute-start | bytes 786440 | tf_op jit(solution)/shard_map/ppermute | solution.py:164
  2.4 17.9 %collective-permute-start = (f32[2,1,32,1024]{3,2,1,0:T(8,128)S(1)}, f32[2,1,32,1024]{3,2,1,0:T(8,128)S(1)}, u32[]{:S(2)}, u32[]{:S(2)}) collective-permute-start(f32[2,1,32,1024]{3,2,1,0:T(8,128)S(1)} %get-tuple-element.8), channel_id=1, source_target_pairs={{0,1},{1,2},{2,3},{3,4},{4,5},{5,6},{6,7},{8,9},{9,10},{10,11},{11... | collective-permute-start | bytes 786440 | tf_op jit(solution)/shard_map/ppermute | solution.py:164
  8.4 11.3 %collective-permute-start.3 = (f32[2,8,1,1024]{3,2,1,0:T(1,128)S(1)}, f32[2,8,1,1024]{3,2,1,0:T(1,128)S(1)}, u32[]{:S(2)}, u32[]{:S(2)}) collective-permute-start(f32[2,8,1,1024]{3,2,1,0:T(1,128)S(1)} %get-tuple-element.5), channel_id=1, source_target_pairs={{8,0},{16,8},{24,16},{32,24},{40,32},{48,40},{56,48},{64,56},{72,6... | collective-permute-start | bytes 196616 | tf_op jit(solution)/shard_map/ppermute | solution.py:172
  17.0 3.2 %collective-permute-start.2 = (f32[2,8,1,1024]{3,2,1,0:T(1,128)S(1)}, f32[2,8,1,1024]{3,2,1,0:T(1,128)S(1)}, u32[]{:S(2)}, u32[]{:S(2)}) collective-permute-start(f32[2,8,1,1024]{3,2,1,0:T(1,128)S(1)} %get-tuple-element.6), channel_id=1, source_target_pairs={{0,8},{8,16},{16,24},{24,32},{32,40},{40,48},{48,56},{56,64},{64,7... | collective-permute-start | bytes 196616 | tf_op jit(solution)/shard_map/ppermute | solution.py:172
  21.0 1.6 copy-start
  22.6 1.6 copy-start.1
  24.2 0.7 copy-start.3
  24.9 8.3 %copy-start.2 = (s32[32,128]{1,0:T(8,128)}, s32[32,128]{1,0:T(8,128)S(1)}, u32[]{:S(2)}) copy-start(s32[32,128]{1,0:T(8,128)S(1)} %broadcast_in_dim.2.back) | copy-start | bytes 49156
  75.1 40.4 %copy-start.4 = (f32[32,32,128]{2,1,0:T(8,128)}, f32[32,32,128]{2,1,0:T(8,128)S(1)}, u32[]{:S(2)}) copy-start(f32[32,32,128]{2,1,0:T(8,128)S(1)} %all-gather) | copy-start | bytes 1572868
  75.1 26.2 %collective-permute-start.6 = (f32[8,4,32,128]{3,2,1,0:T(8,128)S(1)}, f32[8,4,32,128]{3,2,1,0:T(8,128)S(1)}, u32[]{:S(2)}, u32[]{:S(2)}) collective-permute-start(f32[8,4,32,128]{3,2,1,0:T(8,128)S(1)} %bitcast.8), channel_id=1, source_target_pairs={{0,32},{16,48},{32,0},{48,16},{1,33},{17,49},{33,1},{49,17},{2,34}... | collective-permute-start | bytes 1572872 | tf_op jit(solution)/shard_map/ppermute | solution.py:164
  82.9 22.4 %collective-permute-start.5 = (f32[8,4,32,128]{3,2,1,0:T(8,128)S(1)}, f32[8,4,32,128]{3,2,1,0:T(8,128)S(1)}, u32[]{:S(2)}, u32[]{:S(2)}) collective-permute-start(f32[8,4,32,128]{3,2,1,0:T(8,128)S(1)} %bitcast.9), channel_id=1, source_target_pairs={{0,16},{16,32},{32,48},{48,0},{1,17},{17,33},{33,49},{49,1},{2,18}... | collective-permute-start | bytes 1572872 | tf_op jit(solution)/shard_map/ppermute | solution.py:164
  89.8 20.3 %collective-permute-start.4 = (f32[8,4,32,128]{3,2,1,0:T(8,128)S(1)}, f32[8,4,32,128]{3,2,1,0:T(8,128)S(1)}, u32[]{:S(2)}, u32[]{:S(2)}) collective-permute-start(f32[8,4,32,128]{3,2,1,0:T(8,128)S(1)} %bitcast.10), channel_id=1, source_target_pairs={{0,48},{16,0},{32,16},{48,32},{1,49},{17,1},{33,17},{49,33},{2,50}... | collective-permute-start | bytes 1572872 | tf_op jit(solution)/shard_map/ppermute | solution.py:164
  91.7 22.9 %collective-permute-start.7 = (f32[8,4,32,128]{3,2,1,0:T(8,128)S(1)}, f32[8,4,32,128]{3,2,1,0:T(8,128)S(1)}, u32[]{:S(2)}, u32[]{:S(2)}) collective-permute-start(f32[8,4,32,128]{3,2,1,0:T(8,128)S(1)} %bitcast.11), channel_id=1, source_target_pairs={{0,8},{8,0},{1,9},{9,1},{2,10},{10,2},{3,11},{11,3},{4,12},{12,4},... | collective-permute-start | bytes 1572872 | tf_op jit(solution)/shard_map/ppermute | solution.py:189
  101.3 14.2 %copy-start.5 = (f32[8,4,32,128]{3,2,1,0:T(8,128)}, f32[8,4,32,128]{3,2,1,0:T(8,128)S(1)}, u32[]{:S(2)}) copy-start(f32[8,4,32,128]{3,2,1,0:T(8,128)S(1)} %collective-permute-done.6.refs_3_) | copy-start | bytes 1572868
  101.3 13.3 %collective-permute-start.10 = (f32[8,4,32,128]{3,2,1,0:T(8,128)S(1)}, f32[8,4,32,128]{3,2,1,0:T(8,128)S(1)}, u32[]{:S(2)}, u32[]{:S(2)}) collective-permute-start(f32[8,4,32,128]{3,2,1,0:T(8,128)S(1)} %collective-permute-done.6.refs_3_), channel_id=1, source_target_pairs={{0,8},{8,0},{1,9},{9,1},{2,10},{10,2},{3,11},{11,3},{4,12},{12,4},... | collective-permute-start | bytes 1572872 | tf_op jit(solution)/shard_map/ppermute | solution.py:189
  105.3 10.3 %copy-start.6 = (f32[8,4,32,128]{3,2,1,0:T(8,128)}, f32[8,4,32,128]{3,2,1,0:T(8,128)S(1)}, u32[]{:S(2)}) copy-start(f32[8,4,32,128]{3,2,1,0:T(8,128)S(1)} %collective-permute-done.5.refs_2_) | copy-start | bytes 1572868
  105.3 9.4 %collective-permute-start.9 = (f32[8,4,32,128]{3,2,1,0:T(8,128)S(1)}, f32[8,4,32,128]{3,2,1,0:T(8,128)}, u32[]{:S(2)}, u32[]{:S(2)}) collective-permute-start(f32[8,4,32,128]{3,2,1,0:T(8,128)S(1)} %collective-permute-done.5.refs_2_), channel_id=1, source_target_pairs={{0,8},{8,0},{1,9},{9,1},{2,10},{10,2},{3,11},{11,3},{4,12},{12,4},... | collective-permute-start | bytes 1572872 | tf_op jit(solution)/shard_map/ppermute | solution.py:189
  110.1 5.5 %copy-start.7 = (f32[8,4,32,128]{3,2,1,0:T(8,128)}, f32[8,4,32,128]{3,2,1,0:T(8,128)S(1)}, u32[]{:S(2)}) copy-start(f32[8,4,32,128]{3,2,1,0:T(8,128)S(1)} %collective-permute-done.4.refs_1_) | copy-start | bytes 1572868
  110.1 5.5 %collective-permute-start.8 = (f32[8,4,32,128]{3,2,1,0:T(8,128)S(1)}, f32[8,4,32,128]{3,2,1,0:T(8,128)}, u32[]{:S(2)}, u32[]{:S(2)}) collective-permute-start(f32[8,4,32,128]{3,2,1,0:T(8,128)S(1)} %collective-permute-done.4.refs_1_), channel_id=1, source_target_pairs={{0,8},{8,0},{1,9},{9,1},{2,10},{10,2},{3,11},{11,3},{4,12},{12,4},... | collective-permute-start | bytes 1572872 | tf_op jit(solution)/shard_map/ppermute | solution.py:189
  114.6 0.9 copy-start.8
  114.7 1.0 copy-start.9

commit v2 on v0

v2 whole, which is shorter than its diff:
```python
import jax
import jax.numpy as jnp
from jax import lax
from jax.experimental import pallas as pl
from jax.experimental.pallas import tpu as pltpu
from jax.sharding import Mesh, PartitionSpec as P

LANES = 128
SUBS = 8
COLOUR_UNIT = 2.0**-12
OPACITY_UNIT = 2.0**-18
FIELD = 1 << 13

LOOKUP = lax.GatherDimensionNumbers(
    offset_dims=(),
    collapsed_slice_dims=(1,),
    start_index_map=(1,),
    operand_batching_dims=(0,),
    start_indices_batching_dims=(0,),
)


def pick(table, lanes):
    return lax.gather(table, lanes[..., None], LOOKUP, (1, 1), mode=lax.GatherScatterMode.PROMISE_IN_BOUNDS)


def store_tables(colour_ref, opacity_ref, tab):
    for f in range(2):
        colour = [(colour_ref[f, k : k + 1, :].astype(jnp.float32) / COLOUR_UNIT).astype(jnp.int32) for k in range(3)]
        opacity = (opacity_ref[f : f + 1, :].astype(jnp.float32) / OPACITY_UNIT).astype(jnp.int32)
        for w, word in enumerate((colour[0] + colour[1] * FIELD, colour[2] + opacity * FIELD)):
            for h in range(2):
                tab[f, w, h] = jnp.broadcast_to(word[:, h * LANES : (h + 1) * LANES], (SUBS, LANES))


def masks():
    sub = lax.broadcasted_iota(jnp.int32, (SUBS, LANES), 0)
    lane = lax.broadcasted_iota(jnp.int32, (SUBS, LANES), 1)
    return sub == 0, sub == SUBS - 1, lane == 0, lane == LANES - 1


def cell(at, bins_of, tab, edges):
    first_sub, last_sub, first_lane, last_lane = edges
    colour = clear = None
    for f in range(2):
        here = at(f, 0, 0, 0)
        dz = at(f, 1, 0, 0) - at(f, -1, 0, 0)
        after = pltpu.roll(jnp.where(first_sub, at(f, 0, SUBS, 0), here), SUBS - 1, 0)
        before = pltpu.roll(jnp.where(last_sub, at(f, 0, -SUBS, 0), here), 1, 0)
        dx = after - before
        after = pltpu.roll(jnp.where(first_lane, at(f, 0, 0, LANES), here), LANES - 1, 1)
        before = pltpu.roll(jnp.where(last_lane, at(f, 0, 0, -LANES), here), 1, 1)
        dy = after - before
        total = dz * dz + dx * dx + dy * dy
        shade = 0.3 + (0.35 * jnp.abs(dz)) * lax.rsqrt(0.25 * total + 1.0)
        root = total * lax.rsqrt(jnp.maximum(total, 1e-30))
        gain = 0.25 * OPACITY_UNIT + (0.5 * OPACITY_UNIT) * root
        entry = bins_of(f)
        low = entry & (LANES - 1)
        upper = entry >= LANES
        words = [jnp.where(upper, pick(tab[f, w, 1], low), pick(tab[f, w, 0], low)) for w in range(2)]
        alpha = (words[1] >> 13).astype(jnp.float32) * gain
        lit = alpha * shade
        looked = (words[0] & (FIELD - 1), words[0] >> 13, words[1] & (FIELD - 1))
        terms = [lit * value.astype(jnp.float32) for value in looked]
        colour = terms if colour is None else [a + b for a, b in zip(colour, terms)]
        clear = 1.0 - alpha if clear is None else clear * (1.0 - alpha)
    return colour, clear


def composite(elements, backward):
    colour = through = None
    for part, clear in elements:
        if colour is None:
            colour, through = part, clear
        else:
            keep = jnp.where(backward, clear, 1.0)
            weight = jnp.where(backward, 1.0, through)
            colour = [a * keep + weight * b for a, b in zip(colour, part)]
            through = through * clear
    return colour, through


def inner_kernel(fields, bins, colour, opacity, back, cells, picks, mid, tab, field_sem, bin_sem):
    depth, cols, rows = fields.shape[1:]
    groups = cols // SUBS
    spans = [pl.ds(g * SUBS, SUBS) for g in range(groups)]
    field_copies, bin_copies = [], []
    for g, span in enumerate(spans):
        target = cells.at[:, :, span, pl.ds(LANES, rows)]
        field_copies.append(pltpu.make_async_copy(fields.at[:, :, span, :], target, field_sem.at[g]))
        bin_copies.append(pltpu.make_async_copy(bins.at[:, :, span, :], picks.at[:, :, span, :], bin_sem.at[g]))
    for copy in field_copies[:3] + [bin_copies[1]] + field_copies[3:] + bin_copies[2:] + [bin_copies[0]]:
        copy.start()
    zero = jnp.zeros((cols, LANES), jnp.float32)
    for f in range(2):
        for d in range(depth):
            cells[f, d, :, 0:LANES] = zero
            cells[f, d, :, LANES + rows :] = zero
    store_tables(colour, opacity, tab)
    edges = masks()
    field_copies[0].wait()
    for g in range(1, groups - 1):
        if g == 1:
            field_copies[1].wait()
        field_copies[g + 1].wait()
        bin_copies[g].wait()
        backward = back[g * SUBS : (g + 1) * SUBS, :] == 1

        def tile(b, carry, g=g, backward=backward):
            start = pl.multiple_of(b * LANES, LANES)

            def element(d):
                def at(f, dd, dc, dr):
                    return cells[f, d + dd, pl.ds(g * SUBS + dc, SUBS), pl.ds(start + (LANES + dr), LANES)]

                def bins_of(f):
                    return picks[f, d, pl.ds(g * SUBS, SUBS), pl.ds(start, LANES)]

                return cell(at, bins_of, tab, edges)

            parts, through = composite((element(d) for d in range(1, depth - 1)), backward)
            for k, part in enumerate(parts + [through]):
                mid[b, k, pl.ds((g - 1) * SUBS, SUBS), :] = part
            return carry

        lax.fori_loop(0, rows // LANES, tile, 0)
    bin_copies[0].wait()
    bin_copies[groups - 1].wait()


def outer_kernel(cells, zlo, zhi, xlo, xhi, picks, mid, colour, opacity, back, out, tab):
    depth, cols, rows = picks.shape[1:]
    groups = cols // SUBS
    store_tables(colour, opacity, tab)
    edges = masks()
    for g in range(groups):
        backward = back[g * SUBS : (g + 1) * SUBS, :] == 1
        inside = 0 < g < groups - 1

        def tile(b, carry, g=g, backward=backward, inside=inside):
            start = pl.multiple_of(b * LANES, LANES)
            here = pl.ds(start, LANES)

            def element(d):
                def at(f, dd, dc, dr):
                    if d + dd < 0:
                        return zlo[f, 0, pl.ds(g * SUBS, SUBS), here]
                    if d + dd == depth:
                        return zhi[f, 0, pl.ds(g * SUBS, SUBS), here]
                    if g * SUBS + dc < 0:
                        return jnp.broadcast_to(xlo[f, d, :, here], (SUBS, LANES))
                    if g * SUBS + dc == cols:
                        return jnp.broadcast_to(xhi[f, d, :, here], (SUBS, LANES))
                    return cells[f, d + dd, pl.ds(g * SUBS + dc, SUBS), pl.ds(start + (LANES + dr), LANES)]

                def bins_of(f):
                    return picks[f, d, pl.ds(g * SUBS, SUBS), here]

                return cell(at, bins_of, tab, edges)

            def middle():
                parts = [mid[b, k, pl.ds((g - 1) * SUBS, SUBS), :] for k in range(4)]
                return parts[:3], parts[3]

            if inside:
                elements = (element(0) if n == 0 else middle() if n == 1 else element(depth - 1) for n in range(3))
            else:
                elements = (element(d) for d in range(depth))
            parts, through = composite(elements, backward)
            for k, part in enumerate(parts):
                out[b, k, pl.ds(g * SUBS, SUBS), :] = part * COLOUR_UNIT
            out[b, 3, pl.ds(g * SUBS, SUBS), :] = 1.0 - through
            return carry

        lax.fori_loop(0, rows // LANES, tile, 0)


VMEM = pl.BlockSpec(memory_space=pltpu.VMEM)
SMEM = pl.BlockSpec(memory_space=pltpu.SMEM)
ANY = pl.BlockSpec(memory_space=pl.ANY)
LIMIT = 24 * 2**20


TAB = pltpu.VMEM((2, 2, 2, SUBS, LANES), jnp.int32)


def march_inner(fields, bins, colour, opacity, back):
    _, depth, cols, rows = fields.shape
    within = cols - 2 * SUBS
    return pl.pallas_call(
        inner_kernel,
        out_shape=[
            pltpu.VMEM((2, depth, cols, rows + 2 * LANES), jnp.float32),
            pltpu.VMEM((2, depth, cols, rows), jnp.int32),
            pltpu.VMEM((rows // LANES, 4, within, LANES), jnp.float32),
        ],
        in_specs=[ANY, ANY, VMEM, VMEM, VMEM],
        out_specs=[VMEM] * 3,
        scratch_shapes=[TAB, pltpu.SemaphoreType.DMA((cols // SUBS,)), pltpu.SemaphoreType.DMA((cols // SUBS,))],
        compiler_params=pltpu.CompilerParams(vmem_limit_bytes=LIMIT),
        cost_estimate=pl.CostEstimate(flops=100 * 2 * (depth - 2) * within * rows, bytes_accessed=8 * 2**20, transcendentals=0),
        name="march_inner",
    )(
        pltpu.with_memory_space_constraint(fields, pltpu.HBM),
        pltpu.with_memory_space_constraint(bins, pltpu.HBM),
        colour,
        opacity,
        back,
    )


def march_outer(cells, zlo, zhi, xlo, xhi, picks, mid, colour, opacity, back):
    _, depth, cols, rows = picks.shape
    return pl.pallas_call(
        outer_kernel,
        out_shape=jax.ShapeDtypeStruct((rows // LANES, 4, cols, LANES), jnp.float32),
        in_specs=[VMEM] * 10,
        out_specs=VMEM,
        scratch_shapes=[TAB],
        compiler_params=pltpu.CompilerParams(vmem_limit_bytes=LIMIT),
        name="march_outer",
    )(cells, zlo, zhi, xlo, xhi, picks, mid, colour, opacity, back)


def join_kernel(parts, back, out):
    depth, _, cols, _ = parts.shape
    for group in range(cols // SUBS):
        span = pl.ds(group * SUBS, SUBS)
        elements = (([parts[d, k, span, :] for k in range(3)], 1.0 - parts[d, 3, span, :]) for d in range(depth))
        colour, through = composite(elements, back[span, :] == 1)
        for k in range(3):
            out[k, span, :] = colour[k]
        out[3, span, :] = 1.0 - through


def join(parts, back):
    return pl.pallas_call(
        join_kernel,
        out_shape=jax.ShapeDtypeStruct(parts.shape[1:], jnp.float32),
        in_specs=[VMEM, VMEM],
        out_specs=VMEM,
        name="join",
    )(parts, back)


def place_kernel(spots, *refs):
    pieces, out = refs[:-1], refs[-1]
    x_count = len(pieces) // 2
    channel = pl.program_id(0)
    for n, piece in enumerate(pieces):
        x, c = spots[n % x_count], spots[x_count + n // x_count]
        for high in range(2):
            for mid in range(2):
                for low in range(2):
                    out[0, 4 * high + 2 * mid + low, x, c] = piece[low, mid, high, channel]


def place(pieces, others, spots):
    x_count = len(pieces)
    channels, cols, rows = pieces[0].shape[3:]
    whole = (channels, 8, x_count, 2, cols, rows)
    frame = pl.pallas_call(
        place_kernel,
        grid=(channels,),
        out_shape=jax.ShapeDtypeStruct(whole, jnp.float32),
        in_specs=[SMEM] + [VMEM] * (2 * x_count),
        out_specs=pl.BlockSpec((1,) + whole[1:], lambda channel: (channel, 0, 0, 0, 0, 0)),
        compiler_params=pltpu.CompilerParams(vmem_limit_bytes=LIMIT),
        name="place",
    )(spots, *pieces, *others)
    return frame.reshape(channels, 16 * x_count * cols, rows)


def shifted(value, axis, step, wrap=True):
    count = lax.axis_size(axis)
    route = [(i, (i + step) % count) for i in range(count) if wrap or 0 <= i + step < count]
    return lax.ppermute(value, axis, route)


WIDE = ("z_high", "z_mid", "z_low", "x", "core")


def on_device(fields, field_bins, colour_table, opacity_table, view_dir):
    depth, cols = fields.shape[1:3]
    zlo = shifted(fields[:, depth - 1 :], "y", 1, wrap=False)
    zhi = shifted(fields[:, :1], "y", -1, wrap=False)
    xlo = shifted(fields[:, :, cols - 1 :], WIDE, 1, wrap=False)
    xhi = shifted(fields[:, :, :1], WIDE, -1, wrap=False)
    back = jnp.broadcast_to(view_dir[:, None], (cols, LANES))
    cells, picks, mid = march_inner(fields, field_bins, colour_table, opacity_table, back)
    partial = march_outer(cells, zlo, zhi, xlo, xhi, picks, mid, colour_table, opacity_table, back)
    partial = lax.all_to_all(partial, "y", 0, 0)
    column = join(partial, back)
    for axis in ("z_high", "z_mid", "z_low"):
        column = lax.all_gather(column, axis)
    x_count = lax.axis_size("x")
    steps = [0, 1, x_count - 1] + list(range(2, x_count - 1))
    pieces = [column] + [shifted(column, "x", -step) for step in steps[1:]]
    others = [lax.ppermute(piece, "core", [(0, 1), (1, 0)]) for piece in pieces]
    x, core = lax.axis_index("x"), lax.axis_index("core")
    spots = jnp.stack([(x + step) % x_count for step in steps] + [core, 1 - core])
    return place(pieces, others, spots)


def solution(mesh):
    grid = Mesh(mesh.devices.reshape(2, 2, 2, 4, 2, 8), WIDE + ("y",))
    split = P(None, "y", WIDE, None)
    return jax.shard_map(
        on_device,
        mesh=grid,
        in_specs=(split, split, P(), P(), P(WIDE)),
        out_specs=P(None, None, "y"),
        check_vma=False,
    )
```

time: 329 us -> 123 us (0.37)
  waiting for transfers between devices: 113 us -> 9.5 us
  matrix products: 87.7 us -> 0 us
  blocking collectives: 0 us -> 48.3 us
  local copies, waits for them, and re-layouts: 37.7 us -> 4.55 us
  other arithmetic: 30.5 us -> 0 us
  loops' own time: 17.7 us -> 0 us
  Pallas kernels: 0 us -> 16.3 us
  starting transfers between devices: 27.5 us -> 43.8 us
  between operations: 13.7 us -> 0.21 us
    all_gather x1 -> x0, waiting for transfers between devices: 88.7 us -> none  [on_device(): return lax.all_gather(finished, 'wide', axis=1, tiled=True)]
    dot_general x64 -> x0, matrix products: 87.7 us -> none  [one_block(): return jnp.dot(table_rows, one_hot, preferred_element_type=jnp.float32)]
    all_gather x0 -> x3, blocking collectives: none -> 27.5 us  [on_device(): column = lax.all_gather(column, axis)]
    all_to_all x0 -> x1, blocking collectives: none -> 20.8 us  [on_device(): partial = lax.all_to_all(partial, 'y', 0, 0)]
    another operation x17 -> x0, loops' own time: 17.7 us -> none  [the longest x1 17.1 us: on_device(): lax.scan(march_step, start, jnp.arange(depth_count, dtype=jnp.int32))]
    pallas_call x0 -> x4, Pallas kernels: none -> 16.3 us  [the longest x1 6.06 us: march_outer(): pl.pallas_call(outer_kernel, out_shape=jax.ShapeDtypeStruct((rows // LANE...]
    ppermute x7 -> x11, starting transfers between devices: 27.5 us -> 43.8 us  [the longest x7 30.1 us: shifted(): return lax.ppermute(value, axis, route)]
    mul x27 -> x0, other arithmetic: 16.2 us -> none  [the longest x8 8.15 us: make_sample(): opacity[0] * shading[0] * looked_up[0, :3]]
  transfers between devices with their start and end apart: 8 -> 11, of which waited for: 6 -> 3; matrix products, arithmetic and copies ran while one was open for 1% -> 2% of each run, Pallas kernels for 0% -> 4%
where the time goes in v2:
time: 123 us
  blocking collectives  48.3 us (39%)
  starting transfers between devices  43.8 us (36%)
  Pallas kernels  16.3 us (13%)
  waiting for transfers between devices  9.5 us (8%)
  local copies, waits for them, and re-layouts  4.55 us (4%)
    ppermute x7, starting transfers between devices, shifted(): return lax.ppermute(value, axis, route)  30.1 us
    all_gather x3, blocking collectives, on_device(): column = lax.all_gather(column, axis)  27.5 us
    all_to_all x1, blocking collectives, on_device(): partial = lax.all_to_all(partial, 'y', 0, 0)  20.8 us
    ppermute x4, starting transfers between devices, on_device(): others = [lax.ppermute(piece, 'core', [(0, 1), (1, 0)]) for piece in pieces]  13.8 us
    ppermute x7, waiting for transfers between devices, shifted(): return lax.ppermute(value, axis, route)  7.63 us
    pallas_call x1, Pallas kernels, march_outer(): pl.pallas_call(outer_kernel, out_shape=jax.ShapeDtypeStruct((rows // LANE...  6.06 us
    pallas_call x1, Pallas kernels, march_inner(): pl.pallas_call(inner_kernel, out_shape=[pltpu.VMEM((2, depth, cols, rows...  4.89 us
    pallas_call x1, Pallas kernels, place(): pl.pallas_call(place_kernel, grid=(channels,), out_shape=jax.ShapeDtypeSt...  3.65 us
  transfers between devices with their start and end apart: 11, of which 3 were waited for; matrix products, arithmetic and copies ran while one was open for 2% of the time, Pallas kernels for 4%

profile of v2, /device:TPU:1, one launch (start us, length us, event | category | flops | bytes accessed | tf_op | source)
XLA Modules:
  0.0 122.8 jit_solution(9672105660364676426)
XLA Ops:
  0.0 1.1 fusion.1
  1.1 1.3 %collective-permute-start.1 = (f32[2,1,32,1024]{3,2,1,0:T(8,128)S(1)}, f32[2,1,32,1024]{3,2,1,0:T(8,128)S(1)}, u32[]{:S(2)}, u32[]{:S(2)}) collective-permute-start(f32[2,1,32,1024]{3,2,1,0:T(8,128)S(1)} %get-tuple-element.13), channel_id=1, source_target_pairs={{1,0},{2,1},{3,2},{4,3},{5,4},{6,5},{7,6},{9,8},{10,9},{11,10},{12... | collective-permute-start | bytes 786440 | tf_op jit(solution)/shard_map/ppermute | solution.py:278
  2.4 4.7 %collective-permute-start = (f32[2,1,32,1024]{3,2,1,0:T(8,128)S(1)}, f32[2,1,32,1024]{3,2,1,0:T(8,128)S(1)}, u32[]{:S(2)}, u32[]{:S(2)}) collective-permute-start(f32[2,1,32,1024]{3,2,1,0:T(8,128)S(1)} %get-tuple-element.14), channel_id=1, source_target_pairs={{0,1},{1,2},{2,3},{3,4},{4,5},{5,6},{6,7},{8,9},{9,10},{10,11},{11... | collective-permute-start | bytes 786440 | tf_op jit(solution)/shard_map/ppermute | solution.py:278
  7.1 1.3 %fusion = (f32[2,8,1,1024]{3,2,1,0:T(1,128)S(1)}, f32[2,8,1,1024]{3,2,1,0:T(1,128)S(1)}) fusion(f32[2,8,32,1024]{3,2,1,0:T(8,128)} %fields.1), kind=kLoop, calls=%fused_computation | loop fusion | bytes 262144 | tf_op jit(solution)/shard_map/slice | solution.py:289
  8.4 8.7 %collective-permute-start.3 = (f32[2,8,1,1024]{3,2,1,0:T(1,128)S(1)}, f32[2,8,1,1024]{3,2,1,0:T(1,128)S(1)}, u32[]{:S(2)}, u32[]{:S(2)}) collective-permute-start(f32[2,8,1,1024]{3,2,1,0:T(1,128)S(1)} %get-tuple-element.11), channel_id=1, source_target_pairs={{8,0},{16,8},{24,16},{32,24},{40,32},{48,40},{56,48},{64,56},{72,6... | collective-permute-start | bytes 196616 | tf_op jit(solution)/shard_map/ppermute | solution.py:278
  17.0 1.9 %collective-permute-start.2 = (f32[2,8,1,1024]{3,2,1,0:T(1,128)S(1)}, f32[2,8,1,1024]{3,2,1,0:T(1,128)S(1)}, u32[]{:S(2)}, u32[]{:S(2)}) collective-permute-start(f32[2,8,1,1024]{3,2,1,0:T(1,128)S(1)} %get-tuple-element.12), channel_id=1, source_target_pairs={{0,8},{8,16},{16,24},{24,32},{32,40},{40,48},{48,56},{56,64},{64,7... | collective-permute-start | bytes 196616 | tf_op jit(solution)/shard_map/ppermute | solution.py:278
  19.0 0.7 copy.8.colour
  19.7 0.7 broadcast_in_dim.2.back
  20.4 0.0 copy-start.1
  20.4 0.7 copy-done.1
  21.1 0.0 copy-start
  21.1 4.9 %march_inner.1 = (f32[2,8,32,1280]{3,2,1,0:T(8,128)S(1)}, s32[2,8,32,1024]{3,2,1,0:T(8,128)S(1)}, f32[8,4,16,128]{3,2,1,0:T(8,128)S(1)}) custom-call(f32[2,8,32,1024]{3,2,1,0:T(8,128)} %fields.1, s32[2,8,32,1024]{3,2,1,0:T(8,128)} %bins.1, bf16[2,3,256]{2,1,0:T(4,128)(2,1)S(1)} %copy.8.colour, bf16[2,256]{1,0:T(2,128)(2,1)S(1)} %copy-done.1, ...), custom_call_target="tpu_custom_call" | custom-call | flops 19660800 | bytes 8388608 | tf_op jit(solution)/shard_map/march_inner/pallas_call | solution.py:191
  26.0 0.0 collective-permute-done.3.xhi
  26.0 0.0 collective-permute-done.2.xlo
  26.0 0.0 collective-permute-done.1.zhi
  26.0 0.0 collective-permute-done.zlo
  26.0 0.0 copy-done
  26.0 6.1 %march_outer.1 = f32[8,4,32,128]{3,2,1,0:T(8,128)S(1)} custom-call(f32[2,8,32,1280]{3,2,1,0:T(8,128)S(1)} %get-tuple-element.8.cells, f32[2,1,32,1024]{3,2,1,0:T(8,128)S(1)} %collective-permute-done.zlo, f32[2,1,32,1024]{3,2,1,0:T(8,128)S(1)} %collective-permute-done.1.zhi, f32[2,8,1,1024]{3,2,1,0:T(1,128)S(1)} %collective-permute-done.2.xlo, ...), custom_call_target="tpu_custom_call" | custom-call | tf_op jit(solution)/shard_map/march_outer/pallas_call | solution.py:215
  32.1 20.8 %all_to_all.5.parts = f32[8,4,32,128]{3,2,1,0:T(8,128)} all-to-all(f32[8,4,32,128]{3,2,1,0:T(8,128)S(1)} %march_outer.1), channel_id=1, replica_groups=mesh['z_high'=2,'z_mid'=2,'z_low'=2,'x'=4,'core'=2,'y'=8] {'y'}, dimensions={0} | all-to-all | bytes 1048576 | tf_op jit(solution)/shard_map/all_to_all | solution.py:293
  52.9 1.7 %join.1 = f32[4,32,128]{2,1,0:T(8,128)} custom-call(f32[8,4,32,128]{3,2,1,0:T(8,128)} %all_to_all.5.parts, s32[32,128]{1,0:T(8,128)} %copy-done), custom_call_target="tpu_custom_call" | custom-call | tf_op jit(solution)/shard_map/join/pallas_call | solution.py:238
  54.6 11.4 %all-gather = f32[8,32,128]{2,1,0:T(8,128)S(1)} all-gather(f32[4,32,128]{2,1,0:T(8,128)} %join.1), channel_id=2, replica_groups=mesh['z_high'=2,'z_mid'=2,'z_low'=2,'x'=4,'core'=2,'y'=8] {'z_high'}, dimensions={0}, use_global_device_ids=true | all-gather | bytes 196608 | tf_op jit(solution)/shard_map/all_gather | solution.py:296
  66.0 8.8 %all-gather.1 = f32[4,4,32,128]{3,2,1,0:T(8,128)S(1)} all-gather(f32[2,4,32,128]{3,2,1,0:T(8,128)S(1)} %bitcast.16), channel_id=3, replica_groups=mesh['z_high'=2,'z_mid'=2,'z_low'=2,'x'=4,'core'=2,'y'=8] {'z_mid'}, dimensions={0}, use_global_device_ids=true | all-gather | bytes 393216 | tf_op jit(solution)/shard_map/all_gather | solution.py:296
  74.8 7.4 %all-gather.2 = f32[4,2,4,32,128]{4,3,2,1,0:T(8,128)S(1)} all-gather(f32[2,2,4,32,128]{4,3,2,1,0:T(8,128)S(1)} %bitcast.15), channel_id=4, replica_groups=mesh['z_high'=2,'z_mid'=2,'z_low'=2,'x'=4,'core'=2,'y'=8] {'z_low'}, dimensions={0}, use_global_device_ids=true | all-gather | bytes 786432 | tf_op jit(solution)/shard_map/all_gather | solution.py:296
  82.2 7.0 %collective-permute-start.6 = (f32[2,2,2,4,32,128]{5,4,3,2,1,0:T(8,128)S(1)}, f32[2,2,2,4,32,128]{5,4,3,2,1,0:T(8,128)S(1)}, u32[]{:S(2)}, u32[]{:S(2)}) collective-permute-start(f32[2,2,2,4,32,128]{5,4,3,2,1,0:T(8,128)S(1)} %bitcast.10), channel_id=1, source_target_pairs={{0,32},{16,48},{32,0},{48,16},{1,33},{17,49},{33,1},{49,17},{2,34}... | collective-permute-start | bytes 1572872 | tf_op jit(solution)/shard_map/ppermute | solution.py:278
  89.2 2.0 %collective-permute-start.5 = (f32[2,2,2,4,32,128]{5,4,3,2,1,0:T(8,128)S(1)}, f32[2,2,2,4,32,128]{5,4,3,2,1,0:T(8,128)S(1)}, u32[]{:S(2)}, u32[]{:S(2)}) collective-permute-start(f32[2,2,2,4,32,128]{5,4,3,2,1,0:T(8,128)S(1)} %bitcast.11), channel_id=1, source_target_pairs={{0,16},{16,32},{32,48},{48,0},{1,17},{17,33},{33,49},{49,1},{2,18}... | collective-permute-start | bytes 1572872 | tf_op jit(solution)/shard_map/ppermute | solution.py:278
  91.2 4.5 %collective-permute-start.4 = (f32[2,2,2,4,32,128]{5,4,3,2,1,0:T(8,128)S(1)}, f32[2,2,2,4,32,128]{5,4,3,2,1,0:T(8,128)S(1)}, u32[]{:S(2)}, u32[]{:S(2)}) collective-permute-start(f32[2,2,2,4,32,128]{5,4,3,2,1,0:T(8,128)S(1)} %bitcast.12), channel_id=1, source_target_pairs={{0,48},{16,0},{32,16},{48,32},{1,49},{17,1},{33,17},{49,33},{2,50}... | collective-permute-start | bytes 1572872 | tf_op jit(solution)/shard_map/ppermute | solution.py:278
  95.7 4.1 %collective-permute-start.7 = (f32[2,2,2,4,32,128]{5,4,3,2,1,0:T(8,128)S(1)}, f32[2,2,2,4,32,128]{5,4,3,2,1,0:T(8,128)S(1)}, u32[]{:S(2)}, u32[]{:S(2)}) collective-permute-start(f32[2,2,2,4,32,128]{5,4,3,2,1,0:T(8,128)S(1)} %bitcast.13), channel_id=1, source_target_pairs={{0,8},{8,0},{1,9},{9,1},{2,10},{10,2},{3,11},{11,3},{4,12},{12,4},... | collective-permute-start | bytes 1572872 | tf_op jit(solution)/shard_map/ppermute | solution.py:300
  99.7 0.4 collective-permute-done.6.refs_3_
  100.1 5.4 %collective-permute-start.10 = (f32[2,2,2,4,32,128]{5,4,3,2,1,0:T(8,128)S(1)}, f32[2,2,2,4,32,128]{5,4,3,2,1,0:T(8,128)S(1)}, u32[]{:S(2)}, u32[]{:S(2)}) collective-permute-start(f32[2,2,2,4,32,128]{5,4,3,2,1,0:T(8,128)S(1)} %collective-permute-done.6.refs_3_), channel_id=1, source_target_pairs={{0,8},{8,0},{1,9},{9,1},{2,10},{10,2},{3,11},{11,3},{4,12},{12,4},... | collective-permute-start | bytes 1572872 | tf_op jit(solution)/shard_map/ppermute | solution.py:300
  105.5 7.2 %collective-permute-done.5.refs_2_ = f32[2,2,2,4,32,128]{5,4,3,2,1,0:T(8,128)S(1)} collective-permute-done((f32[2,2,2,4,32,128]{5,4,3,2,1,0:T(8,128)S(1)}, f32[2,2,2,4,32,128]{5,4,3,2,1,0:T(8,128)S(1)}, u32[]{:S(2)}, u32[]{:S(2)}) %collective-permute-start.5) | collective-permute-done | bytes 524320 | tf_op jit(solution)/shard_map/ppermute | solution.py:278
  112.8 2.4 %collective-permute-start.9 = (f32[2,2,2,4,32,128]{5,4,3,2,1,0:T(8,128)S(1)}, f32[2,2,2,4,32,128]{5,4,3,2,1,0:T(8,128)}, u32[]{:S(2)}, u32[]{:S(2)}) collective-permute-start(f32[2,2,2,4,32,128]{5,4,3,2,1,0:T(8,128)S(1)} %collective-permute-done.5.refs_2_), channel_id=1, source_target_pairs={{0,8},{8,0},{1,9},{9,1},{2,10},{10,2},{3,11},{11,3},{4,12},{12,4},... | collective-permute-start | bytes 1572872 | tf_op jit(solution)/shard_map/ppermute | solution.py:300
  115.2 0.0 collective-permute-done.4.refs_1_
  115.2 1.9 %collective-permute-start.8 = (f32[2,2,2,4,32,128]{5,4,3,2,1,0:T(8,128)S(1)}, f32[2,2,2,4,32,128]{5,4,3,2,1,0:T(8,128)}, u32[]{:S(2)}, u32[]{:S(2)}) collective-permute-start(f32[2,2,2,4,32,128]{5,4,3,2,1,0:T(8,128)S(1)} %collective-permute-done.4.refs_1_), channel_id=1, source_target_pairs={{0,8},{8,0},{1,9},{9,1},{2,10},{10,2},{3,11},{11,3},{4,12},{12,4},... | collective-permute-start | bytes 1572872 | tf_op jit(solution)/shard_map/ppermute | solution.py:300
  117.2 0.1 stack.27.spots
  117.2 0.0 collective-permute-done.7.refs_4_
  117.2 0.0 collective-permute-done.10.refs_7_
  117.3 0.0 collective-permute-done.9.refs_6_
  117.3 1.9 %collective-permute-done.8.refs_5_ = f32[2,2,2,4,32,128]{5,4,3,2,1,0:T(8,128)} collective-permute-done((f32[2,2,2,4,32,128]{5,4,3,2,1,0:T(8,128)S(1)}, f32[2,2,2,4,32,128]{5,4,3,2,1,0:T(8,128)}, u32[]{:S(2)}, u32[]{:S(2)}) %collective-permute-start.8) | collective-permute-done | bytes 524320 | tf_op jit(solution)/shard_map/ppermute | solution.py:300
  119.1 3.6 %place.1 = f32[4,8,4,2,32,128]{5,4,3,2,1,0:T(8,128)} custom-call(s32[6]{0:T(128)S(1)} %stack.27.spots, f32[2,2,2,4,32,128]{5,4,3,2,1,0:T(8,128)S(1)} %bitcast.14, f32[2,2,2,4,32,128]{5,4,3,2,1,0:T(8,128)S(1)} %collective-permute-done.4.refs_1_, f32[2,2,2,4,32,128]{5,4,3,2,1,0:T(8,128)S(1)} %collective-permute-done.5.refs_2_, ...), custom_call_target="tpu_custom_call" | custom-call | tf_op jit(solution)/shard_map/place/pallas_call | solution.py:263
Async XLA Ops:
  1.1 24.9 %collective-permute-start.1 = (f32[2,1,32,1024]{3,2,1,0:T(8,128)S(1)}, f32[2,1,32,1024]{3,2,1,0:T(8,128)S(1)}, u32[]{:S(2)}, u32[]{:S(2)}) collective-permute-start(f32[2,1,32,1024]{3,2,1,0:T(8,128)S(1)} %get-tuple-element.13), channel_id=1, source_target_pairs={{1,0},{2,1},{3,2},{4,3},{5,4},{6,5},{7,6},{9,8},{10,9},{11,10},{12... | collective-permute-start | bytes 786440 | tf_op jit(solution)/shard_map/ppermute | solution.py:278
  2.4 23.6 %collective-permute-start = (f32[2,1,32,1024]{3,2,1,0:T(8,128)S(1)}, f32[2,1,32,1024]{3,2,1,0:T(8,128)S(1)}, u32[]{:S(2)}, u32[]{:S(2)}) collective-permute-start(f32[2,1,32,1024]{3,2,1,0:T(8,128)S(1)} %get-tuple-element.14), channel_id=1, source_target_pairs={{0,1},{1,2},{2,3},{3,4},{4,5},{5,6},{6,7},{8,9},{9,10},{10,11},{11... | collective-permute-start | bytes 786440 | tf_op jit(solution)/shard_map/ppermute | solution.py:278
  8.4 17.6 %collective-permute-start.3 = (f32[2,8,1,1024]{3,2,1,0:T(1,128)S(1)}, f32[2,8,1,1024]{3,2,1,0:T(1,128)S(1)}, u32[]{:S(2)}, u32[]{:S(2)}) collective-permute-start(f32[2,8,1,1024]{3,2,1,0:T(1,128)S(1)} %get-tuple-element.11), channel_id=1, source_target_pairs={{8,0},{16,8},{24,16},{32,24},{40,32},{48,40},{56,48},{64,56},{72,6... | collective-permute-start | bytes 196616 | tf_op jit(solution)/shard_map/ppermute | solution.py:278
  17.0 8.9 %collective-permute-start.2 = (f32[2,8,1,1024]{3,2,1,0:T(1,128)S(1)}, f32[2,8,1,1024]{3,2,1,0:T(1,128)S(1)}, u32[]{:S(2)}, u32[]{:S(2)}) collective-permute-start(f32[2,8,1,1024]{3,2,1,0:T(1,128)S(1)} %get-tuple-element.12), channel_id=1, source_target_pairs={{0,8},{8,16},{16,24},{24,32},{32,40},{40,48},{48,56},{56,64},{64,7... | collective-permute-start | bytes 196616 | tf_op jit(solution)/shard_map/ppermute | solution.py:278
  20.4 0.7 copy-start.1
  21.1 4.9 %copy-start = (s32[32,128]{1,0:T(8,128)}, s32[32,128]{1,0:T(8,128)S(1)}, u32[]{:S(2)}) copy-start(s32[32,128]{1,0:T(8,128)S(1)} %broadcast_in_dim.2.back) | copy-start | bytes 49156
  82.2 18.0 %collective-permute-start.6 = (f32[2,2,2,4,32,128]{5,4,3,2,1,0:T(8,128)S(1)}, f32[2,2,2,4,32,128]{5,4,3,2,1,0:T(8,128)S(1)}, u32[]{:S(2)}, u32[]{:S(2)}) collective-permute-start(f32[2,2,2,4,32,128]{5,4,3,2,1,0:T(8,128)S(1)} %bitcast.10), channel_id=1, source_target_pairs={{0,32},{16,48},{32,0},{48,16},{1,33},{17,49},{33,1},{49,17},{2,34}... | collective-permute-start | bytes 1572872 | tf_op jit(solution)/shard_map/ppermute | solution.py:278
  89.2 23.6 %collective-permute-start.5 = (f32[2,2,2,4,32,128]{5,4,3,2,1,0:T(8,128)S(1)}, f32[2,2,2,4,32,128]{5,4,3,2,1,0:T(8,128)S(1)}, u32[]{:S(2)}, u32[]{:S(2)}) collective-permute-start(f32[2,2,2,4,32,128]{5,4,3,2,1,0:T(8,128)S(1)} %bitcast.11), channel_id=1, source_target_pairs={{0,16},{16,32},{32,48},{48,0},{1,17},{17,33},{33,49},{49,1},{2,18}... | collective-permute-start | bytes 1572872 | tf_op jit(solution)/shard_map/ppermute | solution.py:278
  91.2 24.0 %collective-permute-start.4 = (f32[2,2,2,4,32,128]{5,4,3,2,1,0:T(8,128)S(1)}, f32[2,2,2,4,32,128]{5,4,3,2,1,0:T(8,128)S(1)}, u32[]{:S(2)}, u32[]{:S(2)}) collective-permute-start(f32[2,2,2,4,32,128]{5,4,3,2,1,0:T(8,128)S(1)} %bitcast.12), channel_id=1, source_target_pairs={{0,48},{16,0},{32,16},{48,32},{1,49},{17,1},{33,17},{49,33},{2,50}... | collective-permute-start | bytes 1572872 | tf_op jit(solution)/shard_map/ppermute | solution.py:278
  95.7 21.6 %collective-permute-start.7 = (f32[2,2,2,4,32,128]{5,4,3,2,1,0:T(8,128)S(1)}, f32[2,2,2,4,32,128]{5,4,3,2,1,0:T(8,128)S(1)}, u32[]{:S(2)}, u32[]{:S(2)}) collective-permute-start(f32[2,2,2,4,32,128]{5,4,3,2,1,0:T(8,128)S(1)} %bitcast.13), channel_id=1, source_target_pairs={{0,8},{8,0},{1,9},{9,1},{2,10},{10,2},{3,11},{11,3},{4,12},{12,4},... | collective-permute-start | bytes 1572872 | tf_op jit(solution)/shard_map/ppermute | solution.py:300
  100.1 17.1 %collective-permute-start.10 = (f32[2,2,2,4,32,128]{5,4,3,2,1,0:T(8,128)S(1)}, f32[2,2,2,4,32,128]{5,4,3,2,1,0:T(8,128)S(1)}, u32[]{:S(2)}, u32[]{:S(2)}) collective-permute-start(f32[2,2,2,4,32,128]{5,4,3,2,1,0:T(8,128)S(1)} %collective-permute-done.6.refs_3_), channel_id=1, source_target_pairs={{0,8},{8,0},{1,9},{9,1},{2,10},{10,2},{3,11},{11,3},{4,12},{12,4},... | collective-permute-start | bytes 1572872 | tf_op jit(solution)/shard_map/ppermute | solution.py:300
  112.8 4.5 %collective-permute-start.9 = (f32[2,2,2,4,32,128]{5,4,3,2,1,0:T(8,128)S(1)}, f32[2,2,2,4,32,128]{5,4,3,2,1,0:T(8,128)}, u32[]{:S(2)}, u32[]{:S(2)}) collective-permute-start(f32[2,2,2,4,32,128]{5,4,3,2,1,0:T(8,128)S(1)} %collective-permute-done.5.refs_2_), channel_id=1, source_target_pairs={{0,8},{8,0},{1,9},{9,1},{2,10},{10,2},{3,11},{11,3},{4,12},{12,4},... | collective-permute-start | bytes 1572872 | tf_op jit(solution)/shard_map/ppermute | solution.py:300
  115.2 3.9 %collective-permute-start.8 = (f32[2,2,2,4,32,128]{5,4,3,2,1,0:T(8,128)S(1)}, f32[2,2,2,4,32,128]{5,4,3,2,1,0:T(8,128)}, u32[]{:S(2)}, u32[]{:S(2)}) collective-permute-start(f32[2,2,2,4,32,128]{5,4,3,2,1,0:T(8,128)S(1)} %collective-permute-done.4.refs_1_), channel_id=1, source_target_pairs={{0,8},{8,0},{1,9},{9,1},{2,10},{10,2},{3,11},{11,3},{4,12},{12,4},... | collective-permute-start | bytes 1572872 | tf_op jit(solution)/shard_map/ppermute | solution.py:300

commit v3 on v2

v3 whole, which is shorter than its diff:
```python
import jax
import jax.numpy as jnp
from jax import lax
from jax.experimental import pallas as pl
from jax.experimental.pallas import tpu as pltpu
from jax.sharding import Mesh, PartitionSpec as P

LANES = 128
SUBS = 8
COLOUR_UNIT = 2.0**-12
OPACITY_UNIT = 2.0**-18
FIELD = 1 << 13

LOOKUP = lax.GatherDimensionNumbers(
    offset_dims=(),
    collapsed_slice_dims=(1,),
    start_index_map=(1,),
    operand_batching_dims=(0,),
    start_indices_batching_dims=(0,),
)


def pick(table, lanes):
    return lax.gather(table, lanes[..., None], LOOKUP, (1, 1), mode=lax.GatherScatterMode.PROMISE_IN_BOUNDS)


def store_tables(colour_ref, opacity_ref, tab):
    for f in range(2):
        colour = [(colour_ref[k, f : f + 1, :].astype(jnp.float32) / COLOUR_UNIT).astype(jnp.int32) for k in range(3)]
        opacity = (opacity_ref[f : f + 1, :].astype(jnp.float32) / OPACITY_UNIT).astype(jnp.int32)
        for w, word in enumerate((colour[0] + colour[1] * FIELD, colour[2] + opacity * FIELD)):
            for h in range(2):
                tab[f, w, h] = jnp.broadcast_to(word[:, h * LANES : (h + 1) * LANES], (SUBS, LANES))


def masks():
    sub = lax.broadcasted_iota(jnp.int32, (SUBS, LANES), 0)
    lane = lax.broadcasted_iota(jnp.int32, (SUBS, LANES), 1)
    return sub == 0, sub == SUBS - 1, lane == 0, lane == LANES - 1


def cell(at, bins_of, d, tab, edges):
    first_sub, last_sub, first_lane, last_lane = edges
    colour = clear = None
    for f in range(2):
        here = at(f, d, 0, 0)
        dz = at(f, d + 1, 0, 0) - at(f, d - 1, 0, 0)
        after = pltpu.roll(jnp.where(first_sub, at(f, d, SUBS, 0), here), SUBS - 1, 0)
        before = pltpu.roll(jnp.where(last_sub, at(f, d, -SUBS, 0), here), 1, 0)
        dx = after - before
        after = pltpu.roll(jnp.where(first_lane, at(f, d, 0, LANES), here), LANES - 1, 1)
        before = pltpu.roll(jnp.where(last_lane, at(f, d, 0, -LANES), here), 1, 1)
        dy = after - before
        total = dz * dz + dx * dx + dy * dy
        shade = 0.3 + (0.35 * jnp.abs(dz)) * lax.rsqrt(0.25 * total + 1.0)
        root = total * lax.rsqrt(jnp.maximum(total, 1e-30))
        gain = 0.25 * OPACITY_UNIT + (0.5 * OPACITY_UNIT) * root
        entry = bins_of(f)
        low = entry & (LANES - 1)
        upper = entry >= LANES
        words = [jnp.where(upper, pick(tab[f, w, 1], low), pick(tab[f, w, 0], low)) for w in range(2)]
        alpha = (words[1] >> 13).astype(jnp.float32) * gain
        lit = alpha * shade
        looked = (words[0] & (FIELD - 1), words[0] >> 13, words[1] & (FIELD - 1))
        terms = [lit * value.astype(jnp.float32) for value in looked]
        colour = terms if colour is None else [a + b for a, b in zip(colour, terms)]
        clear = 1.0 - alpha if clear is None else clear * (1.0 - alpha)
    return colour, clear


def composite(elements, backward):
    colour = through = None
    for part, clear in elements:
        if colour is None:
            colour, through = part, clear
        else:
            keep = jnp.where(backward, clear, 1.0)
            weight = jnp.where(backward, 1.0, through)
            colour = [a * keep + weight * b for a, b in zip(colour, part)]
            through = through * clear
    return colour, through


def lattice(cells, xlo, xhi, zlo, zhi, g, start):
    _, depth, cols, _ = cells.shape
    span, here = pl.ds(g * SUBS, SUBS), pl.ds(start, LANES)

    def at(f, d, dc, dr):
        if d < 0:
            return zlo[f, 0, span, here]
        if d == depth:
            return zhi[f, 0, span, here]
        if g * SUBS + dc < 0:
            return jnp.broadcast_to(xlo[f, d, :, here], (SUBS, LANES))
        if g * SUBS + dc == cols:
            return jnp.broadcast_to(xhi[f, d, :, here], (SUBS, LANES))
        return cells[f, d, pl.ds(g * SUBS + dc, SUBS), pl.ds(start + (LANES + dr), LANES)]

    return at


def inner_kernel(
    fields, bins, xlo, xhi, colour, opacity, view, cells, picks, mid, tab, back, colour_now, opacity_now, field_sem, bin_sem, tab_sem
):
    depth, cols, rows = fields.shape[1:]
    groups = cols // SUBS
    spans = [pl.ds(g * SUBS, SUBS) for g in range(groups)]
    tab_copies = [
        pltpu.make_async_copy(colour, colour_now, tab_sem.at[0]),
        pltpu.make_async_copy(opacity, opacity_now, tab_sem.at[1]),
    ]
    field_copies, bin_copies = [], []
    for g, span in enumerate(spans):
        target = cells.at[:, :, span, pl.ds(LANES, rows)]
        field_copies.append(pltpu.make_async_copy(fields.at[:, :, span, :], target, field_sem.at[g]))
        bin_copies.append(pltpu.make_async_copy(bins.at[:, :, span, :], picks.at[:, :, span, :], bin_sem.at[g]))
    for copy in tab_copies + [field_copies[0], bin_copies[0], field_copies[1]]:
        copy.start()
    for g in range(1, groups):
        bin_copies[g].start()
        if g + 1 < groups:
            field_copies[g + 1].start()
    zero = jnp.zeros((cols, LANES), jnp.float32)
    for f in range(2):
        for d in range(depth):
            cells[f, d, :, 0:LANES] = zero
            cells[f, d, :, LANES + rows :] = zero
    sub = lax.broadcasted_iota(jnp.int32, (SUBS, LANES), 0)
    for g in range(groups):
        towards = jnp.zeros((SUBS, LANES), jnp.int32)
        for k in range(SUBS):
            towards = jnp.where(sub == k, view[g * SUBS + k], towards)
        back[g * SUBS : (g + 1) * SUBS, :] = towards
    for copy in tab_copies:
        copy.wait()
    store_tables(colour_now, opacity_now, tab)
    edges = masks()
    field_copies[0].wait()
    for g in range(groups):
        if g + 1 < groups:
            field_copies[g + 1].wait()
        bin_copies[g].wait()
        backward = back[g * SUBS : (g + 1) * SUBS, :] == 1

        def tile(b, carry, g=g, backward=backward):
            start = pl.multiple_of(b * LANES, LANES)
            at = lattice(cells, xlo, xhi, None, None, g, start)

            def element(d):
                return cell(at, lambda f: picks[f, d, pl.ds(g * SUBS, SUBS), pl.ds(start, LANES)], d, tab, edges)

            parts, through = composite((element(d) for d in range(1, depth - 1)), backward)
            for k, part in enumerate(parts + [through]):
                mid[b, k, pl.ds(g * SUBS, SUBS), :] = part
            return carry

        lax.fori_loop(0, rows // LANES, tile, 0, unroll=4)


def outer_kernel(cells, zlo, zhi, xlo, xhi, picks, mid, tab, back, out):
    depth, cols, rows = picks.shape[1:]
    edges = masks()
    for g in range(cols // SUBS):
        backward = back[g * SUBS : (g + 1) * SUBS, :] == 1

        def tile(b, carry, g=g, backward=backward):
            start = pl.multiple_of(b * LANES, LANES)
            at = lattice(cells, xlo, xhi, zlo, zhi, g, start)

            def element(d):
                return cell(at, lambda f: picks[f, d, pl.ds(g * SUBS, SUBS), pl.ds(start, LANES)], d, tab, edges)

            middle = [mid[b, k, pl.ds(g * SUBS, SUBS), :] for k in range(4)]
            elements = [element(0), (middle[:3], middle[3]), element(depth - 1)]
            parts, through = composite(elements, backward)
            for k, part in enumerate(parts):
                out[b, k, pl.ds(g * SUBS, SUBS), :] = part * COLOUR_UNIT
            out[b, 3, pl.ds(g * SUBS, SUBS), :] = 1.0 - through
            return carry

        lax.fori_loop(0, rows // LANES, tile, 0, unroll=8)


VMEM = pl.BlockSpec(memory_space=pltpu.VMEM)
SMEM = pl.BlockSpec(memory_space=pltpu.SMEM)
ANY = pl.BlockSpec(memory_space=pl.ANY)
LIMIT = 24 * 2**20


def march_inner(fields, bins, xlo, xhi, colour, opacity, view):
    _, depth, cols, rows = fields.shape
    resident = [pltpu.with_memory_space_constraint(x, pltpu.HBM) for x in (fields, bins)]
    tables = [pltpu.with_memory_space_constraint(x, pltpu.HBM) for x in (colour, opacity)]
    return pl.pallas_call(
        inner_kernel,
        out_shape=[
            pltpu.VMEM((2, depth, cols, rows + 2 * LANES), jnp.float32),
            pltpu.VMEM((2, depth, cols, rows), jnp.int32),
            pltpu.VMEM((rows // LANES, 4, cols, LANES), jnp.float32),
            pltpu.VMEM((2, 2, 2, SUBS, LANES), jnp.int32),
            pltpu.VMEM((cols, LANES), jnp.int32),
        ],
        in_specs=[ANY, ANY, VMEM, VMEM, ANY, ANY, SMEM],
        out_specs=[VMEM] * 5,
        scratch_shapes=[
            pltpu.VMEM(colour.shape, colour.dtype),
            pltpu.VMEM(opacity.shape, opacity.dtype),
            pltpu.SemaphoreType.DMA((cols // SUBS,)),
            pltpu.SemaphoreType.DMA((cols // SUBS,)),
            pltpu.SemaphoreType.DMA((2,)),
        ],
        compiler_params=pltpu.CompilerParams(vmem_limit_bytes=LIMIT),
        cost_estimate=pl.CostEstimate(flops=100 * 2 * depth * cols * rows, bytes_accessed=8 * 2**20, transcendentals=0),
        name="march_inner",
    )(*resident, xlo, xhi, *tables, view)


def march_outer(cells, zlo, zhi, xlo, xhi, picks, mid, tab, back):
    _, depth, cols, rows = picks.shape
    return pl.pallas_call(
        outer_kernel,
        out_shape=pltpu.VMEM((rows // LANES, 4, cols, LANES), jnp.float32),
        in_specs=[VMEM] * 9,
        out_specs=VMEM,
        compiler_params=pltpu.CompilerParams(vmem_limit_bytes=LIMIT),
        name="march_outer",
    )(cells, zlo, zhi, xlo, xhi, picks, mid, tab, back)


def join_kernel(parts, back, out):
    depth, _, cols, _ = parts.shape
    for group in range(cols // SUBS):
        span = pl.ds(group * SUBS, SUBS)
        elements = (([parts[d, k, span, :] for k in range(3)], 1.0 - parts[d, 3, span, :]) for d in range(depth))
        colour, through = composite(elements, back[span, :] == 1)
        for k in range(3):
            out[k, span, :] = colour[k]
        out[3, span, :] = 1.0 - through


def join(parts, back):
    return pl.pallas_call(
        join_kernel,
        out_shape=jax.ShapeDtypeStruct(parts.shape[1:], jnp.float32),
        in_specs=[VMEM, VMEM],
        out_specs=VMEM,
        name="join",
    )(parts, back)


def place_kernel(core, pieces, *refs):
    out = refs[-1]
    channel = pl.program_id(0)
    for x in range(pieces.shape[0]):
        for high in range(2):
            for mid in range(2):
                for low in range(2):
                    out[0, 4 * high + 2 * mid + low, x, 0] = pieces[x, low, mid, high, channel]


def place(pieces, core, frame=None):
    x_count = pieces.shape[0]
    channels, cols, rows = pieces.shape[4:]
    whole = (channels, 8, x_count, 2, cols, rows)
    block = (1, 8, x_count, 1, cols, rows)
    kept = [] if frame is None else [frame]
    return pl.pallas_call(
        place_kernel,
        grid_spec=pltpu.PrefetchScalarGridSpec(
            num_scalar_prefetch=1,
            grid=(channels,),
            in_specs=[VMEM] + [ANY] * len(kept),
            out_specs=pl.BlockSpec(block, lambda channel, core: (channel, 0, 0, core[0], 0, 0)),
        ),
        out_shape=jax.ShapeDtypeStruct(whole, jnp.float32),
        input_output_aliases={2: 0} if kept else {},
        compiler_params=pltpu.CompilerParams(vmem_limit_bytes=LIMIT),
        cost_estimate=pl.CostEstimate(flops=0, bytes_accessed=4 * 2**20, transcendentals=0),
        name="place",
    )(core.reshape(1), pieces, *kept)


def shifted(value, axis, step, wrap=True):
    count = lax.axis_size(axis)
    route = [(i, (i + step) % count) for i in range(count) if wrap or 0 <= i + step < count]
    return lax.ppermute(value, axis, route)


WIDE = ("z_high", "z_mid", "z_low", "x", "core")


def on_device(fields, field_bins, colour_table, opacity_table, view_dir):
    depth, cols = fields.shape[1:3]
    xlo = shifted(fields[:, :, cols - 1 :], WIDE, 1, wrap=False)
    xhi = shifted(fields[:, :, :1], WIDE, -1, wrap=False)
    zlo = shifted(fields[:, depth - 1 :], "y", 1, wrap=False)
    zhi = shifted(fields[:, :1], "y", -1, wrap=False)
    colour = jnp.transpose(colour_table, (1, 0, 2))
    cells, picks, mid, tab, back = march_inner(fields, field_bins, xlo, xhi, colour, opacity_table, view_dir)
    partial = march_outer(cells, zlo, zhi, xlo, xhi, picks, mid, tab, back)
    partial = lax.all_to_all(partial, "y", 0, 0)
    column = join(partial, back)
    for axis in ("z_high", "z_mid", "z_low"):
        column = lax.all_gather(column, axis)
    x_count = lax.axis_size("x")
    own = lax.all_to_all(jnp.broadcast_to(column[None], (x_count,) + column.shape), "x", 0, 0)
    other = lax.ppermute(own, "core", [(0, 1), (1, 0)])
    core = lax.axis_index("core").astype(jnp.int32)
    frame = place(other, 1 - core, place(own, core))
    channels, _, _, _, _, rows = frame.shape
    return frame.reshape(channels, -1, rows)


def solution(mesh):
    grid = Mesh(mesh.devices.reshape(2, 2, 2, 4, 2, 8), WIDE + ("y",))
    split = P(None, "y", WIDE, None)
    return jax.shard_map(
        on_device,
        mesh=grid,
        in_specs=(split, split, P(), P(), P(WIDE)),
        out_specs=P(None, None, "y"),
        check_vma=False,
    )
```

time: 123 us -> 125 us (1.016)
  blocking collectives: 48.3 us -> 80.8 us
  starting transfers between devices: 43.8 us -> 21 us
  waiting for transfers between devices: 9.5 us -> 3.34 us
  local copies, waits for them, and re-layouts: 4.55 us -> 3.28 us
    all_to_all x0 -> x1, blocking collectives: none -> 38.6 us  [on_device(): lax.all_to_all(jnp.broadcast_to(column[None], (x_count,) + column.shape),...]
    ppermute x7 -> x4, starting transfers between devices: 30.1 us -> 16.6 us  [shifted(): return lax.ppermute(value, axis, route)]
    ppermute x4 -> x1, starting transfers between devices: 13.8 us -> 4.41 us  [on_device(): other = lax.ppermute(own, 'core', [(0, 1), (1, 0)])]
    all_gather x3, blocking collectives: 27.5 us -> 21.1 us  [on_device(): column = lax.all_gather(column, axis)]
    ppermute x7 -> x4, waiting for transfers between devices: 7.63 us -> 1.31 us  [shifted(): return lax.ppermute(value, axis, route)]
    pallas_call x2 -> x3, Pallas kernels: 9.71 us -> 6.72 us  [the longest x2 5.27 us: place(): pl.pallas_call(place_kernel, grid_spec=pltpu.PrefetchScalarGridSpec(num_s...]
    pallas_call x1, Pallas kernels: 4.89 us -> 7.33 us  [march_inner(): pl.pallas_call(inner_kernel, out_shape=[pltpu.VMEM((2, depth, cols, rows...]
  transfers between devices with their start and end apart: 11 -> 5, of which waited for: 3 -> 2; matrix products, arithmetic and copies ran while one was open for 2% -> 1% of each run, Pallas kernels for 4% -> 7%
where the time goes in v3:
time: 125 us; the launch traced here: 124 us
  blocking collectives  80.8 us (65%)
  starting transfers between devices  21 us (17%)
  Pallas kernels  15.8 us (13%)
  waiting for transfers between devices  3.34 us (3%)
  local copies, waits for them, and re-layouts  3.28 us (3%)
    all_to_all x1, blocking collectives, on_device(): lax.all_to_all(jnp.broadcast_to(column[None], (x_count,) + column.shape),...  38.6 us
    all_gather x3, blocking collectives, on_device(): column = lax.all_gather(column, axis)  21.1 us
    all_to_all x1, blocking collectives, on_device(): partial = lax.all_to_all(partial, 'y', 0, 0)  21.1 us
    ppermute x4, starting transfers between devices, shifted(): return lax.ppermute(value, axis, route)  16.6 us
    pallas_call x1, Pallas kernels, march_inner(): pl.pallas_call(inner_kernel, out_shape=[pltpu.VMEM((2, depth, cols, rows...  7.33 us
    pallas_call x2, Pallas kernels, place(): pl.pallas_call(place_kernel, grid_spec=pltpu.PrefetchScalarGridSpec(num_s...  5.27 us
    ppermute x1, starting transfers between devices, on_device(): other = lax.ppermute(own, 'core', [(0, 1), (1, 0)])  4.41 us
  transfers between devices with their start and end apart: 5, of which 2 were waited for; matrix products, arithmetic and copies ran while one was open for 1% of the time, Pallas kernels for 7%

profile of v3, /device:TPU:1, one launch (start us, length us, event | category | flops | bytes accessed | tf_op | source)
XLA Modules:
  0.0 124.3 jit_solution(1366983736644776235)
XLA Ops:
  0.0 1.1 fusion
  1.1 1.3 %collective-permute-start.3 = (f32[2,1,32,1024]{3,2,1,0:T(8,128)S(1)}, f32[2,1,32,1024]{3,2,1,0:T(8,128)S(1)}, u32[]{:S(2)}, u32[]{:S(2)}) collective-permute-start(f32[2,1,32,1024]{3,2,1,0:T(8,128)S(1)} %get-tuple-element.15), channel_id=1, source_target_pairs={{1,0},{2,1},{3,2},{4,3},{5,4},{6,5},{7,6},{9,8},{10,9},{11,10},{12... | collective-permute-start | bytes 786440 | tf_op jit(solution)/shard_map/ppermute | solution.py:286
  2.4 4.7 %collective-permute-start.2 = (f32[2,1,32,1024]{3,2,1,0:T(8,128)S(1)}, f32[2,1,32,1024]{3,2,1,0:T(8,128)S(1)}, u32[]{:S(2)}, u32[]{:S(2)}) collective-permute-start(f32[2,1,32,1024]{3,2,1,0:T(8,128)S(1)} %get-tuple-element.16), channel_id=1, source_target_pairs={{0,1},{1,2},{2,3},{3,4},{4,5},{5,6},{6,7},{8,9},{9,10},{10,11},{11... | collective-permute-start | bytes 786440 | tf_op jit(solution)/shard_map/ppermute | solution.py:286
  7.1 1.3 %fusion.1 = (f32[2,8,1,1024]{3,2,1,0:T(1,128)S(1)}, f32[2,8,1,1024]{3,2,1,0:T(1,128)S(1)}) fusion(f32[2,8,32,1024]{3,2,1,0:T(8,128)} %fields.1), kind=kLoop, calls=%fused_computation.1 | loop fusion | bytes 262144 | tf_op jit(solution)/shard_map/slice | solution.py:295
  8.4 8.7 %collective-permute-start.1 = (f32[2,8,1,1024]{3,2,1,0:T(1,128)S(1)}, f32[2,8,1,1024]{3,2,1,0:T(1,128)S(1)}, u32[]{:S(2)}, u32[]{:S(2)}) collective-permute-start(f32[2,8,1,1024]{3,2,1,0:T(1,128)S(1)} %get-tuple-element.17), channel_id=1, source_target_pairs={{8,0},{16,8},{24,16},{32,24},{40,32},{48,40},{56,48},{64,56},{72,6... | collective-permute-start | bytes 196616 | tf_op jit(solution)/shard_map/ppermute | solution.py:286
  17.0 1.9 %collective-permute-start = (f32[2,8,1,1024]{3,2,1,0:T(1,128)S(1)}, f32[2,8,1,1024]{3,2,1,0:T(1,128)S(1)}, u32[]{:S(2)}, u32[]{:S(2)}) collective-permute-start(f32[2,8,1,1024]{3,2,1,0:T(1,128)S(1)} %get-tuple-element.18), channel_id=1, source_target_pairs={{0,8},{8,16},{16,24},{24,32},{32,40},{40,48},{48,56},{56,64},{64,7... | collective-permute-start | bytes 196616 | tf_op jit(solution)/shard_map/ppermute | solution.py:286
  19.0 0.0 collective-permute-done.1.xhi
  19.0 1.3 %collective-permute-done.xlo = f32[2,8,1,1024]{3,2,1,0:T(1,128)S(1)} collective-permute-done((f32[2,8,1,1024]{3,2,1,0:T(1,128)S(1)}, f32[2,8,1,1024]{3,2,1,0:T(1,128)S(1)}, u32[]{:S(2)}, u32[]{:S(2)}) %collective-permute-start) | collective-permute-done | bytes 65568 | tf_op jit(solution)/shard_map/ppermute | solution.py:286
  20.3 0.0 copy-start.1
  20.3 0.7 copy-done.1
  20.9 7.3 %march_inner.1 = (f32[2,8,32,1280]{3,2,1,0:T(8,128)S(1)}, s32[2,8,32,1024]{3,2,1,0:T(8,128)S(1)}, f32[8,4,32,128]{3,2,1,0:T(8,128)S(1)}, s32[2,2,2,8,128]{4,3,2,1,0:T(8,128)S(1)}, s32[32,128]{1,0:T(8,128)S(1)}) custom-call(f32[2,8,32,1024]{3,2,1,0:T(8,128)} %fields.1, s32[2,8,32,1024]{3,2,1,0:T(8,128)} %bins.1, ...), custom_call_target="tpu_custom_call" | custom-call | flops 52428800 | bytes 8388608 | tf_op jit(solution)/shard_map/march_inner/pallas_call | solution.py:194
  28.3 0.0 copy-start
  28.3 0.0 collective-permute-done.3.zhi
  28.3 0.0 collective-permute-done.2.zlo
  28.3 1.4 %march_outer.1 = f32[8,4,32,128]{3,2,1,0:T(8,128)S(1)} custom-call(f32[2,8,32,1280]{3,2,1,0:T(8,128)S(1)} %get-tuple-element.10.cells, f32[2,1,32,1024]{3,2,1,0:T(8,128)S(1)} %collective-permute-done.2.zlo, f32[2,1,32,1024]{3,2,1,0:T(8,128)S(1)} %collective-permute-done.3.zhi, f32[2,8,1,1024]{3,2,1,0:T(1,128)S(1)} %collective-permute-done.xlo, ...), custom_call_target="tpu_custom_call" | custom-call | tf_op jit(solution)/shard_map/march_outer/pallas_call | solution.py:220
  29.8 0.0 copy-done
  29.8 21.1 %all_to_all.10.parts = f32[8,4,32,128]{3,2,1,0:T(8,128)} all-to-all(f32[8,4,32,128]{3,2,1,0:T(8,128)S(1)} %march_outer.1), channel_id=1, replica_groups=mesh['z_high'=2,'z_mid'=2,'z_low'=2,'x'=4,'core'=2,'y'=8] {'y'}, dimensions={0} | all-to-all | bytes 1048576 | tf_op jit(solution)/shard_map/all_to_all | solution.py:301
  50.8 1.7 %join.1 = f32[4,32,128]{2,1,0:T(8,128)} custom-call(f32[8,4,32,128]{3,2,1,0:T(8,128)} %all_to_all.10.parts, s32[32,128]{1,0:T(8,128)} %copy-done), custom_call_target="tpu_custom_call" | custom-call | tf_op jit(solution)/shard_map/join/pallas_call | solution.py:242
  52.6 7.9 %all-gather = f32[8,32,128]{2,1,0:T(8,128)S(1)} all-gather(f32[4,32,128]{2,1,0:T(8,128)} %join.1), channel_id=2, replica_groups=mesh['z_high'=2,'z_mid'=2,'z_low'=2,'x'=4,'core'=2,'y'=8] {'z_high'}, dimensions={0}, use_global_device_ids=true | all-gather | bytes 196608 | tf_op jit(solution)/shard_map/all_gather | solution.py:304
  60.5 5.9 %all-gather.1 = f32[4,4,32,128]{3,2,1,0:T(8,128)S(1)} all-gather(f32[2,4,32,128]{3,2,1,0:T(8,128)S(1)} %bitcast.9), channel_id=3, replica_groups=mesh['z_high'=2,'z_mid'=2,'z_low'=2,'x'=4,'core'=2,'y'=8] {'z_mid'}, dimensions={0}, use_global_device_ids=true | all-gather | bytes 393216 | tf_op jit(solution)/shard_map/all_gather | solution.py:304
  66.4 7.3 %all-gather.2 = f32[4,2,4,32,128]{4,3,2,1,0:T(8,128)S(1)} all-gather(f32[2,2,4,32,128]{4,3,2,1,0:T(8,128)S(1)} %bitcast.8), channel_id=4, replica_groups=mesh['z_high'=2,'z_mid'=2,'z_low'=2,'x'=4,'core'=2,'y'=8] {'z_low'}, dimensions={0}, use_global_device_ids=true | all-gather | bytes 786432 | tf_op jit(solution)/shard_map/all_gather | solution.py:304
  73.7 0.3 broadcast_in_dim.2
  73.9 38.6 %all_to_all.11.pieces = f32[4,2,2,2,4,32,128]{6,5,4,3,2,1,0:T(8,128)S(1)} all-to-all(f32[4,2,2,2,4,32,128]{6,5,4,3,2,1,0:T(8,128)S(1)} %broadcast_in_dim.2), channel_id=1, replica_groups=mesh['z_high'=2,'z_mid'=2,'z_low'=2,'x'=4,'core'=2,'y'=8] {'x'}, dimensions={0} | all-to-all | bytes 4194304 | tf_op jit(solution)/shard_map/all_to_all | solution.py:306
  112.6 4.4 %collective-permute-start.4 = (f32[4,2,2,2,4,32,128]{6,5,4,3,2,1,0:T(8,128)S(1)}, f32[4,2,2,2,4,32,128]{6,5,4,3,2,1,0:T(8,128)}, u32[]{:S(2)}, u32[]{:S(2)}) collective-permute-start(f32[4,2,2,2,4,32,128]{6,5,4,3,2,1,0:T(8,128)S(1)} %all_to_all.11.pieces), channel_id=1, source_target_pairs={{0,8},{8,0},{1,9},{9,1},{2,10},{10,2},{3,11},{11,3},{4,12},{12,4},... | collective-permute-start | bytes 6291464 | tf_op jit(solution)/shard_map/ppermute | solution.py:307
  117.0 1.9 %place.2.refs_0_ = f32[4,8,4,2,32,128]{5,4,3,2,1,0:T(8,128)} custom-call(s32[1]{0:T(128)} %bitcast.5.core, f32[4,2,2,2,4,32,128]{6,5,4,3,2,1,0:T(8,128)S(1)} %all_to_all.11.pieces), custom_call_target="tpu_custom_call" | custom-call | bytes 4194304 | tf_op jit(solution)/shard_map/place/pallas_call | solution.py:267
  118.9 2.0 %collective-permute-done.4.pieces = f32[4,2,2,2,4,32,128]{6,5,4,3,2,1,0:T(8,128)} collective-permute-done((f32[4,2,2,2,4,32,128]{6,5,4,3,2,1,0:T(8,128)S(1)}, f32[4,2,2,2,4,32,128]{6,5,4,3,2,1,0:T(8,128)}, u32[]{:S(2)}, u32[]{:S(2)}) %collective-permute-start.4) | collective-permute-done | bytes 2097184 | tf_op jit(solution)/shard_map/ppermute | solution.py:307
  120.9 3.4 %place.3 = f32[4,8,4,2,32,128]{5,4,3,2,1,0:T(8,128)} custom-call(s32[1]{0:T(128)} %bitcast.core, f32[4,2,2,2,4,32,128]{6,5,4,3,2,1,0:T(8,128)} %collective-permute-done.4.pieces, f32[4,8,4,2,32,128]{5,4,3,2,1,0:T(8,128)} %place.2.refs_0_), custom_call_target="tpu_custom_call", output_to_operand_aliasing={{}: (2, {})} | custom-call | bytes 4194304 | tf_op jit(solution)/shard_map/place/pallas_call | solution.py:267
Async XLA Ops:
  1.1 27.2 %collective-permute-start.3 = (f32[2,1,32,1024]{3,2,1,0:T(8,128)S(1)}, f32[2,1,32,1024]{3,2,1,0:T(8,128)S(1)}, u32[]{:S(2)}, u32[]{:S(2)}) collective-permute-start(f32[2,1,32,1024]{3,2,1,0:T(8,128)S(1)} %get-tuple-element.15), channel_id=1, source_target_pairs={{1,0},{2,1},{3,2},{4,3},{5,4},{6,5},{7,6},{9,8},{10,9},{11,10},{12... | collective-permute-start | bytes 786440 | tf_op jit(solution)/shard_map/ppermute | solution.py:286
  2.4 25.9 %collective-permute-start.2 = (f32[2,1,32,1024]{3,2,1,0:T(8,128)S(1)}, f32[2,1,32,1024]{3,2,1,0:T(8,128)S(1)}, u32[]{:S(2)}, u32[]{:S(2)}) collective-permute-start(f32[2,1,32,1024]{3,2,1,0:T(8,128)S(1)} %get-tuple-element.16), channel_id=1, source_target_pairs={{0,1},{1,2},{2,3},{3,4},{4,5},{5,6},{6,7},{8,9},{9,10},{10,11},{11... | collective-permute-start | bytes 786440 | tf_op jit(solution)/shard_map/ppermute | solution.py:286
  8.4 10.6 %collective-permute-start.1 = (f32[2,8,1,1024]{3,2,1,0:T(1,128)S(1)}, f32[2,8,1,1024]{3,2,1,0:T(1,128)S(1)}, u32[]{:S(2)}, u32[]{:S(2)}) collective-permute-start(f32[2,8,1,1024]{3,2,1,0:T(1,128)S(1)} %get-tuple-element.17), channel_id=1, source_target_pairs={{8,0},{16,8},{24,16},{32,24},{40,32},{48,40},{56,48},{64,56},{72,6... | collective-permute-start | bytes 196616 | tf_op jit(solution)/shard_map/ppermute | solution.py:286
  17.0 3.2 %collective-permute-start = (f32[2,8,1,1024]{3,2,1,0:T(1,128)S(1)}, f32[2,8,1,1024]{3,2,1,0:T(1,128)S(1)}, u32[]{:S(2)}, u32[]{:S(2)}) collective-permute-start(f32[2,8,1,1024]{3,2,1,0:T(1,128)S(1)} %get-tuple-element.18), channel_id=1, source_target_pairs={{0,8},{8,16},{16,24},{24,32},{32,40},{40,48},{48,56},{56,64},{64,7... | collective-permute-start | bytes 196616 | tf_op jit(solution)/shard_map/ppermute | solution.py:286
  20.3 0.7 copy-start.1
  28.3 1.5 %copy-start = (s32[32,128]{1,0:T(8,128)}, s32[32,128]{1,0:T(8,128)S(1)}, u32[]{:S(2)}) copy-start(s32[32,128]{1,0:T(8,128)S(1)} %get-tuple-element.14.back) | copy-start | bytes 49156
  112.6 8.3 %collective-permute-start.4 = (f32[4,2,2,2,4,32,128]{6,5,4,3,2,1,0:T(8,128)S(1)}, f32[4,2,2,2,4,32,128]{6,5,4,3,2,1,0:T(8,128)}, u32[]{:S(2)}, u32[]{:S(2)}) collective-permute-start(f32[4,2,2,2,4,32,128]{6,5,4,3,2,1,0:T(8,128)S(1)} %all_to_all.11.pieces), channel_id=1, source_target_pairs={{0,8},{8,0},{1,9},{9,1},{2,10},{10,2},{3,11},{11,3},{4,12},{12,4},... | collective-permute-start | bytes 6291464 | tf_op jit(solution)/shard_map/ppermute | solution.py:307

commit v4 on v3

--- a/solution.py
+++ b/solution.py
@@ -1,9 +1,11 @@
+import functools
+
 import jax
 import jax.numpy as jnp
 from jax import lax
 from jax.experimental import pallas as pl
 from jax.experimental.pallas import tpu as pltpu
-from jax.sharding import Mesh, PartitionSpec as P
+from jax.sharding import PartitionSpec as P
 
 LANES = 128
 SUBS = 8
@@ -100,46 +102,48 @@
 
 
 def inner_kernel(
-    fields, bins, xlo, xhi, colour, opacity, view, cells, picks, mid, tab, back, colour_now, opacity_now, field_sem, bin_sem, tab_sem
+    fields, bins, xlo, xhi, colour, opacity, view, cells, picks, mid, tab, back, colour_now, opacity_now, view_now, field_sem, bin_sem, tab_sem
 ):
     depth, cols, rows = fields.shape[1:]
-    groups = cols // SUBS
-    spans = [pl.ds(g * SUBS, SUBS) for g in range(groups)]
-    tab_copies = [
-        pltpu.make_async_copy(colour, colour_now, tab_sem.at[0]),
-        pltpu.make_async_copy(opacity, opacity_now, tab_sem.at[1]),
+    groups, half = cols // SUBS, rows // 2
+    small = [
+        pltpu.make_async_copy(source, target, tab_sem.at[n])
+        for n, (source, target) in enumerate(((colour, colour_now), (opacity, opacity_now), (view, view_now)))
     ]
-    field_copies, bin_copies = [], []
-    for g, span in enumerate(spans):
-        target = cells.at[:, :, span, pl.ds(LANES, rows)]
-        field_copies.append(pltpu.make_async_copy(fields.at[:, :, span, :], target, field_sem.at[g]))
-        bin_copies.append(pltpu.make_async_copy(bins.at[:, :, span, :], picks.at[:, :, span, :], bin_sem.at[g]))
-    for copy in tab_copies + [field_copies[0], bin_copies[0], field_copies[1]]:
+    parts = (pl.ds(0, half + LANES), pl.ds(half + LANES, half - LANES))
+    field_copies, bin_copies = {}, {}
+    for g in range(groups):
+        span = pl.ds(g * SUBS, SUBS)
+        for h, part in enumerate(parts):
+            target = cells.at[:, :, span, pl.ds(LANES + part.start, part.size)]
+            field_copies[g, h] = pltpu.make_async_copy(fields.at[:, :, span, part], target, field_sem.at[g, h])
+            part = pl.ds(h * half, half)
+            bin_copies[g, h] = pltpu.make_async_copy(bins.at[:, :, span, part], picks.at[:, :, span, part], bin_sem.at[g, h])
+    for copy in small:
         copy.start()
-    for g in range(1, groups):
-        bin_copies[g].start()
-        if g + 1 < groups:
-            field_copies[g + 1].start()
+    for g in range(groups):
+        for h in range(2):
+            if g == 0:
+                field_copies[g, h].start()
+            if g + 1 < groups:
+                field_copies[g + 1, h].start()
+            bin_copies[g, h].start()
     zero = jnp.zeros((cols, LANES), jnp.float32)
     for f in range(2):
         for d in range(depth):
             cells[f, d, :, 0:LANES] = zero
             cells[f, d, :, LANES + rows :] = zero
+    for copy in small:
+        copy.wait()
     sub = lax.broadcasted_iota(jnp.int32, (SUBS, LANES), 0)
     for g in range(groups):
         towards = jnp.zeros((SUBS, LANES), jnp.int32)
         for k in range(SUBS):
-            towards = jnp.where(sub == k, view[g * SUBS + k], towards)
+            towards = jnp.where(sub == k, view_now[g * SUBS + k], towards)
         back[g * SUBS : (g + 1) * SUBS, :] = towards
-    for copy in tab_copies:
-        copy.wait()
     store_tables(colour_now, opacity_now, tab)
     edges = masks()
-    field_copies[0].wait()
     for g in range(groups):
-        if g + 1 < groups:
-            field_copies[g + 1].wait()
-        bin_copies[g].wait()
         backward = back[g * SUBS : (g + 1) * SUBS, :] == 1
 
         def tile(b, carry, g=g, backward=backward):
@@ -149,12 +153,18 @@
             def element(d):
                 return cell(at, lambda f: picks[f, d, pl.ds(g * SUBS, SUBS), pl.ds(start, LANES)], d, tab, edges)
 
-            parts, through = composite((element(d) for d in range(1, depth - 1)), backward)
-            for k, part in enumerate(parts + [through]):
-                mid[b, k, pl.ds(g * SUBS, SUBS), :] = part
+            colours, through = composite((element(d) for d in range(1, depth - 1)), backward)
+            for k, value in enumerate(colours + [through]):
+                mid[b, k, pl.ds(g * SUBS, SUBS), :] = value
             return carry
 
-        lax.fori_loop(0, rows // LANES, tile, 0, unroll=4)
+        for h in range(2):
+            if g == 0:
+                field_copies[g, h].wait()
+            if g + 1 < groups:
+                field_copies[g + 1, h].wait()
+            bin_copies[g, h].wait()
+            lax.fori_loop(h * half // LANES, (h + 1) * half // LANES, tile, 0, unroll=4)
 
 
 def outer_kernel(cells, zlo, zhi, xlo, xhi, picks, mid, tab, back, out):
@@ -190,7 +200,7 @@
 def march_inner(fields, bins, xlo, xhi, colour, opacity, view):
     _, depth, cols, rows = fields.shape
     resident = [pltpu.with_memory_space_constraint(x, pltpu.HBM) for x in (fields, bins)]
-    tables = [pltpu.with_memory_space_constraint(x, pltpu.HBM) for x in (colour, opacity)]
+    tables = [pltpu.with_memory_space_constraint(x, pltpu.HBM) for x in (colour, opacity, view)]
     return pl.pallas_call(
         inner_kernel,
         out_shape=[
@@ -200,19 +210,20 @@
             pltpu.VMEM((2, 2, 2, SUBS, LANES), jnp.int32),
             pltpu.VMEM((cols, LANES), jnp.int32),
         ],
-        in_specs=[ANY, ANY, VMEM, VMEM, ANY, ANY, SMEM],
+        in_specs=[ANY, ANY, VMEM, VMEM, ANY, ANY, ANY],
         out_specs=[VMEM] * 5,
         scratch_shapes=[
             pltpu.VMEM(colour.shape, colour.dtype),
             pltpu.VMEM(opacity.shape, opacity.dtype),
-            pltpu.SemaphoreType.DMA((cols // SUBS,)),
-            pltpu.SemaphoreType.DMA((cols // SUBS,)),
-            pltpu.SemaphoreType.DMA((2,)),
+            pltpu.SMEM(view.shape, view.dtype),
+            pltpu.SemaphoreType.DMA((cols // SUBS, 2)),
+            pltpu.SemaphoreType.DMA((cols // SUBS, 2)),
+            pltpu.SemaphoreType.DMA((3,)),
         ],
         compiler_params=pltpu.CompilerParams(vmem_limit_bytes=LIMIT),
-        cost_estimate=pl.CostEstimate(flops=100 * 2 * depth * cols * rows, bytes_accessed=8 * 2**20, transcendentals=0),
+        cost_estimate=pl.CostEstimate(flops=50_000 * 2 * depth * cols * rows, bytes_accessed=64 * 2**20, transcendentals=0),
         name="march_inner",
-    )(*resident, xlo, xhi, *tables, view)
+    )(*resident, xlo, xhi, *tables)
 
 
 def march_outer(cells, zlo, zhi, xlo, xhi, picks, mid, tab, back):
@@ -241,43 +252,86 @@
 def join(parts, back):
     return pl.pallas_call(
         join_kernel,
-        out_shape=jax.ShapeDtypeStruct(parts.shape[1:], jnp.float32),
+        out_shape=pltpu.VMEM(parts.shape[1:], jnp.float32),
         in_specs=[VMEM, VMEM],
         out_specs=VMEM,
         name="join",
-    )(parts, back)
-
-
-def place_kernel(core, pieces, *refs):
-    out = refs[-1]
+    )(pltpu.with_memory_space_constraint(parts, pltpu.VMEM), back)
+
+
+Z, X, CORES = 8, 4, 2
+
+
+def device(z, x, core):
+    return (z % Z * X + x % X) * CORES + core
+
+
+def everywhere(target):
+    places = [(z, x, core) for z in range(Z) for x in range(X) for core in range(CORES)]
+    return [(device(*spot), device(*target(*spot))) for spot in places]
+
+
+def pairs(partner):
+    return [list(pair) for pair in everywhere(partner) if pair[0] < pair[1]]
+
+
+DOUBLINGS = (
+    pairs(lambda z, x, core: (z, x ^ 2, core) if core else (z ^ 4, x, core)),
+    pairs(lambda z, x, core: (z, x ^ 1, core) if core else (z ^ 2, x, core)),
+    pairs(lambda z, x, core: (z ^ 4, x, core) if core else (z ^ 1, x, core)),
+)
+MOVES = (
+    everywhere(lambda z, x, core: (z + 1, x, core) if core else (z, x + 1, core)),
+    everywhere(lambda z, x, core: (z - 1, x, core) if core else (z, x - 1, core)),
+    everywhere(lambda z, x, core: (z - 2 if z % 2 else z + 2, x, core) if core else (z, x + 2, core)),
+)
+STEPS = (0, 1, -1, 2)
+SWAP = everywhere(lambda z, x, core: (z, x, 1 - core))
+
+
+def gather(block):
+    for groups in DOUBLINGS:
+        block = lax.all_gather(block, "wide", axis_index_groups=groups)
+    return [block] + [lax.ppermute(block, "wide", move) for move in MOVES]
+
+
+def place_kernel(swapped, spot, *refs):
+    pieces, out = refs[: len(STEPS)], refs[-1]
     channel = pl.program_id(0)
-    for x in range(pieces.shape[0]):
-        for high in range(2):
-            for mid in range(2):
-                for low in range(2):
-                    out[0, 4 * high + 2 * mid + low, x, 0] = pieces[x, low, mid, high, channel]
-
-
-def place(pieces, core, frame=None):
-    x_count = pieces.shape[0]
-    channels, cols, rows = pieces.shape[4:]
-    whole = (channels, 8, x_count, 2, cols, rows)
-    block = (1, 8, x_count, 1, cols, rows)
+    wide = spot[0]
+    core = (wide + swapped) % CORES
+    x, z = wide // CORES % X, wide // (CORES * X)
+    for piece, step in enumerate(STEPS):
+        x_from, z_from = (x + X - step) % X, (z + Z - step) % (Z // 2)
+        for third in range(2):
+            for second in range(2):
+                for first in range(2):
+                    z_zero, x_zero = 4 * first + 2 * second + third, x_from
+                    z_one, x_one = 4 * third + z_from, 2 * first + second
+                    z_now = jnp.where(core == 0, z_zero, z_one)
+                    x_now = jnp.where(core == 0, x_zero, x_one)
+                    out[0, z_now, x_now, 0] = pieces[piece][third, second, first, channel]
+
+
+def place(pieces, spot, swapped, frame=None):
+    channels, cols, rows = pieces[0].shape[3:]
     kept = [] if frame is None else [frame]
     return pl.pallas_call(
-        place_kernel,
+        functools.partial(place_kernel, swapped),
         grid_spec=pltpu.PrefetchScalarGridSpec(
             num_scalar_prefetch=1,
             grid=(channels,),
-            in_specs=[VMEM] + [ANY] * len(kept),
-            out_specs=pl.BlockSpec(block, lambda channel, core: (channel, 0, 0, core[0], 0, 0)),
+            in_specs=[VMEM] * len(pieces) + [ANY] * len(kept),
+            out_specs=pl.BlockSpec(
+                (1, Z, X, 1, cols, rows), lambda channel, spot: (channel, 0, 0, (spot[0] + swapped) % CORES, 0, 0)
+            ),
         ),
-        out_shape=jax.ShapeDtypeStruct(whole, jnp.float32),
-        input_output_aliases={2: 0} if kept else {},
+        out_shape=jax.ShapeDtypeStruct((channels, Z, X, CORES, cols, rows), jnp.float32),
+        input_output_aliases={1 + len(pieces): 0} if kept else {},
         compiler_params=pltpu.CompilerParams(vmem_limit_bytes=LIMIT),
         cost_estimate=pl.CostEstimate(flops=0, bytes_accessed=4 * 2**20, transcendentals=0),
         name="place",
-    )(core.reshape(1), pieces, *kept)
+    )(spot, *(pltpu.with_memory_space_constraint(piece, pltpu.VMEM) for piece in pieces), *kept)
 
 
 def shifted(value, axis, step, wrap=True):
@@ -286,38 +340,30 @@
     return lax.ppermute(value, axis, route)
 
 
-WIDE = ("z_high", "z_mid", "z_low", "x", "core")
-
-
 def on_device(fields, field_bins, colour_table, opacity_table, view_dir):
     depth, cols = fields.shape[1:3]
-    xlo = shifted(fields[:, :, cols - 1 :], WIDE, 1, wrap=False)
-    xhi = shifted(fields[:, :, :1], WIDE, -1, wrap=False)
-    zlo = shifted(fields[:, depth - 1 :], "y", 1, wrap=False)
-    zhi = shifted(fields[:, :1], "y", -1, wrap=False)
+    left, right, fields_after = lax.optimization_barrier((fields[:, :, :1], fields[:, :, cols - 1 :], fields))
+    xlo = shifted(right, "wide", 1, wrap=False)
+    xhi = shifted(left, "wide", -1, wrap=False)
+    zlo = shifted(fields_after[:, depth - 1 :], "narrow", 1, wrap=False)
+    zhi = shifted(fields_after[:, :1], "narrow", -1, wrap=False)
     colour = jnp.transpose(colour_table, (1, 0, 2))
     cells, picks, mid, tab, back = march_inner(fields, field_bins, xlo, xhi, colour, opacity_table, view_dir)
     partial = march_outer(cells, zlo, zhi, xlo, xhi, picks, mid, tab, back)
-    partial = lax.all_to_all(partial, "y", 0, 0)
-    column = join(partial, back)
-    for axis in ("z_high", "z_mid", "z_low"):
-        column = lax.all_gather(column, axis)
-    x_count = lax.axis_size("x")
-    own = lax.all_to_all(jnp.broadcast_to(column[None], (x_count,) + column.shape), "x", 0, 0)
-    other = lax.ppermute(own, "core", [(0, 1), (1, 0)])
-    core = lax.axis_index("core").astype(jnp.int32)
-    frame = place(other, 1 - core, place(own, core))
-    channels, _, _, _, _, rows = frame.shape
-    return frame.reshape(channels, -1, rows)
+    partial = lax.all_to_all(partial, "narrow", 0, 0)
+    own = gather(join(partial, back))
+    other = [lax.ppermute(piece, "wide", SWAP) for piece in own]
+    spot = lax.axis_index("wide").reshape(1)
+    frame = place(other, spot, 1, place(own, spot, 0))
+    return frame.reshape(frame.shape[0], -1, frame.shape[-1])
 
 
 def solution(mesh):
-    grid = Mesh(mesh.devices.reshape(2, 2, 2, 4, 2, 8), WIDE + ("y",))
-    split = P(None, "y", WIDE, None)
+    split = P(None, "narrow", "wide", None)
     return jax.shard_map(
         on_device,
-        mesh=grid,
-        in_specs=(split, split, P(), P(), P(WIDE)),
-        out_specs=P(None, None, "y"),
+        mesh=mesh,
+        in_specs=(split, split, P(), P(), P("wide")),
+        out_specs=P(None, None, "narrow"),
         check_vma=False,
     )

time: 125 us -> 110 us (0.88)
  blocking collectives: 80.8 us -> 43.8 us
  starting transfers between devices: 21 us -> 49 us
  waiting for transfers between devices: 3.34 us -> 0.03 us
  Pallas kernels: 15.8 us -> 14.1 us
    all_to_all x2 -> x1, blocking collectives: 59.7 us -> 21 us  [on_device(): partial = lax.all_to_all(partial, 'narrow', 0, 0)]
    ppermute x1 -> x7, starting transfers between devices: 4.41 us -> 33.6 us  [the longest x4 22.4 us: on_device(): other = [lax.ppermute(piece, 'wide', SWAP) for piece in own]]
    ppermute x1 -> x7, waiting for transfers between devices: 2.03 us -> 0.02 us  [the longest x4 0.01 us: on_device(): other = [lax.ppermute(piece, 'wide', SWAP) for piece in own]]
    all_gather x3, blocking collectives: 21.1 us -> 22.8 us  [gather(): block = lax.all_gather(block, 'wide', axis_index_groups=groups)]
    ppermute x4, waiting for transfers between devices: 1.31 us -> 0.01 us  [shifted(): return lax.ppermute(value, axis, route)]
  transfers between devices with their start and end apart: 5 -> 11, of which waited for: 2 -> 0; matrix products, arithmetic and copies ran while one was open for 1% -> 1% of each run, Pallas kernels for 7% -> 8%
where the time goes in v4:
time: 110 us
  starting transfers between devices  49 us (45%)
  blocking collectives  43.8 us (40%)
  Pallas kernels  14.1 us (13%)
  local copies, waits for them, and re-layouts  2.37 us (2%)
    all_gather x3, blocking collectives, gather(): block = lax.all_gather(block, 'wide', axis_index_groups=groups)  22.8 us
    ppermute x4, starting transfers between devices, on_device(): other = [lax.ppermute(piece, 'wide', SWAP) for piece in own]  22.4 us
    all_to_all x1, blocking collectives, on_device(): partial = lax.all_to_all(partial, 'narrow', 0, 0)  21 us
    ppermute x4, starting transfers between devices, shifted(): return lax.ppermute(value, axis, route)  15.4 us
    ppermute x3, starting transfers between devices, gather(): return [block] + [lax.ppermute(block, 'wide', move) for move in MOVES]  11.3 us
    pallas_call x1, Pallas kernels, march_inner(): pl.pallas_call(inner_kernel, out_shape=[pltpu.VMEM((2, depth, cols, rows...  6.82 us
    pallas_call x2, Pallas kernels, place(): pl.pallas_call(functools.partial(place_kernel, swapped), grid_spec=pltpu....  5.06 us
  transfers between devices with their start and end apart: 11, of which 0 were waited for; matrix products, arithmetic and copies ran while one was open for 1% of the time, Pallas kernels for 8%

profile of v4, /device:TPU:1, one launch (start us, length us, event | category | flops | bytes accessed | tf_op | source)
XLA Modules:
  0.0 109.5 jit_solution(13772646187602696097)
XLA Ops:
  0.0 1.3 %fusion.1 = (f32[2,8,1,1024]{3,2,1,0:T(1,128)S(1)}, f32[2,8,1,1024]{3,2,1,0:T(1,128)S(1)}) fusion(f32[2,8,32,1024]{3,2,1,0:T(8,128)} %fields.1), kind=kLoop, calls=%fused_computation.1 | loop fusion | bytes 262144 | tf_op jit(solution)/shard_map/slice | solution.py:345
  1.3 4.5 %collective-permute-start = (f32[2,8,1,1024]{3,2,1,0:T(1,128)S(1)}, f32[2,8,1,1024]{3,2,1,0:T(1,128)S(1)}, u32[]{:S(2)}, u32[]{:S(2)}) collective-permute-start(f32[2,8,1,1024]{3,2,1,0:T(1,128)S(1)} %get-tuple-element.13), channel_id=1, source_target_pairs={{0,8},{8,16},{16,24},{24,32},{32,40},{40,48},{48,56},{56,64},{64,7... | collective-permute-start | bytes 196616 | tf_op jit(solution)/shard_map/ppermute | solution.py:340
  5.8 5.6 %collective-permute-start.1 = (f32[2,8,1,1024]{3,2,1,0:T(1,128)S(1)}, f32[2,8,1,1024]{3,2,1,0:T(1,128)S(1)}, u32[]{:S(2)}, u32[]{:S(2)}) collective-permute-start(f32[2,8,1,1024]{3,2,1,0:T(1,128)S(1)} %get-tuple-element.14), channel_id=1, source_target_pairs={{8,0},{16,8},{24,16},{32,24},{40,32},{48,40},{56,48},{64,56},{72,6... | collective-permute-start | bytes 196616 | tf_op jit(solution)/shard_map/ppermute | solution.py:340
  11.4 1.1 fusion
  12.5 1.3 %collective-permute-start.3 = (f32[2,1,32,1024]{3,2,1,0:T(8,128)S(1)}, f32[2,1,32,1024]{3,2,1,0:T(8,128)S(1)}, u32[]{:S(2)}, u32[]{:S(2)}) collective-permute-start(f32[2,1,32,1024]{3,2,1,0:T(8,128)S(1)} %get-tuple-element.21), channel_id=1, source_target_pairs={{1,0},{2,1},{3,2},{4,3},{5,4},{6,5},{7,6},{9,8},{10,9},{11,10},{12... | collective-permute-start | bytes 786440 | tf_op jit(solution)/shard_map/ppermute | solution.py:340
  13.8 4.0 %collective-permute-start.2 = (f32[2,1,32,1024]{3,2,1,0:T(8,128)S(1)}, f32[2,1,32,1024]{3,2,1,0:T(8,128)S(1)}, u32[]{:S(2)}, u32[]{:S(2)}) collective-permute-start(f32[2,1,32,1024]{3,2,1,0:T(8,128)S(1)} %get-tuple-element.22), channel_id=1, source_target_pairs={{0,1},{1,2},{2,3},{3,4},{4,5},{5,6},{6,7},{8,9},{9,10},{10,11},{11... | collective-permute-start | bytes 786440 | tf_op jit(solution)/shard_map/ppermute | solution.py:340
  17.8 0.0 collective-permute-done.xlo
  17.8 0.0 collective-permute-done.1.xhi
  17.8 6.8 %march_inner.1 = (f32[2,8,32,1280]{3,2,1,0:T(8,128)S(1)}, s32[2,8,32,1024]{3,2,1,0:T(8,128)S(1)}, f32[8,4,32,128]{3,2,1,0:T(8,128)S(1)}, s32[2,2,2,8,128]{4,3,2,1,0:T(8,128)S(1)}, s32[32,128]{1,0:T(8,128)S(1)}) custom-call(f32[2,8,32,1024]{3,2,1,0:T(8,128)} %fields.1, s32[2,8,32,1024]{3,2,1,0:T(8,128)} %bins.1, ...), custom_call_target="tpu_custom_call" | custom-call | flops 26214400000 | bytes 67108864 | tf_op jit(solution)/shard_map/march_inner/pallas_call | solution.py:204
  24.6 0.0 copy-start
  24.6 0.0 collective-permute-done.3.zhi
  24.7 0.0 collective-permute-done.2.zlo
  24.7 1.4 %march_outer.1 = f32[8,4,32,128]{3,2,1,0:T(8,128)S(1)} custom-call(f32[2,8,32,1280]{3,2,1,0:T(8,128)S(1)} %get-tuple-element.15.cells, f32[2,1,32,1024]{3,2,1,0:T(8,128)S(1)} %collective-permute-done.2.zlo, f32[2,1,32,1024]{3,2,1,0:T(8,128)S(1)} %collective-permute-done.3.zhi, f32[2,8,1,1024]{3,2,1,0:T(1,128)S(1)} %collective-permute-done.xlo, ...), custom_call_target="tpu_custom_call" | custom-call | tf_op jit(solution)/shard_map/march_outer/pallas_call | solution.py:231
  26.1 0.0 copy-done
  26.1 21.0 %all_to_all.5.parts = f32[8,4,32,128]{3,2,1,0:T(8,128)S(1)} all-to-all(f32[8,4,32,128]{3,2,1,0:T(8,128)S(1)} %march_outer.1), channel_id=1, replica_groups=mesh['wide'=64,'narrow'=8] {'narrow'}, dimensions={0} | all-to-all | bytes 1048576 | tf_op jit(solution)/shard_map/all_to_all | solution.py:353
  47.1 0.8 join.1
  47.9 5.3 %all-gather = f32[8,32,128]{2,1,0:T(8,128)S(1)} all-gather(f32[4,32,128]{2,1,0:T(8,128)S(1)} %join.1), channel_id=2, replica_groups={{0,256},{8,40},{16,272},{24,56},{32,288},{48,304},{64,320},{72,104},{80..., dimensions={0}, use_global_device_ids=true | all-gather | bytes 196608 | tf_op jit(solution)/shard_map/all_gather | solution.py:294
  53.1 4.8 %all-gather.1 = f32[4,4,32,128]{3,2,1,0:T(8,128)S(1)} all-gather(f32[2,4,32,128]{3,2,1,0:T(8,128)S(1)} %bitcast.12), channel_id=3, replica_groups={{0,128},{8,24},{16,144},{32,160},{40,56},{48,176},{64,192},{72,88},{80,..., dimensions={0}, use_global_device_ids=true | all-gather | bytes 393216 | tf_op jit(solution)/shard_map/all_gather | solution.py:294
  57.9 12.8 %all-gather.2 = f32[4,2,4,32,128]{4,3,2,1,0:T(8,128)S(1)} all-gather(f32[2,2,4,32,128]{4,3,2,1,0:T(8,128)S(1)} %bitcast.11), channel_id=4, replica_groups={{0,64},{8,264},{16,80},{24,280},{32,96},{40,296},{48,112},{56,312},{72,..., dimensions={0}, use_global_device_ids=true | all-gather | bytes 786432 | tf_op jit(solution)/shard_map/all_gather | solution.py:294
  70.7 3.4 %collective-permute-start.9 = (f32[2,2,2,4,32,128]{5,4,3,2,1,0:T(8,128)S(1)}, f32[2,2,2,4,32,128]{5,4,3,2,1,0:T(8,128)S(1)}, u32[]{:S(2)}, u32[]{:S(2)}) collective-permute-start(f32[2,2,2,4,32,128]{5,4,3,2,1,0:T(8,128)S(1)} %bitcast.6), channel_id=1, source_target_pairs={{0,32},{8,136},{16,48},{24,152},{32,0},{40,168},{48,16},{56,184},{... | collective-permute-start | bytes 1572872 | tf_op jit(solution)/shard_map/ppermute | solution.py:295
  74.1 4.8 %collective-permute-start.7 = (f32[2,2,2,4,32,128]{5,4,3,2,1,0:T(8,128)S(1)}, f32[2,2,2,4,32,128]{5,4,3,2,1,0:T(8,128)S(1)}, u32[]{:S(2)}, u32[]{:S(2)}) collective-permute-start(f32[2,2,2,4,32,128]{5,4,3,2,1,0:T(8,128)S(1)} %bitcast.7), channel_id=1, source_target_pairs={{0,48},{8,456},{16,0},{24,472},{32,16},{40,488},{48,32},{56,504},{... | collective-permute-start | bytes 1572872 | tf_op jit(solution)/shard_map/ppermute | solution.py:295
  78.9 3.1 %collective-permute-start.5 = (f32[2,2,2,4,32,128]{5,4,3,2,1,0:T(8,128)S(1)}, f32[2,2,2,4,32,128]{5,4,3,2,1,0:T(8,128)S(1)}, u32[]{:S(2)}, u32[]{:S(2)}) collective-permute-start(f32[2,2,2,4,32,128]{5,4,3,2,1,0:T(8,128)S(1)} %bitcast.8), channel_id=1, source_target_pairs={{0,16},{8,72},{16,32},{24,88},{32,48},{40,104},{48,0},{56,120},{64... | collective-permute-start | bytes 1572872 | tf_op jit(solution)/shard_map/ppermute | solution.py:295
  82.0 12.7 %collective-permute-start.4 = (f32[2,2,2,4,32,128]{5,4,3,2,1,0:T(8,128)S(1)}, f32[2,2,2,4,32,128]{5,4,3,2,1,0:T(8,128)S(1)}, u32[]{:S(2)}, u32[]{:S(2)}) collective-permute-start(f32[2,2,2,4,32,128]{5,4,3,2,1,0:T(8,128)S(1)} %bitcast.9), channel_id=1, source_target_pairs={{0,8},{8,0},{16,24},{24,16},{32,40},{40,32},{48,56},{56,48},{64,72... | collective-permute-start | bytes 1572872 | tf_op jit(solution)/shard_map/ppermute | solution.py:355
  94.7 0.0 collective-permute-done.9.refs_3_
  94.7 2.1 %collective-permute-start.10 = (f32[2,2,2,4,32,128]{5,4,3,2,1,0:T(8,128)S(1)}, f32[2,2,2,4,32,128]{5,4,3,2,1,0:T(8,128)S(1)}, u32[]{:S(2)}, u32[]{:S(2)}) collective-permute-start(f32[2,2,2,4,32,128]{5,4,3,2,1,0:T(8,128)S(1)} %collective-permute-done.9.refs_3_), channel_id=1, source_target_pairs={{0,8},{8,0},{16,24},{24,16},{32,40},{40,32},{48,56},{56,48},{64,72... | collective-permute-start | bytes 1572872 | tf_op jit(solution)/shard_map/ppermute | solution.py:355
  96.7 0.0 collective-permute-done.7.refs_2_
  96.7 5.2 %collective-permute-start.8 = (f32[2,2,2,4,32,128]{5,4,3,2,1,0:T(8,128)S(1)}, f32[2,2,2,4,32,128]{5,4,3,2,1,0:T(8,128)}, u32[]{:S(2)}, u32[]{:S(2)}) collective-permute-start(f32[2,2,2,4,32,128]{5,4,3,2,1,0:T(8,128)S(1)} %collective-permute-done.7.refs_2_), channel_id=1, source_target_pairs={{0,8},{8,0},{16,24},{24,16},{32,40},{40,32},{48,56},{56,48},{64,72... | collective-permute-start | bytes 1572872 | tf_op jit(solution)/shard_map/ppermute | solution.py:355
  102.0 0.0 collective-permute-done.5.refs_1_
  102.0 2.4 %collective-permute-start.6 = (f32[2,2,2,4,32,128]{5,4,3,2,1,0:T(8,128)S(1)}, f32[2,2,2,4,32,128]{5,4,3,2,1,0:T(8,128)}, u32[]{:S(2)}, u32[]{:S(2)}) collective-permute-start(f32[2,2,2,4,32,128]{5,4,3,2,1,0:T(8,128)S(1)} %collective-permute-done.5.refs_1_), channel_id=1, source_target_pairs={{0,8},{8,0},{16,24},{24,16},{32,40},{40,32},{48,56},{56,48},{64,72... | collective-permute-start | bytes 1572872 | tf_op jit(solution)/shard_map/ppermute | solution.py:355
  104.4 2.0 %place.2.refs_4_ = f32[4,8,4,2,32,128]{5,4,3,2,1,0:T(8,128)} custom-call(s32[1]{0:T(128)} %bitcast.spot, f32[2,2,2,4,32,128]{5,4,3,2,1,0:T(8,128)S(1)} %bitcast.10, f32[2,2,2,4,32,128]{5,4,3,2,1,0:T(8,128)S(1)} %collective-permute-done.5.refs_1_, f32[2,2,2,4,32,128]{5,4,3,2,1,0:T(8,128)S(1)} %collective-permute-done.7.refs_2_, ...), custom_call_target="tpu_custom_call" | custom-call | bytes 4194304 | tf_op jit(solution)/shard_map/place/pallas_call | solution.py:319
  106.4 0.0 collective-permute-done.4.refs_0_
  106.4 0.0 collective-permute-done.10.refs_3_
  106.4 0.0 collective-permute-done.8.refs_2_
  106.4 0.0 collective-permute-done.6.refs_1_
  106.4 3.1 %place.3 = f32[4,8,4,2,32,128]{5,4,3,2,1,0:T(8,128)} custom-call(s32[1]{0:T(128)} %bitcast.spot, f32[2,2,2,4,32,128]{5,4,3,2,1,0:T(8,128)S(1)} %collective-permute-done.4.refs_0_, f32[2,2,2,4,32,128]{5,4,3,2,1,0:T(8,128)} %collective-permute-done.6.refs_1_, f32[2,2,2,4,32,128]{5,4,3,2,1,0:T(8,128)} %collective-permute-done.8.refs_2_, ...), custom_call_target="tpu_custom_call", output_to_operand_aliasing={{}: (5, {})} | custom-call | bytes 4194304 | tf_op jit(solution)/shard_map/place/pallas_call | solution.py:319
Async XLA Ops:
  1.3 16.5 %collective-permute-start = (f32[2,8,1,1024]{3,2,1,0:T(1,128)S(1)}, f32[2,8,1,1024]{3,2,1,0:T(1,128)S(1)}, u32[]{:S(2)}, u32[]{:S(2)}) collective-permute-start(f32[2,8,1,1024]{3,2,1,0:T(1,128)S(1)} %get-tuple-element.13), channel_id=1, source_target_pairs={{0,8},{8,16},{16,24},{24,32},{32,40},{40,48},{48,56},{56,64},{64,7... | collective-permute-start | bytes 196616 | tf_op jit(solution)/shard_map/ppermute | solution.py:340
  5.8 12.0 %collective-permute-start.1 = (f32[2,8,1,1024]{3,2,1,0:T(1,128)S(1)}, f32[2,8,1,1024]{3,2,1,0:T(1,128)S(1)}, u32[]{:S(2)}, u32[]{:S(2)}) collective-permute-start(f32[2,8,1,1024]{3,2,1,0:T(1,128)S(1)} %get-tuple-element.14), channel_id=1, source_target_pairs={{8,0},{16,8},{24,16},{32,24},{40,32},{48,40},{56,48},{64,56},{72,6... | collective-permute-start | bytes 196616 | tf_op jit(solution)/shard_map/ppermute | solution.py:340
  12.5 12.2 %collective-permute-start.3 = (f32[2,1,32,1024]{3,2,1,0:T(8,128)S(1)}, f32[2,1,32,1024]{3,2,1,0:T(8,128)S(1)}, u32[]{:S(2)}, u32[]{:S(2)}) collective-permute-start(f32[2,1,32,1024]{3,2,1,0:T(8,128)S(1)} %get-tuple-element.21), channel_id=1, source_target_pairs={{1,0},{2,1},{3,2},{4,3},{5,4},{6,5},{7,6},{9,8},{10,9},{11,10},{12... | collective-permute-start | bytes 786440 | tf_op jit(solution)/shard_map/ppermute | solution.py:340
  13.8 10.9 %collective-permute-start.2 = (f32[2,1,32,1024]{3,2,1,0:T(8,128)S(1)}, f32[2,1,32,1024]{3,2,1,0:T(8,128)S(1)}, u32[]{:S(2)}, u32[]{:S(2)}) collective-permute-start(f32[2,1,32,1024]{3,2,1,0:T(8,128)S(1)} %get-tuple-element.22), channel_id=1, source_target_pairs={{0,1},{1,2},{2,3},{3,4},{4,5},{5,6},{6,7},{8,9},{9,10},{10,11},{11... | collective-permute-start | bytes 786440 | tf_op jit(solution)/shard_map/ppermute | solution.py:340
  24.6 1.5 %copy-start = (s32[32,128]{1,0:T(8,128)}, s32[32,128]{1,0:T(8,128)S(1)}, u32[]{:S(2)}) copy-start(s32[32,128]{1,0:T(8,128)S(1)} %get-tuple-element.20.back) | copy-start | bytes 49156
  70.7 24.0 %collective-permute-start.9 = (f32[2,2,2,4,32,128]{5,4,3,2,1,0:T(8,128)S(1)}, f32[2,2,2,4,32,128]{5,4,3,2,1,0:T(8,128)S(1)}, u32[]{:S(2)}, u32[]{:S(2)}) collective-permute-start(f32[2,2,2,4,32,128]{5,4,3,2,1,0:T(8,128)S(1)} %bitcast.6), channel_id=1, source_target_pairs={{0,32},{8,136},{16,48},{24,152},{32,0},{40,168},{48,16},{56,184},{... | collective-permute-start | bytes 1572872 | tf_op jit(solution)/shard_map/ppermute | solution.py:295
  74.1 22.6 %collective-permute-start.7 = (f32[2,2,2,4,32,128]{5,4,3,2,1,0:T(8,128)S(1)}, f32[2,2,2,4,32,128]{5,4,3,2,1,0:T(8,128)S(1)}, u32[]{:S(2)}, u32[]{:S(2)}) collective-permute-start(f32[2,2,2,4,32,128]{5,4,3,2,1,0:T(8,128)S(1)} %bitcast.7), channel_id=1, source_target_pairs={{0,48},{8,456},{16,0},{24,472},{32,16},{40,488},{48,32},{56,504},{... | collective-permute-start | bytes 1572872 | tf_op jit(solution)/shard_map/ppermute | solution.py:295
  78.9 23.1 %collective-permute-start.5 = (f32[2,2,2,4,32,128]{5,4,3,2,1,0:T(8,128)S(1)}, f32[2,2,2,4,32,128]{5,4,3,2,1,0:T(8,128)S(1)}, u32[]{:S(2)}, u32[]{:S(2)}) collective-permute-start(f32[2,2,2,4,32,128]{5,4,3,2,1,0:T(8,128)S(1)} %bitcast.8), channel_id=1, source_target_pairs={{0,16},{8,72},{16,32},{24,88},{32,48},{40,104},{48,0},{56,120},{64... | collective-permute-start | bytes 1572872 | tf_op jit(solution)/shard_map/ppermute | solution.py:295
  82.0 24.4 %collective-permute-start.4 = (f32[2,2,2,4,32,128]{5,4,3,2,1,0:T(8,128)S(1)}, f32[2,2,2,4,32,128]{5,4,3,2,1,0:T(8,128)S(1)}, u32[]{:S(2)}, u32[]{:S(2)}) collective-permute-start(f32[2,2,2,4,32,128]{5,4,3,2,1,0:T(8,128)S(1)} %bitcast.9), channel_id=1, source_target_pairs={{0,8},{8,0},{16,24},{24,16},{32,40},{40,32},{48,56},{56,48},{64,72... | collective-permute-start | bytes 1572872 | tf_op jit(solution)/shard_map/ppermute | solution.py:355
  94.7 11.7 %collective-permute-start.10 = (f32[2,2,2,4,32,128]{5,4,3,2,1,0:T(8,128)S(1)}, f32[2,2,2,4,32,128]{5,4,3,2,1,0:T(8,128)S(1)}, u32[]{:S(2)}, u32[]{:S(2)}) collective-permute-start(f32[2,2,2,4,32,128]{5,4,3,2,1,0:T(8,128)S(1)} %collective-permute-done.9.refs_3_), channel_id=1, source_target_pairs={{0,8},{8,0},{16,24},{24,16},{32,40},{40,32},{48,56},{56,48},{64,72... | collective-permute-start | bytes 1572872 | tf_op jit(solution)/shard_map/ppermute | solution.py:355
  96.7 9.7 %collective-permute-start.8 = (f32[2,2,2,4,32,128]{5,4,3,2,1,0:T(8,128)S(1)}, f32[2,2,2,4,32,128]{5,4,3,2,1,0:T(8,128)}, u32[]{:S(2)}, u32[]{:S(2)}) collective-permute-start(f32[2,2,2,4,32,128]{5,4,3,2,1,0:T(8,128)S(1)} %collective-permute-done.7.refs_2_), channel_id=1, source_target_pairs={{0,8},{8,0},{16,24},{24,16},{32,40},{40,32},{48,56},{56,48},{64,72... | collective-permute-start | bytes 1572872 | tf_op jit(solution)/shard_map/ppermute | solution.py:355
  102.0 4.4 %collective-permute-start.6 = (f32[2,2,2,4,32,128]{5,4,3,2,1,0:T(8,128)S(1)}, f32[2,2,2,4,32,128]{5,4,3,2,1,0:T(8,128)}, u32[]{:S(2)}, u32[]{:S(2)}) collective-permute-start(f32[2,2,2,4,32,128]{5,4,3,2,1,0:T(8,128)S(1)} %collective-permute-done.5.refs_1_), channel_id=1, source_target_pairs={{0,8},{8,0},{16,24},{24,16},{32,40},{40,32},{48,56},{56,48},{64,72... | collective-permute-start | bytes 1572872 | tf_op jit(solution)/shard_map/ppermute | solution.py:355

commit v5 on v4

--- a/solution.py
+++ b/solution.py
@@ -83,26 +83,27 @@
     return colour, through
 
 
-def lattice(cells, xlo, xhi, zlo, zhi, g, start):
+def lattice(cells, columns, depths, odd, g, start):
     _, depth, cols, _ = cells.shape
     span, here = pl.ds(g * SUBS, SUBS), pl.ds(start, LANES)
 
+    def ghost(faces, is_odd, after, *index):
+        inner, outer = (face[index] for face in faces)
+        return jnp.where(is_odd != after, inner, outer)
+
     def at(f, d, dc, dr):
-        if d < 0:
-            return zlo[f, 0, span, here]
-        if d == depth:
-            return zhi[f, 0, span, here]
-        if g * SUBS + dc < 0:
-            return jnp.broadcast_to(xlo[f, d, :, here], (SUBS, LANES))
-        if g * SUBS + dc == cols:
-            return jnp.broadcast_to(xhi[f, d, :, here], (SUBS, LANES))
+        if d < 0 or d == depth:
+            return ghost(depths, odd[1], d == depth, f, 0, span, here)
+        if g * SUBS + dc < 0 or g * SUBS + dc == cols:
+            face = ghost(columns, odd[0], dc > 0, f, d, slice(None), here)
+            return jnp.broadcast_to(face, (SUBS, LANES))
         return cells[f, d, pl.ds(g * SUBS + dc, SUBS), pl.ds(start + (LANES + dr), LANES)]
 
     return at
 
 
 def inner_kernel(
-    fields, bins, xlo, xhi, colour, opacity, view, cells, picks, mid, tab, back, colour_now, opacity_now, view_now, field_sem, bin_sem, tab_sem
+    wide, fields, bins, xin, xout, colour, opacity, view, cells, picks, mid, tab, back, colour_now, opacity_now, view_now, field_sem, bin_sem, tab_sem
 ):
     depth, cols, rows = fields.shape[1:]
     groups, half = cols // SUBS, rows // 2
@@ -148,7 +149,7 @@
 
         def tile(b, carry, g=g, backward=backward):
             start = pl.multiple_of(b * LANES, LANES)
-            at = lattice(cells, xlo, xhi, None, None, g, start)
+            at = lattice(cells, (xin, xout), None, (wide[0] % 2 == 1, None), g, start)
 
             def element(d):
                 return cell(at, lambda f: picks[f, d, pl.ds(g * SUBS, SUBS), pl.ds(start, LANES)], d, tab, edges)
@@ -167,7 +168,7 @@
             lax.fori_loop(h * half // LANES, (h + 1) * half // LANES, tile, 0, unroll=4)
 
 
-def outer_kernel(cells, zlo, zhi, xlo, xhi, picks, mid, tab, back, out):
+def outer_kernel(wide, narrow, cells, zin, zout, xin, xout, picks, mid, tab, back, out):
     depth, cols, rows = picks.shape[1:]
     edges = masks()
     for g in range(cols // SUBS):
@@ -175,7 +176,7 @@
 
         def tile(b, carry, g=g, backward=backward):
             start = pl.multiple_of(b * LANES, LANES)
-            at = lattice(cells, xlo, xhi, zlo, zhi, g, start)
+            at = lattice(cells, (xin, xout), (zin, zout), (wide[0] % 2 == 1, narrow[0] % 2 == 1), g, start)
 
             def element(d):
                 return cell(at, lambda f: picks[f, d, pl.ds(g * SUBS, SUBS), pl.ds(start, LANES)], d, tab, edges)
@@ -197,7 +198,7 @@
 LIMIT = 24 * 2**20
 
 
-def march_inner(fields, bins, xlo, xhi, colour, opacity, view):
+def march_inner(wide, fields, bins, xin, xout, colour, opacity, view):
     _, depth, cols, rows = fields.shape
     resident = [pltpu.with_memory_space_constraint(x, pltpu.HBM) for x in (fields, bins)]
     tables = [pltpu.with_memory_space_constraint(x, pltpu.HBM) for x in (colour, opacity, view)]
@@ -210,7 +211,7 @@
             pltpu.VMEM((2, 2, 2, SUBS, LANES), jnp.int32),
             pltpu.VMEM((cols, LANES), jnp.int32),
         ],
-        in_specs=[ANY, ANY, VMEM, VMEM, ANY, ANY, ANY],
+        in_specs=[SMEM, ANY, ANY, VMEM, VMEM, ANY, ANY, ANY],
         out_specs=[VMEM] * 5,
         scratch_shapes=[
             pltpu.VMEM(colour.shape, colour.dtype),
@@ -223,19 +224,19 @@
         compiler_params=pltpu.CompilerParams(vmem_limit_bytes=LIMIT),
         cost_estimate=pl.CostEstimate(flops=50_000 * 2 * depth * cols * rows, bytes_accessed=64 * 2**20, transcendentals=0),
         name="march_inner",
-    )(*resident, xlo, xhi, *tables)
-
-
-def march_outer(cells, zlo, zhi, xlo, xhi, picks, mid, tab, back):
+    )(wide, *resident, xin, xout, *tables)
+
+
+def march_outer(wide, narrow, cells, zin, zout, xin, xout, picks, mid, tab, back):
     _, depth, cols, rows = picks.shape
     return pl.pallas_call(
         outer_kernel,
         out_shape=pltpu.VMEM((rows // LANES, 4, cols, LANES), jnp.float32),
-        in_specs=[VMEM] * 9,
+        in_specs=[SMEM] * 2 + [VMEM] * 9,
         out_specs=VMEM,
         compiler_params=pltpu.CompilerParams(vmem_limit_bytes=LIMIT),
         name="march_outer",
-    )(cells, zlo, zhi, xlo, xhi, picks, mid, tab, back)
+    )(wide, narrow, cells, zin, zout, xin, xout, picks, mid, tab, back)
 
 
 def join_kernel(parts, back, out):
@@ -260,6 +261,7 @@
 
 
 Z, X, CORES = 8, 4, 2
+PIECES = 4
 
 
 def device(z, x, core):
@@ -276,16 +278,21 @@
 
 
 DOUBLINGS = (
-    pairs(lambda z, x, core: (z, x ^ 2, core) if core else (z ^ 4, x, core)),
-    pairs(lambda z, x, core: (z, x ^ 1, core) if core else (z ^ 2, x, core)),
-    pairs(lambda z, x, core: (z ^ 4, x, core) if core else (z ^ 1, x, core)),
+    pairs(lambda z, x, core: (z ^ 4, x, core)),
+    pairs(lambda z, x, core: (z, x ^ 2, core) if core else (z ^ 2, x, core)),
+    pairs(lambda z, x, core: (z, x ^ 1, core) if core else (z ^ 1, x, core)),
 )
+
+
+def beside(place):
+    return place + 1 if place % 2 else place - 1
+
+
 MOVES = (
-    everywhere(lambda z, x, core: (z + 1, x, core) if core else (z, x + 1, core)),
-    everywhere(lambda z, x, core: (z - 1, x, core) if core else (z, x - 1, core)),
+    everywhere(lambda z, x, core: (z ^ 1, x, core) if core else (z, x ^ 1, core)),
+    everywhere(lambda z, x, core: (beside(z), x, core) if core else (z, beside(x), core)),
     everywhere(lambda z, x, core: (z - 2 if z % 2 else z + 2, x, core) if core else (z, x + 2, core)),
 )
-STEPS = (0, 1, -1, 2)
 SWAP = everywhere(lambda z, x, core: (z, x, 1 - core))
 
 
@@ -296,21 +303,25 @@
 
 
 def place_kernel(swapped, spot, *refs):
-    pieces, out = refs[: len(STEPS)], refs[-1]
-    channel = pl.program_id(0)
+    pieces, out, sem = refs[:PIECES], refs[-2], refs[-1]
     wide = spot[0]
     core = (wide + swapped) % CORES
     x, z = wide // CORES % X, wide // (CORES * X)
-    for piece, step in enumerate(STEPS):
-        x_from, z_from = (x + X - step) % X, (z + Z - step) % (Z // 2)
+    copies = []
+    for piece in range(PIECES):
+        steps = (0, 1 - 2 * (z % 2), 2 * (z % 2) - 1, 2), (0, 1 - 2 * (x % 2), 2 * (x % 2) - 1, 2)
+        z_from, x_from = (z + Z + steps[0][piece]) % (Z // 2), (x + X + steps[1][piece]) % X
         for third in range(2):
             for second in range(2):
                 for first in range(2):
-                    z_zero, x_zero = 4 * first + 2 * second + third, x_from
-                    z_one, x_one = 4 * third + z_from, 2 * first + second
-                    z_now = jnp.where(core == 0, z_zero, z_one)
-                    x_now = jnp.where(core == 0, x_zero, x_one)
-                    out[0, z_now, x_now, 0] = pieces[piece][third, second, first, channel]
+                    z_now = jnp.where(core == 0, 4 * first + 2 * second + third, 4 * first + z_from)
+                    x_now = jnp.where(core == 0, x_from, 2 * second + third)
+                    target = out.at[:, z_now, x_now, core]
+                    copies.append(pltpu.make_async_copy(pieces[piece].at[third, second, first], target, sem))
+    for copy in copies:
+        copy.start()
+    for copy in copies:
+        copy.wait()
 
 
 def place(pieces, spot, swapped, frame=None):
@@ -318,43 +329,41 @@
     kept = [] if frame is None else [frame]
     return pl.pallas_call(
         functools.partial(place_kernel, swapped),
-        grid_spec=pltpu.PrefetchScalarGridSpec(
-            num_scalar_prefetch=1,
-            grid=(channels,),
-            in_specs=[VMEM] * len(pieces) + [ANY] * len(kept),
-            out_specs=pl.BlockSpec(
-                (1, Z, X, 1, cols, rows), lambda channel, spot: (channel, 0, 0, (spot[0] + swapped) % CORES, 0, 0)
-            ),
-        ),
+        in_specs=[SMEM] + [VMEM] * PIECES + [ANY] * len(kept),
+        out_specs=ANY,
         out_shape=jax.ShapeDtypeStruct((channels, Z, X, CORES, cols, rows), jnp.float32),
-        input_output_aliases={1 + len(pieces): 0} if kept else {},
-        compiler_params=pltpu.CompilerParams(vmem_limit_bytes=LIMIT),
+        scratch_shapes=[pltpu.SemaphoreType.DMA],
+        input_output_aliases={1 + PIECES: 0} if kept else {},
+        compiler_params=pltpu.CompilerParams(vmem_limit_bytes=2**20),
         cost_estimate=pl.CostEstimate(flops=0, bytes_accessed=4 * 2**20, transcendentals=0),
         name="place",
     )(spot, *(pltpu.with_memory_space_constraint(piece, pltpu.VMEM) for piece in pieces), *kept)
 
 
-def shifted(value, axis, step, wrap=True):
+def faces(low, high, axis):
+    odd = lax.axis_index(axis) & 1 == 1
+    return jnp.where(odd, low, high), jnp.where(odd, high, low)
+
+
+def change(inner, outer, axis):
     count = lax.axis_size(axis)
-    route = [(i, (i + step) % count) for i in range(count) if wrap or 0 <= i + step < count]
-    return lax.ppermute(value, axis, route)
+    route = [(i, beside(i)) for i in range(count) if 0 <= beside(i) < count]
+    return lax.ppermute(inner, axis, [(i, i ^ 1) for i in range(count)]), lax.ppermute(outer, axis, route)
 
 
 def on_device(fields, field_bins, colour_table, opacity_table, view_dir):
     depth, cols = fields.shape[1:3]
-    left, right, fields_after = lax.optimization_barrier((fields[:, :, :1], fields[:, :, cols - 1 :], fields))
-    xlo = shifted(right, "wide", 1, wrap=False)
-    xhi = shifted(left, "wide", -1, wrap=False)
-    zlo = shifted(fields_after[:, depth - 1 :], "narrow", 1, wrap=False)
-    zhi = shifted(fields_after[:, :1], "narrow", -1, wrap=False)
+    wide, narrow = (lax.axis_index(axis).reshape(1) for axis in ("wide", "narrow"))
+    *columns, fields_after = lax.optimization_barrier((*faces(fields[:, :, :1], fields[:, :, cols - 1 :], "wide"), fields))
+    xin, xout = change(*columns, "wide")
+    zin, zout = change(*faces(fields_after[:, :1], fields_after[:, depth - 1 :], "narrow"), "narrow")
     colour = jnp.transpose(colour_table, (1, 0, 2))
-    cells, picks, mid, tab, back = march_inner(fields, field_bins, xlo, xhi, colour, opacity_table, view_dir)
-    partial = march_outer(cells, zlo, zhi, xlo, xhi, picks, mid, tab, back)
+    cells, picks, mid, tab, back = march_inner(wide, fields, field_bins, xin, xout, colour, opacity_table, view_dir)
+    partial = march_outer(wide, narrow, cells, zin, zout, xin, xout, picks, mid, tab, back)
     partial = lax.all_to_all(partial, "narrow", 0, 0)
     own = gather(join(partial, back))
     other = [lax.ppermute(piece, "wide", SWAP) for piece in own]
-    spot = lax.axis_index("wide").reshape(1)
-    frame = place(other, spot, 1, place(own, spot, 0))
+    frame = place(other, wide, 1, place(own, wide, 0))
     return frame.reshape(frame.shape[0], -1, frame.shape[-1])
 
 

time: 110 us -> 101 us (0.918)
  starting transfers between devices: 49 us -> 41.1 us
  other arithmetic: 0 us -> 2.37 us
  local copies, waits for them, and re-layouts: 2.37 us -> 0.01 us
  Pallas kernels: 14.1 us -> 11.8 us
  waiting for transfers between devices: 0.03 us -> 1.26 us
    ppermute x4, starting transfers between devices: 22.4 us -> 14.8 us  [on_device(): other = [lax.ppermute(piece, 'wide', SWAP) for piece in own]]
    pallas_call x2, Pallas kernels: 5.06 us -> 2.61 us  [place(): pl.pallas_call(functools.partial(place_kernel, swapped), in_specs=[SMEM]...]
    select_n x0 -> x2, other arithmetic: none -> 2.37 us  [faces(): return (jnp.where(odd, low, high), jnp.where(odd, high, low))]
    slice x2 -> x0, local copies, waits for them, and re-layouts: 2.37 us -> none  [the longest x1 1.3 us: on_device(): fields[:, :, cols - 1:]]
    ppermute x4, starting transfers between devices: 15.4 us -> 13.3 us  [the longest x2 10.7 us: change(): lax.ppermute(inner, axis, [(i, i ^ 1) for i in range(count)])]
    ppermute x3, starting transfers between devices: 11.3 us -> 13.1 us  [gather(): return [block] + [lax.ppermute(block, 'wide', move) for move in MOVES]]
  transfers between devices with their start and end apart: 11 -> 11, of which waited for: 0 -> 3; matrix products, arithmetic and copies ran while one was open for 1% -> 1% of each run, Pallas kernels for 8% -> 8%
where the time goes in v5:
time: 101 us; the launch traced here: 100 us
  blocking collectives  43.3 us (43%)
  starting transfers between devices  41.1 us (41%)
  Pallas kernels  11.8 us (12%)
  other arithmetic  2.37 us (2%)
  waiting for transfers between devices  1.26 us (1%)
    all_gather x3, blocking collectives, gather(): block = lax.all_gather(block, 'wide', axis_index_groups=groups)  22.5 us
    all_to_all x1, blocking collectives, on_device(): partial = lax.all_to_all(partial, 'narrow', 0, 0)  20.8 us
    ppermute x4, starting transfers between devices, on_device(): other = [lax.ppermute(piece, 'wide', SWAP) for piece in own]  14.8 us
    ppermute x3, starting transfers between devices, gather(): return [block] + [lax.ppermute(block, 'wide', move) for move in MOVES]  13.1 us
    ppermute x2, starting transfers between devices, change(): lax.ppermute(inner, axis, [(i, i ^ 1) for i in range(count)])  10.7 us
    pallas_call x1, Pallas kernels, march_inner(): pl.pallas_call(inner_kernel, out_shape=[pltpu.VMEM((2, depth, cols, rows...  6.88 us
    pallas_call x2, Pallas kernels, place(): pl.pallas_call(functools.partial(place_kernel, swapped), in_specs=[SMEM]...  2.61 us
    ppermute x2, starting transfers between devices, change(): lax.ppermute(outer, axis, route)  2.6 us
  transfers between devices with their start and end apart: 11, of which 3 were waited for; matrix products, arithmetic and copies ran while one was open for 1% of the time, Pallas kernels for 8%

profile of v5, /device:TPU:1, one launch (start us, length us, event | category | flops | bytes accessed | tf_op | source)
XLA Modules:
  0.0 100.1 jit_solution(11046527126857086203)
XLA Ops:
  0.0 1.3 %broadcast_select_fusion = (f32[2,8,1,1024]{3,2,1,0:T(1,128)S(1)}, f32[2,8,1,1024]{3,2,1,0:T(1,128)S(1)}) fusion(pred[]{:T(512)S(6)} %eq.6, f32[2,8,32,1024]{3,2,1,0:T(8,128)} %fields.1), kind=kLoop, calls=%fused_computation.2 | loop fusion | flops 32768 | bytes 262145 | tf_op jit(solution)/shard_map/jit(_where)/select_n | solution.py:345
  1.3 8.8 %collective-permute-start = (f32[2,8,1,1024]{3,2,1,0:T(1,128)S(1)}, f32[2,8,1,1024]{3,2,1,0:T(1,128)S(1)}, u32[]{:S(2)}, u32[]{:S(2)}) collective-permute-start(f32[2,8,1,1024]{3,2,1,0:T(1,128)S(1)} %get-tuple-element.13), channel_id=1, source_target_pairs={{0,8},{8,0},{16,24},{24,16},{32,40},{40,32},{48,56},{56,48},{64,72... | collective-permute-start | bytes 196616 | tf_op jit(solution)/shard_map/ppermute | solution.py:351
  10.1 1.9 %collective-permute-start.1 = (f32[2,8,1,1024]{3,2,1,0:T(1,128)S(1)}, f32[2,8,1,1024]{3,2,1,0:T(1,128)S(1)}, u32[]{:S(2)}, u32[]{:S(2)}) collective-permute-start(f32[2,8,1,1024]{3,2,1,0:T(1,128)S(1)} %get-tuple-element.14), channel_id=1, source_target_pairs={{8,16},{16,8},{24,32},{32,24},{40,48},{48,40},{56,64},{64,56},{72,... | collective-permute-start | bytes 196616 | tf_op jit(solution)/shard_map/ppermute | solution.py:351
  12.0 1.1 %slice_select_fusion = (f32[2,1,32,1024]{3,2,1,0:T(8,128)S(1)}, f32[2,1,32,1024]{3,2,1,0:T(8,128)S(1)}) fusion(f32[2,8,32,1024]{3,2,1,0:T(8,128)} %fields.1, pred[]{:T(512)S(6)} %eq.7), kind=kLoop, calls=%fused_computation | loop fusion | flops 131072 | bytes 1048577 | tf_op jit(solution)/shard_map/jit(_where)/select_n | solution.py:345
  13.1 0.7 collective-permute-start.3
  13.8 1.9 %collective-permute-start.2 = (f32[2,1,32,1024]{3,2,1,0:T(8,128)S(1)}, f32[2,1,32,1024]{3,2,1,0:T(8,128)S(1)}, u32[]{:S(2)}, u32[]{:S(2)}) collective-permute-start(f32[2,1,32,1024]{3,2,1,0:T(8,128)S(1)} %get-tuple-element.22), channel_id=1, source_target_pairs={{0,1},{1,0},{2,3},{3,2},{4,5},{5,4},{6,7},{7,6},{8,9},{9,8},{10,11... | collective-permute-start | bytes 786440 | tf_op jit(solution)/shard_map/ppermute | solution.py:351
  15.7 0.0 collective-permute-done.xin
  15.7 0.0 collective-permute-done.1.xout
  15.7 6.9 %march_inner.1 = (f32[2,8,32,1280]{3,2,1,0:T(8,128)S(1)}, s32[2,8,32,1024]{3,2,1,0:T(8,128)S(1)}, f32[8,4,32,128]{3,2,1,0:T(8,128)S(1)}, s32[2,2,2,8,128]{4,3,2,1,0:T(8,128)S(1)}, s32[32,128]{1,0:T(8,128)S(1)}) custom-call(s32[1]{0:T(128)} %bitcast.wide.spot, f32[2,8,32,1024]{3,2,1,0:T(8,128)} %fields.1, s32[2,8,32,1024]{3,2,1,0:T(8,128)} %bins.1, ...), custom_call_target="tpu_custom_call" | custom-call | flops 26214400000 | bytes 67108864 | tf_op jit(solution)/shard_map/march_inner/pallas_call | solution.py:205
  22.6 0.0 copy-start
  22.7 0.0 collective-permute-done.3.zout
  22.7 0.3 collective-permute-done.2.zin
  22.9 1.5 %march_outer.1 = f32[8,4,32,128]{3,2,1,0:T(8,128)S(1)} custom-call(s32[1]{0:T(128)} %bitcast.wide.spot, s32[1]{0:T(128)} %bitcast.1.narrow, f32[2,8,32,1280]{3,2,1,0:T(8,128)S(1)} %get-tuple-element.15.cells, f32[2,1,32,1024]{3,2,1,0:T(8,128)S(1)} %collective-permute-done.2.zin, f32[2,1,32,1024]{3,2,1,0:T(8,128)S(1)} %collective-permute-done.3.zout, ...), custom_call_target="tpu_custom_call" | custom-call | tf_op jit(solution)/shard_map/march_outer/pallas_call | solution.py:232
  24.4 0.0 copy-done
  24.5 20.8 %all_to_all.5.parts = f32[8,4,32,128]{3,2,1,0:T(8,128)S(1)} all-to-all(f32[8,4,32,128]{3,2,1,0:T(8,128)S(1)} %march_outer.1), channel_id=1, replica_groups=mesh['wide'=64,'narrow'=8] {'narrow'}, dimensions={0} | all-to-all | bytes 1048576 | tf_op jit(solution)/shard_map/all_to_all | solution.py:363
  45.3 0.8 join.1
  46.0 9.4 %all-gather = f32[8,32,128]{2,1,0:T(8,128)S(1)} all-gather(f32[4,32,128]{2,1,0:T(8,128)S(1)} %join.1), channel_id=2, replica_groups={{0,256},{8,264},{16,272},{24,280},{32,288},{40,296},{48,304},{56,312},{..., dimensions={0}, use_global_device_ids=true | all-gather | bytes 196608 | tf_op jit(solution)/shard_map/all_gather | solution.py:301
  55.5 6.5 %all-gather.1 = f32[4,4,32,128]{3,2,1,0:T(8,128)S(1)} all-gather(f32[2,4,32,128]{3,2,1,0:T(8,128)S(1)} %bitcast.13), channel_id=3, replica_groups={{0,128},{8,40},{16,144},{24,56},{32,160},{48,176},{64,192},{72,104},{80..., dimensions={0}, use_global_device_ids=true | all-gather | bytes 393216 | tf_op jit(solution)/shard_map/all_gather | solution.py:301
  62.0 6.6 %all-gather.2 = f32[4,2,4,32,128]{4,3,2,1,0:T(8,128)S(1)} all-gather(f32[2,2,4,32,128]{4,3,2,1,0:T(8,128)S(1)} %bitcast.12), channel_id=4, replica_groups={{0,64},{8,24},{16,80},{32,96},{40,56},{48,112},{72,88},{104,120},{128,1..., dimensions={0}, use_global_device_ids=true | all-gather | bytes 786432 | tf_op jit(solution)/shard_map/all_gather | solution.py:301
  68.6 4.7 %collective-permute-start.9 = (f32[2,2,2,4,32,128]{5,4,3,2,1,0:T(8,128)S(1)}, f32[2,2,2,4,32,128]{5,4,3,2,1,0:T(8,128)S(1)}, u32[]{:S(2)}, u32[]{:S(2)}) collective-permute-start(f32[2,2,2,4,32,128]{5,4,3,2,1,0:T(8,128)S(1)} %bitcast.7), channel_id=1, source_target_pairs={{0,32},{8,136},{16,48},{24,152},{32,0},{40,168},{48,16},{56,184},{... | collective-permute-start | bytes 1572872 | tf_op jit(solution)/shard_map/ppermute | solution.py:302
  73.3 5.3 %collective-permute-start.7 = (f32[2,2,2,4,32,128]{5,4,3,2,1,0:T(8,128)S(1)}, f32[2,2,2,4,32,128]{5,4,3,2,1,0:T(8,128)S(1)}, u32[]{:S(2)}, u32[]{:S(2)}) collective-permute-start(f32[2,2,2,4,32,128]{5,4,3,2,1,0:T(8,128)S(1)} %bitcast.8), channel_id=1, source_target_pairs={{0,48},{8,456},{16,32},{24,472},{32,16},{40,488},{48,0},{56,504},{... | collective-permute-start | bytes 1572872 | tf_op jit(solution)/shard_map/ppermute | solution.py:302
  78.6 3.1 %collective-permute-start.5 = (f32[2,2,2,4,32,128]{5,4,3,2,1,0:T(8,128)S(1)}, f32[2,2,2,4,32,128]{5,4,3,2,1,0:T(8,128)S(1)}, u32[]{:S(2)}, u32[]{:S(2)}) collective-permute-start(f32[2,2,2,4,32,128]{5,4,3,2,1,0:T(8,128)S(1)} %bitcast.9), channel_id=1, source_target_pairs={{0,16},{8,72},{16,0},{24,88},{32,48},{40,104},{48,32},{56,120},{64... | collective-permute-start | bytes 1572872 | tf_op jit(solution)/shard_map/ppermute | solution.py:302
  81.7 5.6 %collective-permute-start.4 = (f32[2,2,2,4,32,128]{5,4,3,2,1,0:T(8,128)S(1)}, f32[2,2,2,4,32,128]{5,4,3,2,1,0:T(8,128)S(1)}, u32[]{:S(2)}, u32[]{:S(2)}) collective-permute-start(f32[2,2,2,4,32,128]{5,4,3,2,1,0:T(8,128)S(1)} %bitcast.10), channel_id=1, source_target_pairs={{0,8},{8,0},{16,24},{24,16},{32,40},{40,32},{48,56},{56,48},{64,72... | collective-permute-start | bytes 1572872 | tf_op jit(solution)/shard_map/ppermute | solution.py:365
  87.3 0.0 collective-permute-done.9.refs_3_
  87.3 2.2 %collective-permute-start.10 = (f32[2,2,2,4,32,128]{5,4,3,2,1,0:T(8,128)S(1)}, f32[2,2,2,4,32,128]{5,4,3,2,1,0:T(8,128)S(1)}, u32[]{:S(2)}, u32[]{:S(2)}) collective-permute-start(f32[2,2,2,4,32,128]{5,4,3,2,1,0:T(8,128)S(1)} %collective-permute-done.9.refs_3_), channel_id=1, source_target_pairs={{0,8},{8,0},{16,24},{24,16},{32,40},{40,32},{48,56},{56,48},{64,72... | collective-permute-start | bytes 1572872 | tf_op jit(solution)/shard_map/ppermute | solution.py:365
  89.5 0.4 collective-permute-done.7.refs_2_
  89.9 5.1 %collective-permute-start.8 = (f32[2,2,2,4,32,128]{5,4,3,2,1,0:T(8,128)S(1)}, f32[2,2,2,4,32,128]{5,4,3,2,1,0:T(8,128)S(1)}, u32[]{:S(2)}, u32[]{:S(2)}) collective-permute-start(f32[2,2,2,4,32,128]{5,4,3,2,1,0:T(8,128)S(1)} %collective-permute-done.7.refs_2_), channel_id=1, source_target_pairs={{0,8},{8,0},{16,24},{24,16},{32,40},{40,32},{48,56},{56,48},{64,72... | collective-permute-start | bytes 1572872 | tf_op jit(solution)/shard_map/ppermute | solution.py:365
  95.0 0.0 collective-permute-done.5.refs_1_
  95.0 1.9 %collective-permute-start.6 = (f32[2,2,2,4,32,128]{5,4,3,2,1,0:T(8,128)S(1)}, f32[2,2,2,4,32,128]{5,4,3,2,1,0:T(8,128)S(1)}, u32[]{:S(2)}, u32[]{:S(2)}) collective-permute-start(f32[2,2,2,4,32,128]{5,4,3,2,1,0:T(8,128)S(1)} %collective-permute-done.5.refs_1_), channel_id=1, source_target_pairs={{0,8},{8,0},{16,24},{24,16},{32,40},{40,32},{48,56},{56,48},{64,72... | collective-permute-start | bytes 1572872 | tf_op jit(solution)/shard_map/ppermute | solution.py:365
  96.9 1.3 %place.2.refs_4_ = f32[4,8,4,2,32,128]{5,4,3,2,1,0:T(8,128)} custom-call(s32[1]{0:T(128)} %bitcast.wide.spot, f32[2,2,2,4,32,128]{5,4,3,2,1,0:T(8,128)S(1)} %bitcast.11, f32[2,2,2,4,32,128]{5,4,3,2,1,0:T(8,128)S(1)} %collective-permute-done.5.refs_1_, f32[2,2,2,4,32,128]{5,4,3,2,1,0:T(8,128)S(1)} %collective-permute-done.7.refs_2_, ...), custom_call_target="tpu_custom_call" | custom-call | bytes 4194304 | tf_op jit(solution)/shard_map/place/pallas_call | solution.py:330
  98.3 0.0 collective-permute-done.4.refs_0_
  98.3 0.0 collective-permute-done.10.refs_3_
  98.3 0.0 collective-permute-done.8.refs_2_
  98.3 0.5 collective-permute-done.6.refs_1_
  98.8 1.3 %place.3 = f32[4,8,4,2,32,128]{5,4,3,2,1,0:T(8,128)} custom-call(s32[1]{0:T(128)} %bitcast.wide.spot, f32[2,2,2,4,32,128]{5,4,3,2,1,0:T(8,128)S(1)} %collective-permute-done.4.refs_0_, f32[2,2,2,4,32,128]{5,4,3,2,1,0:T(8,128)S(1)} %collective-permute-done.6.refs_1_, ...), custom_call_target="tpu_custom_call", output_to_operand_aliasing={{}: (5, {})} | custom-call | bytes 4194304 | tf_op jit(solution)/shard_map/place/pallas_call | solution.py:330
Async XLA Ops:
  1.3 14.4 %collective-permute-start = (f32[2,8,1,1024]{3,2,1,0:T(1,128)S(1)}, f32[2,8,1,1024]{3,2,1,0:T(1,128)S(1)}, u32[]{:S(2)}, u32[]{:S(2)}) collective-permute-start(f32[2,8,1,1024]{3,2,1,0:T(1,128)S(1)} %get-tuple-element.13), channel_id=1, source_target_pairs={{0,8},{8,0},{16,24},{24,16},{32,40},{40,32},{48,56},{56,48},{64,72... | collective-permute-start | bytes 196616 | tf_op jit(solution)/shard_map/ppermute | solution.py:351
  10.1 5.6 %collective-permute-start.1 = (f32[2,8,1,1024]{3,2,1,0:T(1,128)S(1)}, f32[2,8,1,1024]{3,2,1,0:T(1,128)S(1)}, u32[]{:S(2)}, u32[]{:S(2)}) collective-permute-start(f32[2,8,1,1024]{3,2,1,0:T(1,128)S(1)} %get-tuple-element.14), channel_id=1, source_target_pairs={{8,16},{16,8},{24,32},{32,24},{40,48},{48,40},{56,64},{64,56},{72,... | collective-permute-start | bytes 196616 | tf_op jit(solution)/shard_map/ppermute | solution.py:351
  13.1 9.5 %collective-permute-start.3 = (f32[2,1,32,1024]{3,2,1,0:T(8,128)S(1)}, f32[2,1,32,1024]{3,2,1,0:T(8,128)S(1)}, u32[]{:S(2)}, u32[]{:S(2)}) collective-permute-start(f32[2,1,32,1024]{3,2,1,0:T(8,128)S(1)} %get-tuple-element.21), channel_id=1, source_target_pairs={{1,2},{2,1},{3,4},{4,3},{5,6},{6,5},{9,10},{10,9},{11,12},{12,11},... | collective-permute-start | bytes 786440 | tf_op jit(solution)/shard_map/ppermute | solution.py:351
  13.8 9.1 %collective-permute-start.2 = (f32[2,1,32,1024]{3,2,1,0:T(8,128)S(1)}, f32[2,1,32,1024]{3,2,1,0:T(8,128)S(1)}, u32[]{:S(2)}, u32[]{:S(2)}) collective-permute-start(f32[2,1,32,1024]{3,2,1,0:T(8,128)S(1)} %get-tuple-element.22), channel_id=1, source_target_pairs={{0,1},{1,0},{2,3},{3,2},{4,5},{5,4},{6,7},{7,6},{8,9},{9,8},{10,11... | collective-permute-start | bytes 786440 | tf_op jit(solution)/shard_map/ppermute | solution.py:351
  22.6 1.8 %copy-start = (s32[32,128]{1,0:T(8,128)}, s32[32,128]{1,0:T(8,128)S(1)}, u32[]{:S(2)}) copy-start(s32[32,128]{1,0:T(8,128)S(1)} %get-tuple-element.20.back) | copy-start | bytes 49156
  68.6 18.7 %collective-permute-start.9 = (f32[2,2,2,4,32,128]{5,4,3,2,1,0:T(8,128)S(1)}, f32[2,2,2,4,32,128]{5,4,3,2,1,0:T(8,128)S(1)}, u32[]{:S(2)}, u32[]{:S(2)}) collective-permute-start(f32[2,2,2,4,32,128]{5,4,3,2,1,0:T(8,128)S(1)} %bitcast.7), channel_id=1, source_target_pairs={{0,32},{8,136},{16,48},{24,152},{32,0},{40,168},{48,16},{56,184},{... | collective-permute-start | bytes 1572872 | tf_op jit(solution)/shard_map/ppermute | solution.py:302
  73.3 16.6 %collective-permute-start.7 = (f32[2,2,2,4,32,128]{5,4,3,2,1,0:T(8,128)S(1)}, f32[2,2,2,4,32,128]{5,4,3,2,1,0:T(8,128)S(1)}, u32[]{:S(2)}, u32[]{:S(2)}) collective-permute-start(f32[2,2,2,4,32,128]{5,4,3,2,1,0:T(8,128)S(1)} %bitcast.8), channel_id=1, source_target_pairs={{0,48},{8,456},{16,32},{24,472},{32,16},{40,488},{48,0},{56,504},{... | collective-permute-start | bytes 1572872 | tf_op jit(solution)/shard_map/ppermute | solution.py:302
  78.6 16.4 %collective-permute-start.5 = (f32[2,2,2,4,32,128]{5,4,3,2,1,0:T(8,128)S(1)}, f32[2,2,2,4,32,128]{5,4,3,2,1,0:T(8,128)S(1)}, u32[]{:S(2)}, u32[]{:S(2)}) collective-permute-start(f32[2,2,2,4,32,128]{5,4,3,2,1,0:T(8,128)S(1)} %bitcast.9), channel_id=1, source_target_pairs={{0,16},{8,72},{16,0},{24,88},{32,48},{40,104},{48,32},{56,120},{64... | collective-permute-start | bytes 1572872 | tf_op jit(solution)/shard_map/ppermute | solution.py:302
  81.7 16.6 %collective-permute-start.4 = (f32[2,2,2,4,32,128]{5,4,3,2,1,0:T(8,128)S(1)}, f32[2,2,2,4,32,128]{5,4,3,2,1,0:T(8,128)S(1)}, u32[]{:S(2)}, u32[]{:S(2)}) collective-permute-start(f32[2,2,2,4,32,128]{5,4,3,2,1,0:T(8,128)S(1)} %bitcast.10), channel_id=1, source_target_pairs={{0,8},{8,0},{16,24},{24,16},{32,40},{40,32},{48,56},{56,48},{64,72... | collective-permute-start | bytes 1572872 | tf_op jit(solution)/shard_map/ppermute | solution.py:365
  87.3 11.0 %collective-permute-start.10 = (f32[2,2,2,4,32,128]{5,4,3,2,1,0:T(8,128)S(1)}, f32[2,2,2,4,32,128]{5,4,3,2,1,0:T(8,128)S(1)}, u32[]{:S(2)}, u32[]{:S(2)}) collective-permute-start(f32[2,2,2,4,32,128]{5,4,3,2,1,0:T(8,128)S(1)} %collective-permute-done.9.refs_3_), channel_id=1, source_target_pairs={{0,8},{8,0},{16,24},{24,16},{32,40},{40,32},{48,56},{56,48},{64,72... | collective-permute-start | bytes 1572872 | tf_op jit(solution)/shard_map/ppermute | solution.py:365
  89.9 8.4 %collective-permute-start.8 = (f32[2,2,2,4,32,128]{5,4,3,2,1,0:T(8,128)S(1)}, f32[2,2,2,4,32,128]{5,4,3,2,1,0:T(8,128)S(1)}, u32[]{:S(2)}, u32[]{:S(2)}) collective-permute-start(f32[2,2,2,4,32,128]{5,4,3,2,1,0:T(8,128)S(1)} %collective-permute-done.7.refs_2_), channel_id=1, source_target_pairs={{0,8},{8,0},{16,24},{24,16},{32,40},{40,32},{48,56},{56,48},{64,72... | collective-permute-start | bytes 1572872 | tf_op jit(solution)/shard_map/ppermute | solution.py:365
  95.0 3.8 %collective-permute-start.6 = (f32[2,2,2,4,32,128]{5,4,3,2,1,0:T(8,128)S(1)}, f32[2,2,2,4,32,128]{5,4,3,2,1,0:T(8,128)S(1)}, u32[]{:S(2)}, u32[]{:S(2)}) collective-permute-start(f32[2,2,2,4,32,128]{5,4,3,2,1,0:T(8,128)S(1)} %collective-permute-done.5.refs_1_), channel_id=1, source_target_pairs={{0,8},{8,0},{16,24},{24,16},{32,40},{40,32},{48,56},{56,48},{64,72... | collective-permute-start | bytes 1572872 | tf_op jit(solution)/shard_map/ppermute | solution.py:365

commit v6 on v5

--- a/solution.py
+++ b/solution.py
@@ -102,33 +102,22 @@
     return at
 
 
-def inner_kernel(
-    wide, fields, bins, xin, xout, colour, opacity, view, cells, picks, mid, tab, back, colour_now, opacity_now, view_now, field_sem, bin_sem, tab_sem
+def load_kernel(
+    wide, narrow, fields, colour, opacity, view, cells, xin, xout, zin, zout, tab, back, colour_now, opacity_now, view_now, field_sem, tab_sem
 ):
     depth, cols, rows = fields.shape[1:]
-    groups, half = cols // SUBS, rows // 2
     small = [
         pltpu.make_async_copy(source, target, tab_sem.at[n])
         for n, (source, target) in enumerate(((colour, colour_now), (opacity, opacity_now), (view, view_now)))
     ]
-    parts = (pl.ds(0, half + LANES), pl.ds(half + LANES, half - LANES))
-    field_copies, bin_copies = {}, {}
-    for g in range(groups):
-        span = pl.ds(g * SUBS, SUBS)
-        for h, part in enumerate(parts):
-            target = cells.at[:, :, span, pl.ds(LANES + part.start, part.size)]
-            field_copies[g, h] = pltpu.make_async_copy(fields.at[:, :, span, part], target, field_sem.at[g, h])
-            part = pl.ds(h * half, half)
-            bin_copies[g, h] = pltpu.make_async_copy(bins.at[:, :, span, part], picks.at[:, :, span, part], bin_sem.at[g, h])
     for copy in small:
         copy.start()
-    for g in range(groups):
-        for h in range(2):
-            if g == 0:
-                field_copies[g, h].start()
-            if g + 1 < groups:
-                field_copies[g + 1, h].start()
-            bin_copies[g, h].start()
+    ends = (0, depth - 1)
+    order = ends + tuple(range(1, depth - 1))
+    copies = {}
+    for d in order:
+        copies[d] = pltpu.make_async_copy(fields.at[:, d], cells.at[:, d, :, pl.ds(LANES, rows)], field_sem.at[d])
+        copies[d].start()
     zero = jnp.zeros((cols, LANES), jnp.float32)
     for f in range(2):
         for d in range(depth):
@@ -137,59 +126,88 @@
     for copy in small:
         copy.wait()
     sub = lax.broadcasted_iota(jnp.int32, (SUBS, LANES), 0)
-    for g in range(groups):
+    for g in range(cols // SUBS):
         towards = jnp.zeros((SUBS, LANES), jnp.int32)
         for k in range(SUBS):
             towards = jnp.where(sub == k, view_now[g * SUBS + k], towards)
         back[g * SUBS : (g + 1) * SUBS, :] = towards
     store_tables(colour_now, opacity_now, tab)
+    x_odd, z_odd = wide[0] % 2 == 1, narrow[0] % 2 == 1
+    inside = slice(LANES, LANES + rows)
+    for n, d in enumerate(order):
+        copies[d].wait()
+        for f in range(2):
+            low, high = cells[f, d, 0:1, inside], cells[f, d, cols - 1 : cols, inside]
+            xin[f, d] = jnp.where(x_odd, low, high)
+            xout[f, d] = jnp.where(x_odd, high, low)
+            if n == 1:
+                low, high = (cells[f, end, :, inside] for end in ends)
+                zin[f, 0] = jnp.where(z_odd, low, high)
+                zout[f, 0] = jnp.where(z_odd, high, low)
+
+
+def inner_kernel(bins, cells, tab, back, picks, mid, bin_sem):
+    depth, cols, rows = bins.shape[1:]
+    groups, half = cols // SUBS, rows // 2
+    bin_copies = {}
+    inner = range(1, groups - 1)
+    for g in (*inner, 0, groups - 1):
+        for h in range(2):
+            part = pl.ds(g * SUBS, SUBS), pl.ds(h * half, half)
+            bin_copies[g, h] = pltpu.make_async_copy(bins.at[:, :, *part], picks.at[:, :, *part], bin_sem.at[g, h])
+            bin_copies[g, h].start()
     edges = masks()
+    for g in inner:
+        backward = back[g * SUBS : (g + 1) * SUBS, :] == 1
+
+        def tile(b, carry, g=g, backward=backward):
+            start = pl.multiple_of(b * LANES, LANES)
+            at = lattice(cells, None, None, None, g, start)
+
+            def element(d):
+                return cell(at, lambda f: picks[f, d, pl.ds(g * SUBS, SUBS), pl.ds(start, LANES)], d, tab, edges)
+
+            colours, through = composite((element(d) for d in range(1, depth - 1)), backward)
+            for k, value in enumerate(colours + [through]):
+                mid[b, k, pl.ds((g - 1) * SUBS, SUBS), :] = value
+            return carry
+
+        for h in range(2):
+            bin_copies[g, h].wait()
+            lax.fori_loop(h * half // LANES, (h + 1) * half // LANES, tile, 0, unroll=4)
+    for g in (0, groups - 1):
+        for h in range(2):
+            bin_copies[g, h].wait()
+
+
+def outer_kernel(wide, narrow, cells, zin, zout, xin, xout, picks, mid, tab, back, out):
+    depth, cols, rows = picks.shape[1:]
+    groups = cols // SUBS
+    edges = masks()
+    odd = wide[0] % 2 == 1, narrow[0] % 2 == 1
     for g in range(groups):
         backward = back[g * SUBS : (g + 1) * SUBS, :] == 1
-
-        def tile(b, carry, g=g, backward=backward):
+        inside = 0 < g < groups - 1
+
+        def tile(b, carry, g=g, backward=backward, inside=inside):
             start = pl.multiple_of(b * LANES, LANES)
-            at = lattice(cells, (xin, xout), None, (wide[0] % 2 == 1, None), g, start)
+            at = lattice(cells, (xin, xout), (zin, zout), odd, g, start)
 
             def element(d):
                 return cell(at, lambda f: picks[f, d, pl.ds(g * SUBS, SUBS), pl.ds(start, LANES)], d, tab, edges)
 
-            colours, through = composite((element(d) for d in range(1, depth - 1)), backward)
-            for k, value in enumerate(colours + [through]):
-                mid[b, k, pl.ds(g * SUBS, SUBS), :] = value
-            return carry
-
-        for h in range(2):
-            if g == 0:
-                field_copies[g, h].wait()
-            if g + 1 < groups:
-                field_copies[g + 1, h].wait()
-            bin_copies[g, h].wait()
-            lax.fori_loop(h * half // LANES, (h + 1) * half // LANES, tile, 0, unroll=4)
-
-
-def outer_kernel(wide, narrow, cells, zin, zout, xin, xout, picks, mid, tab, back, out):
-    depth, cols, rows = picks.shape[1:]
-    edges = masks()
-    for g in range(cols // SUBS):
-        backward = back[g * SUBS : (g + 1) * SUBS, :] == 1
-
-        def tile(b, carry, g=g, backward=backward):
-            start = pl.multiple_of(b * LANES, LANES)
-            at = lattice(cells, (xin, xout), (zin, zout), (wide[0] % 2 == 1, narrow[0] % 2 == 1), g, start)
-
-            def element(d):
-                return cell(at, lambda f: picks[f, d, pl.ds(g * SUBS, SUBS), pl.ds(start, LANES)], d, tab, edges)
-
-            middle = [mid[b, k, pl.ds(g * SUBS, SUBS), :] for k in range(4)]
-            elements = [element(0), (middle[:3], middle[3]), element(depth - 1)]
-            parts, through = composite(elements, backward)
-            for k, part in enumerate(parts):
-                out[b, k, pl.ds(g * SUBS, SUBS), :] = part * COLOUR_UNIT
+            if inside:
+                middle = [mid[b, k, pl.ds((g - 1) * SUBS, SUBS), :] for k in range(4)]
+                elements = [element(0), (middle[:3], middle[3]), element(depth - 1)]
+            else:
+                elements = (element(d) for d in range(depth))
+            colours, through = composite(elements, backward)
+            for k, value in enumerate(colours):
+                out[b, k, pl.ds(g * SUBS, SUBS), :] = value * COLOUR_UNIT
             out[b, 3, pl.ds(g * SUBS, SUBS), :] = 1.0 - through
             return carry
 
-        lax.fori_loop(0, rows // LANES, tile, 0, unroll=8)
+        lax.fori_loop(0, rows // LANES, tile, 0, unroll=8 if inside else 4)
 
 
 VMEM = pl.BlockSpec(memory_space=pltpu.VMEM)
@@ -198,33 +216,49 @@
 LIMIT = 24 * 2**20
 
 
-def march_inner(wide, fields, bins, xin, xout, colour, opacity, view):
+def load(wide, narrow, fields, colour, opacity, view):
     _, depth, cols, rows = fields.shape
-    resident = [pltpu.with_memory_space_constraint(x, pltpu.HBM) for x in (fields, bins)]
-    tables = [pltpu.with_memory_space_constraint(x, pltpu.HBM) for x in (colour, opacity, view)]
+    fields, colour, opacity, view = (pltpu.with_memory_space_constraint(x, pltpu.HBM) for x in (fields, colour, opacity, view))
     return pl.pallas_call(
-        inner_kernel,
+        load_kernel,
         out_shape=[
             pltpu.VMEM((2, depth, cols, rows + 2 * LANES), jnp.float32),
-            pltpu.VMEM((2, depth, cols, rows), jnp.int32),
-            pltpu.VMEM((rows // LANES, 4, cols, LANES), jnp.float32),
+            pltpu.VMEM((2, depth, 1, rows), jnp.float32),
+            pltpu.VMEM((2, depth, 1, rows), jnp.float32),
+            pltpu.VMEM((2, 1, cols, rows), jnp.float32),
+            pltpu.VMEM((2, 1, cols, rows), jnp.float32),
             pltpu.VMEM((2, 2, 2, SUBS, LANES), jnp.int32),
             pltpu.VMEM((cols, LANES), jnp.int32),
         ],
-        in_specs=[SMEM, ANY, ANY, VMEM, VMEM, ANY, ANY, ANY],
-        out_specs=[VMEM] * 5,
+        in_specs=[SMEM, SMEM, ANY, ANY, ANY, ANY],
+        out_specs=[VMEM] * 7,
         scratch_shapes=[
             pltpu.VMEM(colour.shape, colour.dtype),
             pltpu.VMEM(opacity.shape, opacity.dtype),
             pltpu.SMEM(view.shape, view.dtype),
-            pltpu.SemaphoreType.DMA((cols // SUBS, 2)),
-            pltpu.SemaphoreType.DMA((cols // SUBS, 2)),
+            pltpu.SemaphoreType.DMA((depth,)),
             pltpu.SemaphoreType.DMA((3,)),
         ],
         compiler_params=pltpu.CompilerParams(vmem_limit_bytes=LIMIT),
-        cost_estimate=pl.CostEstimate(flops=50_000 * 2 * depth * cols * rows, bytes_accessed=64 * 2**20, transcendentals=0),
+        name="load",
+    )(wide, narrow, fields, colour, opacity, view)
+
+
+def march_inner(bins, cells, tab, back):
+    _, depth, cols, rows = bins.shape
+    return pl.pallas_call(
+        inner_kernel,
+        out_shape=[
+            pltpu.VMEM((2, depth, cols, rows), jnp.int32),
+            pltpu.VMEM((rows // LANES, 4, cols - 2 * SUBS, LANES), jnp.float32),
+        ],
+        in_specs=[ANY, VMEM, VMEM, VMEM],
+        out_specs=[VMEM] * 2,
+        scratch_shapes=[pltpu.SemaphoreType.DMA((cols // SUBS, 2))],
+        compiler_params=pltpu.CompilerParams(vmem_limit_bytes=LIMIT),
+        cost_estimate=pl.CostEstimate(flops=100 * 2 * depth * cols * rows, bytes_accessed=8 * 2**20, transcendentals=0),
         name="march_inner",
-    )(wide, *resident, xin, xout, *tables)
+    )(pltpu.with_memory_space_constraint(bins, pltpu.HBM), cells, tab, back)
 
 
 def march_outer(wide, narrow, cells, zin, zout, xin, xout, picks, mid, tab, back):
@@ -340,11 +374,6 @@
     )(spot, *(pltpu.with_memory_space_constraint(piece, pltpu.VMEM) for piece in pieces), *kept)
 
 
-def faces(low, high, axis):
-    odd = lax.axis_index(axis) & 1 == 1
-    return jnp.where(odd, low, high), jnp.where(odd, high, low)
-
-
 def change(inner, outer, axis):
     count = lax.axis_size(axis)
     route = [(i, beside(i)) for i in range(count) if 0 <= beside(i) < count]
@@ -352,13 +381,12 @@
 
 
 def on_device(fields, field_bins, colour_table, opacity_table, view_dir):
-    depth, cols = fields.shape[1:3]
     wide, narrow = (lax.axis_index(axis).reshape(1) for axis in ("wide", "narrow"))
-    *columns, fields_after = lax.optimization_barrier((*faces(fields[:, :, :1], fields[:, :, cols - 1 :], "wide"), fields))
-    xin, xout = change(*columns, "wide")
-    zin, zout = change(*faces(fields_after[:, :1], fields_after[:, depth - 1 :], "narrow"), "narrow")
     colour = jnp.transpose(colour_table, (1, 0, 2))
-    cells, picks, mid, tab, back = march_inner(wide, fields, field_bins, xin, xout, colour, opacity_table, view_dir)
+    cells, *faces, tab, back = load(wide, narrow, fields, colour, opacity_table, view_dir)
+    zin, zout = change(*faces[2:], "narrow")
+    xin, xout = change(*faces[:2], "wide")
+    picks, mid = march_inner(field_bins, cells, tab, back)
     partial = march_outer(wide, narrow, cells, zin, zout, xin, xout, picks, mid, tab, back)
     partial = lax.all_to_all(partial, "narrow", 0, 0)
     own = gather(join(partial, back))

time: 101 us -> 99.3 us (0.983)
  starting transfers between devices: 41.1 us -> 37.1 us
  blocking collectives: 43.3 us -> 45.7 us
  other arithmetic: 2.37 us -> 0 us
  waiting for transfers between devices: 1.26 us -> 3.46 us
    ppermute x4, starting transfers between devices: 14.8 us -> 11.5 us  [on_device(): other = [lax.ppermute(piece, 'wide', SWAP) for piece in own]]
    all_to_all x1, blocking collectives: 20.8 us -> 23.4 us  [on_device(): partial = lax.all_to_all(partial, 'narrow', 0, 0)]
    pallas_call x1, Pallas kernels: 1.5 us -> 3.89 us  [march_outer(): pl.pallas_call(outer_kernel, out_shape=pltpu.VMEM((rows // LANES, 4, cols...]
    select_n x2 -> x0, other arithmetic: 2.37 us -> none  [faces(): return (jnp.where(odd, low, high), jnp.where(odd, high, low))]
    ppermute x3, waiting for transfers between devices: 0.45 us -> 2.71 us  [gather(): return [block] + [lax.ppermute(block, 'wide', move) for move in MOVES]]
    pallas_call x1 -> x2, Pallas kernels: 6.88 us -> 5.06 us  [the longest x1 3.42 us: march_inner(): pl.pallas_call(inner_kernel, out_shape=[pltpu.VMEM((2, depth, cols, rows)...]
  transfers between devices with their start and end apart: 11 -> 11, of which waited for: 3 -> 3; matrix products, arithmetic and copies ran while one was open for 1% -> 0% of each run, Pallas kernels for 8% -> 5%
where the time goes in v6:
time: 99.3 us; the launch traced here: 98.7 us
  blocking collectives  45.7 us (46%)
  starting transfers between devices  37.1 us (37%)
  Pallas kernels  12.3 us (12%)
  waiting for transfers between devices  3.46 us (3%)
    all_to_all x1, blocking collectives, on_device(): partial = lax.all_to_all(partial, 'narrow', 0, 0)  23.4 us
    all_gather x3, blocking collectives, gather(): block = lax.all_gather(block, 'wide', axis_index_groups=groups)  22.3 us
    ppermute x3, starting transfers between devices, gather(): return [block] + [lax.ppermute(block, 'wide', move) for move in MOVES]  12.2 us
    ppermute x4, starting transfers between devices, on_device(): other = [lax.ppermute(piece, 'wide', SWAP) for piece in own]  11.5 us
    ppermute x2, starting transfers between devices, change(): lax.ppermute(inner, axis, [(i, i ^ 1) for i in range(count)])  10.7 us
    pallas_call x1, Pallas kernels, march_outer(): pl.pallas_call(outer_kernel, out_shape=pltpu.VMEM((rows // LANES, 4, cols...  3.89 us
    pallas_call x1, Pallas kernels, march_inner(): pl.pallas_call(inner_kernel, out_shape=[pltpu.VMEM((2, depth, cols, rows)...  3.42 us
    ppermute x3, waiting for transfers between devices, gather(): return [block] + [lax.ppermute(block, 'wide', move) for move in MOVES]  2.71 us
  transfers between devices with their start and end apart: 11, of which 3 were waited for; matrix products, arithmetic and copies ran while one was open for 0% of the time, Pallas kernels for 5%

profile of v6, /device:TPU:1, one launch (start us, length us, event | category | flops | bytes accessed | tf_op | source)
XLA Modules:
  0.0 98.7 jit_solution(4136475414963989767)
XLA Ops:
  0.0 1.6 %load.1 = (f32[2,8,32,1280]{3,2,1,0:T(8,128)S(1)}, f32[2,8,1,1024]{3,2,1,0:T(1,128)S(1)}, f32[2,8,1,1024]{3,2,1,0:T(1,128)S(1)}, f32[2,1,32,1024]{3,2,1,0:T(8,12...) custom-call(s32[1]{0:T(128)} %bitcast.wide.spot, ...), custom_call_target="tpu_custom_call" | custom-call | tf_op jit(solution)/shard_map/load/pallas_call | solution.py:222
  1.6 0.0 copy-start
  1.7 4.0 %collective-permute-start = (f32[2,1,32,1024]{3,2,1,0:T(8,128)S(1)}, f32[2,1,32,1024]{3,2,1,0:T(8,128)S(1)}, u32[]{:S(2)}, u32[]{:S(2)}) collective-permute-start(f32[2,1,32,1024]{3,2,1,0:T(8,128)S(1)} %get-tuple-element.15), channel_id=1, source_target_pairs={{0,1},{1,0},{2,3},{3,2},{4,5},{5,4},{6,7},{7,6},{8,9},{9,8},{10,11... | collective-permute-start | bytes 786440 | tf_op jit(solution)/shard_map/ppermute | solution.py:380
  5.7 0.7 collective-permute-start.1
  6.4 6.7 %collective-permute-start.2 = (f32[2,8,1,1024]{3,2,1,0:T(1,128)S(1)}, f32[2,8,1,1024]{3,2,1,0:T(1,128)S(1)}, u32[]{:S(2)}, u32[]{:S(2)}) collective-permute-start(f32[2,8,1,1024]{3,2,1,0:T(1,128)S(1)} %get-tuple-element.17), channel_id=1, source_target_pairs={{0,8},{8,0},{16,24},{24,16},{32,40},{40,32},{48,56},{56,48},{64,72... | collective-permute-start | bytes 196616 | tf_op jit(solution)/shard_map/ppermute | solution.py:380
  13.1 1.9 %collective-permute-start.3 = (f32[2,8,1,1024]{3,2,1,0:T(1,128)S(1)}, f32[2,8,1,1024]{3,2,1,0:T(1,128)S(1)}, u32[]{:S(2)}, u32[]{:S(2)}) collective-permute-start(f32[2,8,1,1024]{3,2,1,0:T(1,128)S(1)} %get-tuple-element.18), channel_id=1, source_target_pairs={{8,16},{16,8},{24,32},{32,24},{40,48},{48,40},{56,64},{64,56},{72,... | collective-permute-start | bytes 196616 | tf_op jit(solution)/shard_map/ppermute | solution.py:380
  15.0 3.4 %march_inner.1 = (s32[2,8,32,1024]{3,2,1,0:T(8,128)S(1)}, f32[8,4,16,128]{3,2,1,0:T(8,128)S(1)}) custom-call(s32[2,8,32,1024]{3,2,1,0:T(8,128)} %bins.1, f32[2,8,32,1280]{3,2,1,0:T(8,128)S(1)} %get-tuple-element.14.cells, s32[2,2,2,8,128]{4,3,2,1,0:T(8,128)S(1)} %get-tuple-element.19.tab, s32[32,128]{1,0:T(8,128)S(1)} %get-tuple-element.20.back), custom_call_target="tpu_custom_call" | custom-call | flops 52428800 | bytes 8388608 | tf_op jit(solution)/shard_map/march_inner/pallas_call | solution.py:249
  18.4 0.0 collective-permute-done.2.xin
  18.4 0.2 collective-permute-done.3.xout
  18.7 0.0 collective-permute-done.zin
  18.7 0.0 collective-permute-done.1.zout
  18.7 3.9 %march_outer.1 = f32[8,4,32,128]{3,2,1,0:T(8,128)S(1)} custom-call(s32[1]{0:T(128)} %bitcast.wide.spot, s32[1]{0:T(128)} %bitcast.1.narrow, f32[2,8,32,1280]{3,2,1,0:T(8,128)S(1)} %get-tuple-element.14.cells, f32[2,1,32,1024]{3,2,1,0:T(8,128)S(1)} %collective-permute-done.zin, f32[2,1,32,1024]{3,2,1,0:T(8,128)S(1)} %collective-permute-done.1.zout, ...), custom_call_target="tpu_custom_call" | custom-call | tf_op jit(solution)/shard_map/march_outer/pallas_call | solution.py:266
  22.6 0.0 copy-done
  22.6 23.4 %all_to_all.5.parts = f32[8,4,32,128]{3,2,1,0:T(8,128)S(1)} all-to-all(f32[8,4,32,128]{3,2,1,0:T(8,128)S(1)} %march_outer.1), channel_id=1, replica_groups=mesh['wide'=64,'narrow'=8] {'narrow'}, dimensions={0} | all-to-all | bytes 1048576 | tf_op jit(solution)/shard_map/all_to_all | solution.py:391
  45.9 0.8 join.1
  46.7 7.7 %all-gather = f32[8,32,128]{2,1,0:T(8,128)S(1)} all-gather(f32[4,32,128]{2,1,0:T(8,128)S(1)} %join.1), channel_id=2, replica_groups={{0,256},{8,264},{16,272},{24,280},{32,288},{40,296},{48,304},{56,312},{..., dimensions={0}, use_global_device_ids=true | all-gather | bytes 196608 | tf_op jit(solution)/shard_map/all_gather | solution.py:335
  54.4 7.5 %all-gather.1 = f32[4,4,32,128]{3,2,1,0:T(8,128)S(1)} all-gather(f32[2,4,32,128]{3,2,1,0:T(8,128)S(1)} %bitcast.13), channel_id=3, replica_groups={{0,128},{8,40},{16,144},{24,56},{32,160},{48,176},{64,192},{72,104},{80..., dimensions={0}, use_global_device_ids=true | all-gather | bytes 393216 | tf_op jit(solution)/shard_map/all_gather | solution.py:335
  61.9 7.1 %all-gather.2 = f32[4,2,4,32,128]{4,3,2,1,0:T(8,128)S(1)} all-gather(f32[2,2,4,32,128]{4,3,2,1,0:T(8,128)S(1)} %bitcast.12), channel_id=4, replica_groups={{0,64},{8,24},{16,80},{32,96},{40,56},{48,112},{72,88},{104,120},{128,1..., dimensions={0}, use_global_device_ids=true | all-gather | bytes 786432 | tf_op jit(solution)/shard_map/all_gather | solution.py:335
  69.0 6.5 %collective-permute-start.9 = (f32[2,2,2,4,32,128]{5,4,3,2,1,0:T(8,128)S(1)}, f32[2,2,2,4,32,128]{5,4,3,2,1,0:T(8,128)S(1)}, u32[]{:S(2)}, u32[]{:S(2)}) collective-permute-start(f32[2,2,2,4,32,128]{5,4,3,2,1,0:T(8,128)S(1)} %bitcast.7), channel_id=1, source_target_pairs={{0,32},{8,136},{16,48},{24,152},{32,0},{40,168},{48,16},{56,184},{... | collective-permute-start | bytes 1572872 | tf_op jit(solution)/shard_map/ppermute | solution.py:336
  75.5 3.8 %collective-permute-start.7 = (f32[2,2,2,4,32,128]{5,4,3,2,1,0:T(8,128)S(1)}, f32[2,2,2,4,32,128]{5,4,3,2,1,0:T(8,128)S(1)}, u32[]{:S(2)}, u32[]{:S(2)}) collective-permute-start(f32[2,2,2,4,32,128]{5,4,3,2,1,0:T(8,128)S(1)} %bitcast.8), channel_id=1, source_target_pairs={{0,48},{8,456},{16,32},{24,472},{32,16},{40,488},{48,0},{56,504},{... | collective-permute-start | bytes 1572872 | tf_op jit(solution)/shard_map/ppermute | solution.py:336
  79.3 1.9 %collective-permute-start.5 = (f32[2,2,2,4,32,128]{5,4,3,2,1,0:T(8,128)S(1)}, f32[2,2,2,4,32,128]{5,4,3,2,1,0:T(8,128)S(1)}, u32[]{:S(2)}, u32[]{:S(2)}) collective-permute-start(f32[2,2,2,4,32,128]{5,4,3,2,1,0:T(8,128)S(1)} %bitcast.9), channel_id=1, source_target_pairs={{0,16},{8,72},{16,0},{24,88},{32,48},{40,104},{48,32},{56,120},{64... | collective-permute-start | bytes 1572872 | tf_op jit(solution)/shard_map/ppermute | solution.py:336
  81.3 4.8 %collective-permute-start.4 = (f32[2,2,2,4,32,128]{5,4,3,2,1,0:T(8,128)S(1)}, f32[2,2,2,4,32,128]{5,4,3,2,1,0:T(8,128)S(1)}, u32[]{:S(2)}, u32[]{:S(2)}) collective-permute-start(f32[2,2,2,4,32,128]{5,4,3,2,1,0:T(8,128)S(1)} %bitcast.10), channel_id=1, source_target_pairs={{0,8},{8,0},{16,24},{24,16},{32,40},{40,32},{48,56},{56,48},{64,72... | collective-permute-start | bytes 1572872 | tf_op jit(solution)/shard_map/ppermute | solution.py:393
  86.1 0.0 collective-permute-done.9.refs_3_
  86.1 2.0 %collective-permute-start.10 = (f32[2,2,2,4,32,128]{5,4,3,2,1,0:T(8,128)S(1)}, f32[2,2,2,4,32,128]{5,4,3,2,1,0:T(8,128)S(1)}, u32[]{:S(2)}, u32[]{:S(2)}) collective-permute-start(f32[2,2,2,4,32,128]{5,4,3,2,1,0:T(8,128)S(1)} %collective-permute-done.9.refs_3_), channel_id=1, source_target_pairs={{0,8},{8,0},{16,24},{24,16},{32,40},{40,32},{48,56},{56,48},{64,72... | collective-permute-start | bytes 1572872 | tf_op jit(solution)/shard_map/ppermute | solution.py:393
  88.1 2.7 %collective-permute-done.7.refs_2_ = f32[2,2,2,4,32,128]{5,4,3,2,1,0:T(8,128)S(1)} collective-permute-done((f32[2,2,2,4,32,128]{5,4,3,2,1,0:T(8,128)S(1)}, f32[2,2,2,4,32,128]{5,4,3,2,1,0:T(8,128)S(1)}, u32[]{:S(2)}, u32[]{:S(2)}) %collective-permute-start.7) | collective-permute-done | bytes 524320 | tf_op jit(solution)/shard_map/ppermute | solution.py:336
  90.8 2.8 %collective-permute-start.8 = (f32[2,2,2,4,32,128]{5,4,3,2,1,0:T(8,128)S(1)}, f32[2,2,2,4,32,128]{5,4,3,2,1,0:T(8,128)S(1)}, u32[]{:S(2)}, u32[]{:S(2)}) collective-permute-start(f32[2,2,2,4,32,128]{5,4,3,2,1,0:T(8,128)S(1)} %collective-permute-done.7.refs_2_), channel_id=1, source_target_pairs={{0,8},{8,0},{16,24},{24,16},{32,40},{40,32},{48,56},{56,48},{64,72... | collective-permute-start | bytes 1572872 | tf_op jit(solution)/shard_map/ppermute | solution.py:393
  93.6 0.0 collective-permute-done.5.refs_1_
  93.6 1.9 %collective-permute-start.6 = (f32[2,2,2,4,32,128]{5,4,3,2,1,0:T(8,128)S(1)}, f32[2,2,2,4,32,128]{5,4,3,2,1,0:T(8,128)S(1)}, u32[]{:S(2)}, u32[]{:S(2)}) collective-permute-start(f32[2,2,2,4,32,128]{5,4,3,2,1,0:T(8,128)S(1)} %collective-permute-done.5.refs_1_), channel_id=1, source_target_pairs={{0,8},{8,0},{16,24},{24,16},{32,40},{40,32},{48,56},{56,48},{64,72... | collective-permute-start | bytes 1572872 | tf_op jit(solution)/shard_map/ppermute | solution.py:393
  95.6 1.3 %place.2.refs_4_ = f32[4,8,4,2,32,128]{5,4,3,2,1,0:T(8,128)} custom-call(s32[1]{0:T(128)} %bitcast.wide.spot, f32[2,2,2,4,32,128]{5,4,3,2,1,0:T(8,128)S(1)} %bitcast.11, f32[2,2,2,4,32,128]{5,4,3,2,1,0:T(8,128)S(1)} %collective-permute-done.5.refs_1_, f32[2,2,2,4,32,128]{5,4,3,2,1,0:T(8,128)S(1)} %collective-permute-done.7.refs_2_, ...), custom_call_target="tpu_custom_call" | custom-call | bytes 4194304 | tf_op jit(solution)/shard_map/place/pallas_call | solution.py:364
  96.9 0.0 collective-permute-done.4.refs_0_
  96.9 0.0 collective-permute-done.10.refs_3_
  96.9 0.0 collective-permute-done.8.refs_2_
  96.9 0.5 collective-permute-done.6.refs_1_
  97.4 1.3 %place.3 = f32[4,8,4,2,32,128]{5,4,3,2,1,0:T(8,128)} custom-call(s32[1]{0:T(128)} %bitcast.wide.spot, f32[2,2,2,4,32,128]{5,4,3,2,1,0:T(8,128)S(1)} %collective-permute-done.4.refs_0_, f32[2,2,2,4,32,128]{5,4,3,2,1,0:T(8,128)S(1)} %collective-permute-done.6.refs_1_, ...), custom_call_target="tpu_custom_call", output_to_operand_aliasing={{}: (5, {})} | custom-call | bytes 4194304 | tf_op jit(solution)/shard_map/place/pallas_call | solution.py:364
Async XLA Ops:
  1.6 20.9 %copy-start = (s32[32,128]{1,0:T(8,128)}, s32[32,128]{1,0:T(8,128)S(1)}, u32[]{:S(2)}) copy-start(s32[32,128]{1,0:T(8,128)S(1)} %get-tuple-element.20.back) | copy-start | bytes 49156
  1.7 17.0 %collective-permute-start = (f32[2,1,32,1024]{3,2,1,0:T(8,128)S(1)}, f32[2,1,32,1024]{3,2,1,0:T(8,128)S(1)}, u32[]{:S(2)}, u32[]{:S(2)}) collective-permute-start(f32[2,1,32,1024]{3,2,1,0:T(8,128)S(1)} %get-tuple-element.15), channel_id=1, source_target_pairs={{0,1},{1,0},{2,3},{3,2},{4,5},{5,4},{6,7},{7,6},{8,9},{9,8},{10,11... | collective-permute-start | bytes 786440 | tf_op jit(solution)/shard_map/ppermute | solution.py:380
  5.7 13.0 %collective-permute-start.1 = (f32[2,1,32,1024]{3,2,1,0:T(8,128)S(1)}, f32[2,1,32,1024]{3,2,1,0:T(8,128)S(1)}, u32[]{:S(2)}, u32[]{:S(2)}) collective-permute-start(f32[2,1,32,1024]{3,2,1,0:T(8,128)S(1)} %get-tuple-element.16), channel_id=1, source_target_pairs={{1,2},{2,1},{3,4},{4,3},{5,6},{6,5},{9,10},{10,9},{11,12},{12,11},... | collective-permute-start | bytes 786440 | tf_op jit(solution)/shard_map/ppermute | solution.py:380
  6.4 12.0 %collective-permute-start.2 = (f32[2,8,1,1024]{3,2,1,0:T(1,128)S(1)}, f32[2,8,1,1024]{3,2,1,0:T(1,128)S(1)}, u32[]{:S(2)}, u32[]{:S(2)}) collective-permute-start(f32[2,8,1,1024]{3,2,1,0:T(1,128)S(1)} %get-tuple-element.17), channel_id=1, source_target_pairs={{0,8},{8,0},{16,24},{24,16},{32,40},{40,32},{48,56},{56,48},{64,72... | collective-permute-start | bytes 196616 | tf_op jit(solution)/shard_map/ppermute | solution.py:380
  13.1 5.6 %collective-permute-start.3 = (f32[2,8,1,1024]{3,2,1,0:T(1,128)S(1)}, f32[2,8,1,1024]{3,2,1,0:T(1,128)S(1)}, u32[]{:S(2)}, u32[]{:S(2)}) collective-permute-start(f32[2,8,1,1024]{3,2,1,0:T(1,128)S(1)} %get-tuple-element.18), channel_id=1, source_target_pairs={{8,16},{16,8},{24,32},{32,24},{40,48},{48,40},{56,64},{64,56},{72,... | collective-permute-start | bytes 196616 | tf_op jit(solution)/shard_map/ppermute | solution.py:380
  69.0 17.1 %collective-permute-start.9 = (f32[2,2,2,4,32,128]{5,4,3,2,1,0:T(8,128)S(1)}, f32[2,2,2,4,32,128]{5,4,3,2,1,0:T(8,128)S(1)}, u32[]{:S(2)}, u32[]{:S(2)}) collective-permute-start(f32[2,2,2,4,32,128]{5,4,3,2,1,0:T(8,128)S(1)} %bitcast.7), channel_id=1, source_target_pairs={{0,32},{8,136},{16,48},{24,152},{32,0},{40,168},{48,16},{56,184},{... | collective-permute-start | bytes 1572872 | tf_op jit(solution)/shard_map/ppermute | solution.py:336
  75.5 15.3 %collective-permute-start.7 = (f32[2,2,2,4,32,128]{5,4,3,2,1,0:T(8,128)S(1)}, f32[2,2,2,4,32,128]{5,4,3,2,1,0:T(8,128)S(1)}, u32[]{:S(2)}, u32[]{:S(2)}) collective-permute-start(f32[2,2,2,4,32,128]{5,4,3,2,1,0:T(8,128)S(1)} %bitcast.8), channel_id=1, source_target_pairs={{0,48},{8,456},{16,32},{24,472},{32,16},{40,488},{48,0},{56,504},{... | collective-permute-start | bytes 1572872 | tf_op jit(solution)/shard_map/ppermute | solution.py:336
  79.3 14.3 %collective-permute-start.5 = (f32[2,2,2,4,32,128]{5,4,3,2,1,0:T(8,128)S(1)}, f32[2,2,2,4,32,128]{5,4,3,2,1,0:T(8,128)S(1)}, u32[]{:S(2)}, u32[]{:S(2)}) collective-permute-start(f32[2,2,2,4,32,128]{5,4,3,2,1,0:T(8,128)S(1)} %bitcast.9), channel_id=1, source_target_pairs={{0,16},{8,72},{16,0},{24,88},{32,48},{40,104},{48,32},{56,120},{64... | collective-permute-start | bytes 1572872 | tf_op jit(solution)/shard_map/ppermute | solution.py:336
  81.3 15.6 %collective-permute-start.4 = (f32[2,2,2,4,32,128]{5,4,3,2,1,0:T(8,128)S(1)}, f32[2,2,2,4,32,128]{5,4,3,2,1,0:T(8,128)S(1)}, u32[]{:S(2)}, u32[]{:S(2)}) collective-permute-start(f32[2,2,2,4,32,128]{5,4,3,2,1,0:T(8,128)S(1)} %bitcast.10), channel_id=1, source_target_pairs={{0,8},{8,0},{16,24},{24,16},{32,40},{40,32},{48,56},{56,48},{64,72... | collective-permute-start | bytes 1572872 | tf_op jit(solution)/shard_map/ppermute | solution.py:393
  86.1 10.8 %collective-permute-start.10 = (f32[2,2,2,4,32,128]{5,4,3,2,1,0:T(8,128)S(1)}, f32[2,2,2,4,32,128]{5,4,3,2,1,0:T(8,128)S(1)}, u32[]{:S(2)}, u32[]{:S(2)}) collective-permute-start(f32[2,2,2,4,32,128]{5,4,3,2,1,0:T(8,128)S(1)} %collective-permute-done.9.refs_3_), channel_id=1, source_target_pairs={{0,8},{8,0},{16,24},{24,16},{32,40},{40,32},{48,56},{56,48},{64,72... | collective-permute-start | bytes 1572872 | tf_op jit(solution)/shard_map/ppermute | solution.py:393
  90.8 6.1 %collective-permute-start.8 = (f32[2,2,2,4,32,128]{5,4,3,2,1,0:T(8,128)S(1)}, f32[2,2,2,4,32,128]{5,4,3,2,1,0:T(8,128)S(1)}, u32[]{:S(2)}, u32[]{:S(2)}) collective-permute-start(f32[2,2,2,4,32,128]{5,4,3,2,1,0:T(8,128)S(1)} %collective-permute-done.7.refs_2_), channel_id=1, source_target_pairs={{0,8},{8,0},{16,24},{24,16},{32,40},{40,32},{48,56},{56,48},{64,72... | collective-permute-start | bytes 1572872 | tf_op jit(solution)/shard_map/ppermute | solution.py:393
  93.6 3.8 %collective-permute-start.6 = (f32[2,2,2,4,32,128]{5,4,3,2,1,0:T(8,128)S(1)}, f32[2,2,2,4,32,128]{5,4,3,2,1,0:T(8,128)S(1)}, u32[]{:S(2)}, u32[]{:S(2)}) collective-permute-start(f32[2,2,2,4,32,128]{5,4,3,2,1,0:T(8,128)S(1)} %collective-permute-done.5.refs_1_), channel_id=1, source_target_pairs={{0,8},{8,0},{16,24},{24,16},{32,40},{40,32},{48,56},{56,48},{64,72... | collective-permute-start | bytes 1572872 | tf_op jit(solution)/shard_map/ppermute | solution.py:393

commit v7 on v6

--- a/solution.py
+++ b/solution.py
@@ -35,24 +35,21 @@
                 tab[f, w, h] = jnp.broadcast_to(word[:, h * LANES : (h + 1) * LANES], (SUBS, LANES))
 
 
-def masks():
-    sub = lax.broadcasted_iota(jnp.int32, (SUBS, LANES), 0)
-    lane = lax.broadcasted_iota(jnp.int32, (SUBS, LANES), 1)
-    return sub == 0, sub == SUBS - 1, lane == 0, lane == LANES - 1
-
-
-def cell(at, bins_of, d, tab, edges):
-    first_sub, last_sub, first_lane, last_lane = edges
+def ends(axis, length):
+    place = lax.broadcasted_iota(jnp.int32, (SUBS, LANES), axis)
+    return place == 0, place == length - 1
+
+
+def cell(at, slope, bins_of, d, tab, edges):
+    first_sub, last_sub = edges
     colour = clear = None
     for f in range(2):
-        here = at(f, d, 0, 0)
-        dz = at(f, d + 1, 0, 0) - at(f, d - 1, 0, 0)
-        after = pltpu.roll(jnp.where(first_sub, at(f, d, SUBS, 0), here), SUBS - 1, 0)
-        before = pltpu.roll(jnp.where(last_sub, at(f, d, -SUBS, 0), here), 1, 0)
+        here = at(f, d, 0)
+        dz = at(f, d + 1, 0) - at(f, d - 1, 0)
+        after = pltpu.roll(jnp.where(first_sub, at(f, d, SUBS), here), SUBS - 1, 0)
+        before = pltpu.roll(jnp.where(last_sub, at(f, d, -SUBS), here), 1, 0)
         dx = after - before
-        after = pltpu.roll(jnp.where(first_lane, at(f, d, 0, LANES), here), LANES - 1, 1)
-        before = pltpu.roll(jnp.where(last_lane, at(f, d, 0, -LANES), here), 1, 1)
-        dy = after - before
+        dy = slope(f)
         total = dz * dz + dx * dx + dy * dy
         shade = 0.3 + (0.35 * jnp.abs(dz)) * lax.rsqrt(0.25 * total + 1.0)
         root = total * lax.rsqrt(jnp.maximum(total, 1e-30))
@@ -91,13 +88,13 @@
         inner, outer = (face[index] for face in faces)
         return jnp.where(is_odd != after, inner, outer)
 
-    def at(f, d, dc, dr):
+    def at(f, d, dc):
         if d < 0 or d == depth:
             return ghost(depths, odd[1], d == depth, f, 0, span, here)
         if g * SUBS + dc < 0 or g * SUBS + dc == cols:
             face = ghost(columns, odd[0], dc > 0, f, d, slice(None), here)
             return jnp.broadcast_to(face, (SUBS, LANES))
-        return cells[f, d, pl.ds(g * SUBS + dc, SUBS), pl.ds(start + (LANES + dr), LANES)]
+        return cells[f, d, pl.ds(g * SUBS + dc, SUBS), here]
 
     return at
 
@@ -112,17 +109,12 @@
     ]
     for copy in small:
         copy.start()
-    ends = (0, depth - 1)
-    order = ends + tuple(range(1, depth - 1))
+    sides = (0, depth - 1)
+    order = sides + tuple(range(1, depth - 1))
     copies = {}
     for d in order:
-        copies[d] = pltpu.make_async_copy(fields.at[:, d], cells.at[:, d, :, pl.ds(LANES, rows)], field_sem.at[d])
+        copies[d] = pltpu.make_async_copy(fields.at[:, d], cells.at[:, d], field_sem.at[d])
         copies[d].start()
-    zero = jnp.zeros((cols, LANES), jnp.float32)
-    for f in range(2):
-        for d in range(depth):
-            cells[f, d, :, 0:LANES] = zero
-            cells[f, d, :, LANES + rows :] = zero
     for copy in small:
         copy.wait()
     sub = lax.broadcasted_iota(jnp.int32, (SUBS, LANES), 0)
@@ -133,20 +125,19 @@
         back[g * SUBS : (g + 1) * SUBS, :] = towards
     store_tables(colour_now, opacity_now, tab)
     x_odd, z_odd = wide[0] % 2 == 1, narrow[0] % 2 == 1
-    inside = slice(LANES, LANES + rows)
     for n, d in enumerate(order):
         copies[d].wait()
         for f in range(2):
-            low, high = cells[f, d, 0:1, inside], cells[f, d, cols - 1 : cols, inside]
+            low, high = cells[f, d, 0:1, :], cells[f, d, cols - 1 : cols, :]
             xin[f, d] = jnp.where(x_odd, low, high)
             xout[f, d] = jnp.where(x_odd, high, low)
             if n == 1:
-                low, high = (cells[f, end, :, inside] for end in ends)
+                low, high = (cells[f, end] for end in sides)
                 zin[f, 0] = jnp.where(z_odd, low, high)
                 zout[f, 0] = jnp.where(z_odd, high, low)
 
 
-def inner_kernel(bins, cells, tab, back, picks, mid, bin_sem):
+def inner_kernel(bins, cells, tab, back, picks, slopes, mid, bin_sem):
     depth, cols, rows = bins.shape[1:]
     groups, half = cols // SUBS, rows // 2
     bin_copies = {}
@@ -156,7 +147,22 @@
             part = pl.ds(g * SUBS, SUBS), pl.ds(h * half, half)
             bin_copies[g, h] = pltpu.make_async_copy(bins.at[:, :, *part], picks.at[:, :, *part], bin_sem.at[g, h])
             bin_copies[g, h].start()
-    edges = masks()
+    first_lane, last_lane = ends(1, LANES)
+    zero = jnp.zeros((SUBS, LANES), jnp.float32)
+
+    def differ(step, carry):
+        d, span = step // groups, pl.ds(pl.multiple_of(step % groups * SUBS, SUBS), SUBS)
+        for f in range(2):
+            tiles = [zero] + [cells[f, d, span, b * LANES : (b + 1) * LANES] for b in range(rows // LANES)] + [zero]
+            for b in range(rows // LANES):
+                before, here, after = tiles[b : b + 3]
+                after = pltpu.roll(jnp.where(first_lane, after, here), LANES - 1, 1)
+                before = pltpu.roll(jnp.where(last_lane, before, here), 1, 1)
+                slopes[f, d, span, b * LANES : (b + 1) * LANES] = after - before
+        return carry
+
+    lax.fori_loop(0, depth * groups, differ, 0, unroll=4)
+    edges = ends(0, SUBS)
     for g in inner:
         backward = back[g * SUBS : (g + 1) * SUBS, :] == 1
 
@@ -165,7 +171,8 @@
             at = lattice(cells, None, None, None, g, start)
 
             def element(d):
-                return cell(at, lambda f: picks[f, d, pl.ds(g * SUBS, SUBS), pl.ds(start, LANES)], d, tab, edges)
+                here = pl.ds(g * SUBS, SUBS), pl.ds(start, LANES)
+                return cell(at, lambda f: slopes[f, d, *here], lambda f: picks[f, d, *here], d, tab, edges)
 
             colours, through = composite((element(d) for d in range(1, depth - 1)), backward)
             for k, value in enumerate(colours + [through]):
@@ -180,10 +187,10 @@
             bin_copies[g, h].wait()
 
 
-def outer_kernel(wide, narrow, cells, zin, zout, xin, xout, picks, mid, tab, back, out):
+def outer_kernel(wide, narrow, cells, slopes, zin, zout, xin, xout, picks, mid, tab, back, out):
     depth, cols, rows = picks.shape[1:]
     groups = cols // SUBS
-    edges = masks()
+    edges = ends(0, SUBS)
     odd = wide[0] % 2 == 1, narrow[0] % 2 == 1
     for g in range(groups):
         backward = back[g * SUBS : (g + 1) * SUBS, :] == 1
@@ -194,7 +201,8 @@
             at = lattice(cells, (xin, xout), (zin, zout), odd, g, start)
 
             def element(d):
-                return cell(at, lambda f: picks[f, d, pl.ds(g * SUBS, SUBS), pl.ds(start, LANES)], d, tab, edges)
+                here = pl.ds(g * SUBS, SUBS), pl.ds(start, LANES)
+                return cell(at, lambda f: slopes[f, d, *here], lambda f: picks[f, d, *here], d, tab, edges)
 
             if inside:
                 middle = [mid[b, k, pl.ds((g - 1) * SUBS, SUBS), :] for k in range(4)]
@@ -207,7 +215,7 @@
             out[b, 3, pl.ds(g * SUBS, SUBS), :] = 1.0 - through
             return carry
 
-        lax.fori_loop(0, rows // LANES, tile, 0, unroll=8 if inside else 4)
+        lax.fori_loop(0, rows // LANES, tile, 0, unroll=8)
 
 
 VMEM = pl.BlockSpec(memory_space=pltpu.VMEM)
@@ -222,7 +230,7 @@
     return pl.pallas_call(
         load_kernel,
         out_shape=[
-            pltpu.VMEM((2, depth, cols, rows + 2 * LANES), jnp.float32),
+            pltpu.VMEM((2, depth, cols, rows), jnp.float32),
             pltpu.VMEM((2, depth, 1, rows), jnp.float32),
             pltpu.VMEM((2, depth, 1, rows), jnp.float32),
             pltpu.VMEM((2, 1, cols, rows), jnp.float32),
@@ -250,10 +258,11 @@
         inner_kernel,
         out_shape=[
             pltpu.VMEM((2, depth, cols, rows), jnp.int32),
+            pltpu.VMEM((2, depth, cols, rows), jnp.float32),
             pltpu.VMEM((rows // LANES, 4, cols - 2 * SUBS, LANES), jnp.float32),
         ],
-        in_specs=[ANY, VMEM, VMEM, VMEM],
-        out_specs=[VMEM] * 2,
+        in_specs=[ANY] + [VMEM] * 3,
+        out_specs=[VMEM] * 3,
         scratch_shapes=[pltpu.SemaphoreType.DMA((cols // SUBS, 2))],
         compiler_params=pltpu.CompilerParams(vmem_limit_bytes=LIMIT),
         cost_estimate=pl.CostEstimate(flops=100 * 2 * depth * cols * rows, bytes_accessed=8 * 2**20, transcendentals=0),
@@ -261,16 +270,16 @@
     )(pltpu.with_memory_space_constraint(bins, pltpu.HBM), cells, tab, back)
 
 
-def march_outer(wide, narrow, cells, zin, zout, xin, xout, picks, mid, tab, back):
+def march_outer(wide, narrow, cells, slopes, zin, zout, xin, xout, picks, mid, tab, back):
     _, depth, cols, rows = picks.shape
     return pl.pallas_call(
         outer_kernel,
         out_shape=pltpu.VMEM((rows // LANES, 4, cols, LANES), jnp.float32),
-        in_specs=[SMEM] * 2 + [VMEM] * 9,
+        in_specs=[SMEM] * 2 + [VMEM] * 10,
         out_specs=VMEM,
         compiler_params=pltpu.CompilerParams(vmem_limit_bytes=LIMIT),
         name="march_outer",
-    )(wide, narrow, cells, zin, zout, xin, xout, picks, mid, tab, back)
+    )(wide, narrow, cells, slopes, zin, zout, xin, xout, picks, mid, tab, back)
 
 
 def join_kernel(parts, back, out):
@@ -386,8 +395,8 @@
     cells, *faces, tab, back = load(wide, narrow, fields, colour, opacity_table, view_dir)
     zin, zout = change(*faces[2:], "narrow")
     xin, xout = change(*faces[:2], "wide")
-    picks, mid = march_inner(field_bins, cells, tab, back)
-    partial = march_outer(wide, narrow, cells, zin, zout, xin, xout, picks, mid, tab, back)
+    picks, slopes, mid = march_inner(field_bins, cells, tab, back)
+    partial = march_outer(wide, narrow, cells, slopes, zin, zout, xin, xout, picks, mid, tab, back)
     partial = lax.all_to_all(partial, "narrow", 0, 0)
     own = gather(join(partial, back))
     other = [lax.ppermute(piece, "wide", SWAP) for piece in own]

time: 99.3 us -> 97.9 us (0.986)
  Pallas kernels: 12.3 us -> 11 us
    pallas_call x1, Pallas kernels: 3.89 us -> 2.5 us  [march_outer(): pl.pallas_call(outer_kernel, out_shape=pltpu.VMEM((rows // LANES, 4, cols...]
where the time goes in v7:
time: 97.9 us; the launch traced here: 97.4 us
  blocking collectives  45.7 us (47%)
  starting transfers between devices  37 us (38%)
  Pallas kernels  11 us (11%)
  waiting for transfers between devices  3.45 us (4%)
    all_to_all x1, blocking collectives, on_device(): partial = lax.all_to_all(partial, 'narrow', 0, 0)  23.4 us
    all_gather x3, blocking collectives, gather(): block = lax.all_gather(block, 'wide', axis_index_groups=groups)  22.4 us
    ppermute x3, starting transfers between devices, gather(): return [block] + [lax.ppermute(block, 'wide', move) for move in MOVES]  12.2 us
    ppermute x4, starting transfers between devices, on_device(): other = [lax.ppermute(piece, 'wide', SWAP) for piece in own]  11.6 us
    ppermute x2, starting transfers between devices, change(): lax.ppermute(inner, axis, [(i, i ^ 1) for i in range(count)])  10.7 us
    pallas_call x1, Pallas kernels, march_inner(): pl.pallas_call(inner_kernel, out_shape=[pltpu.VMEM((2, depth, cols, rows)...  3.49 us
    ppermute x3, waiting for transfers between devices, gather(): return [block] + [lax.ppermute(block, 'wide', move) for move in MOVES]  2.76 us
    pallas_call x2, Pallas kernels, place(): pl.pallas_call(functools.partial(place_kernel, swapped), in_specs=[SMEM]...  2.61 us
  transfers between devices with their start and end apart: 11, of which 3 were waited for; matrix products, arithmetic and copies ran while one was open for 0% of the time, Pallas kernels for 5%

profile of v7, /device:TPU:1, one launch (start us, length us, event | category | flops | bytes accessed | tf_op | source)
XLA Modules:
  0.0 97.4 jit_solution(5931593269335743753)
XLA Ops:
  0.0 1.6 %load.1 = (f32[2,8,32,1024]{3,2,1,0:T(8,128)S(1)}, f32[2,8,1,1024]{3,2,1,0:T(1,128)S(1)}, f32[2,8,1,1024]{3,2,1,0:T(1,128)S(1)}, f32[2,1,32,1024]{3,2,1,0:T(8,12...) custom-call(s32[1]{0:T(128)} %bitcast.wide.spot, ...), custom_call_target="tpu_custom_call" | custom-call | tf_op jit(solution)/shard_map/load/pallas_call | solution.py:230
  1.6 0.0 copy-start
  1.7 4.0 %collective-permute-start = (f32[2,1,32,1024]{3,2,1,0:T(8,128)S(1)}, f32[2,1,32,1024]{3,2,1,0:T(8,128)S(1)}, u32[]{:S(2)}, u32[]{:S(2)}) collective-permute-start(f32[2,1,32,1024]{3,2,1,0:T(8,128)S(1)} %get-tuple-element.19), channel_id=1, source_target_pairs={{0,1},{1,0},{2,3},{3,2},{4,5},{5,4},{6,7},{7,6},{8,9},{9,8},{10,11... | collective-permute-start | bytes 786440 | tf_op jit(solution)/shard_map/ppermute | solution.py:389
  5.7 0.7 collective-permute-start.1
  6.4 6.7 %collective-permute-start.2 = (f32[2,8,1,1024]{3,2,1,0:T(1,128)S(1)}, f32[2,8,1,1024]{3,2,1,0:T(1,128)S(1)}, u32[]{:S(2)}, u32[]{:S(2)}) collective-permute-start(f32[2,8,1,1024]{3,2,1,0:T(1,128)S(1)} %get-tuple-element.21), channel_id=1, source_target_pairs={{0,8},{8,0},{16,24},{24,16},{32,40},{40,32},{48,56},{56,48},{64,72... | collective-permute-start | bytes 196616 | tf_op jit(solution)/shard_map/ppermute | solution.py:389
  13.1 1.9 %collective-permute-start.3 = (f32[2,8,1,1024]{3,2,1,0:T(1,128)S(1)}, f32[2,8,1,1024]{3,2,1,0:T(1,128)S(1)}, u32[]{:S(2)}, u32[]{:S(2)}) collective-permute-start(f32[2,8,1,1024]{3,2,1,0:T(1,128)S(1)} %get-tuple-element.22), channel_id=1, source_target_pairs={{8,16},{16,8},{24,32},{32,24},{40,48},{48,40},{56,64},{64,56},{72,... | collective-permute-start | bytes 196616 | tf_op jit(solution)/shard_map/ppermute | solution.py:389
  15.0 3.5 %march_inner.1 = (s32[2,8,32,1024]{3,2,1,0:T(8,128)S(1)}, f32[2,8,32,1024]{3,2,1,0:T(8,128)S(1)}, f32[8,4,16,128]{3,2,1,0:T(8,128)S(1)}) custom-call(s32[2,8,32,1024]{3,2,1,0:T(8,128)} %bins.1, f32[2,8,32,1024]{3,2,1,0:T(8,128)S(1)} %get-tuple-element.15.cells, s32[2,2,2,8,128]{4,3,2,1,0:T(8,128)S(1)} %get-tuple-element.16.tab, ...), custom_call_target="tpu_custom_call" | custom-call | flops 52428800 | bytes 8388608 | tf_op jit(solution)/shard_map/march_inner/pallas_call | solution.py:257
  18.5 0.0 collective-permute-done.2.xin
  18.5 0.2 collective-permute-done.3.xout
  18.6 0.0 collective-permute-done.zin
  18.6 0.0 collective-permute-done.1.zout
  18.7 0.0 copy-done
  18.7 2.5 %march_outer.1 = f32[8,4,32,128]{3,2,1,0:T(8,128)S(1)} custom-call(s32[1]{0:T(128)} %bitcast.wide.spot, s32[1]{0:T(128)} %bitcast.1.narrow, f32[2,8,32,1024]{3,2,1,0:T(8,128)S(1)} %get-tuple-element.15.cells, f32[2,8,32,1024]{3,2,1,0:T(8,128)S(1)} %get-tuple-element.18.slopes, f32[2,1,32,1024]{3,2,1,0:T(8,128)S(1)} %collective-permute-done.zin, ...), custom_call_target="tpu_custom_call" | custom-call | tf_op jit(solution)/shard_map/march_outer/pallas_call | solution.py:275
  21.2 23.4 %all_to_all.5.parts = f32[8,4,32,128]{3,2,1,0:T(8,128)S(1)} all-to-all(f32[8,4,32,128]{3,2,1,0:T(8,128)S(1)} %march_outer.1), channel_id=1, replica_groups=mesh['wide'=64,'narrow'=8] {'narrow'}, dimensions={0} | all-to-all | bytes 1048576 | tf_op jit(solution)/shard_map/all_to_all | solution.py:400
  44.5 0.8 join.1
  45.3 7.7 %all-gather = f32[8,32,128]{2,1,0:T(8,128)S(1)} all-gather(f32[4,32,128]{2,1,0:T(8,128)S(1)} %join.1), channel_id=2, replica_groups={{0,256},{8,264},{16,272},{24,280},{32,288},{40,296},{48,304},{56,312},{..., dimensions={0}, use_global_device_ids=true | all-gather | bytes 196608 | tf_op jit(solution)/shard_map/all_gather | solution.py:344
  53.0 8.0 %all-gather.1 = f32[4,4,32,128]{3,2,1,0:T(8,128)S(1)} all-gather(f32[2,4,32,128]{3,2,1,0:T(8,128)S(1)} %bitcast.13), channel_id=3, replica_groups={{0,128},{8,40},{16,144},{24,56},{32,160},{48,176},{64,192},{72,104},{80..., dimensions={0}, use_global_device_ids=true | all-gather | bytes 393216 | tf_op jit(solution)/shard_map/all_gather | solution.py:344
  61.0 6.7 %all-gather.2 = f32[4,2,4,32,128]{4,3,2,1,0:T(8,128)S(1)} all-gather(f32[2,2,4,32,128]{4,3,2,1,0:T(8,128)S(1)} %bitcast.12), channel_id=4, replica_groups={{0,64},{8,24},{16,80},{32,96},{40,56},{48,112},{72,88},{104,120},{128,1..., dimensions={0}, use_global_device_ids=true | all-gather | bytes 786432 | tf_op jit(solution)/shard_map/all_gather | solution.py:344
  67.7 6.5 %collective-permute-start.9 = (f32[2,2,2,4,32,128]{5,4,3,2,1,0:T(8,128)S(1)}, f32[2,2,2,4,32,128]{5,4,3,2,1,0:T(8,128)S(1)}, u32[]{:S(2)}, u32[]{:S(2)}) collective-permute-start(f32[2,2,2,4,32,128]{5,4,3,2,1,0:T(8,128)S(1)} %bitcast.7), channel_id=1, source_target_pairs={{0,32},{8,136},{16,48},{24,152},{32,0},{40,168},{48,16},{56,184},{... | collective-permute-start | bytes 1572872 | tf_op jit(solution)/shard_map/ppermute | solution.py:345
  74.2 3.7 %collective-permute-start.7 = (f32[2,2,2,4,32,128]{5,4,3,2,1,0:T(8,128)S(1)}, f32[2,2,2,4,32,128]{5,4,3,2,1,0:T(8,128)S(1)}, u32[]{:S(2)}, u32[]{:S(2)}) collective-permute-start(f32[2,2,2,4,32,128]{5,4,3,2,1,0:T(8,128)S(1)} %bitcast.8), channel_id=1, source_target_pairs={{0,48},{8,456},{16,32},{24,472},{32,16},{40,488},{48,0},{56,504},{... | collective-permute-start | bytes 1572872 | tf_op jit(solution)/shard_map/ppermute | solution.py:345
  77.9 1.9 %collective-permute-start.5 = (f32[2,2,2,4,32,128]{5,4,3,2,1,0:T(8,128)S(1)}, f32[2,2,2,4,32,128]{5,4,3,2,1,0:T(8,128)S(1)}, u32[]{:S(2)}, u32[]{:S(2)}) collective-permute-start(f32[2,2,2,4,32,128]{5,4,3,2,1,0:T(8,128)S(1)} %bitcast.9), channel_id=1, source_target_pairs={{0,16},{8,72},{16,0},{24,88},{32,48},{40,104},{48,32},{56,120},{64... | collective-permute-start | bytes 1572872 | tf_op jit(solution)/shard_map/ppermute | solution.py:345
  79.9 4.9 %collective-permute-start.4 = (f32[2,2,2,4,32,128]{5,4,3,2,1,0:T(8,128)S(1)}, f32[2,2,2,4,32,128]{5,4,3,2,1,0:T(8,128)S(1)}, u32[]{:S(2)}, u32[]{:S(2)}) collective-permute-start(f32[2,2,2,4,32,128]{5,4,3,2,1,0:T(8,128)S(1)} %bitcast.10), channel_id=1, source_target_pairs={{0,8},{8,0},{16,24},{24,16},{32,40},{40,32},{48,56},{56,48},{64,72... | collective-permute-start | bytes 1572872 | tf_op jit(solution)/shard_map/ppermute | solution.py:402
  84.8 0.0 collective-permute-done.9.refs_3_
  84.8 2.0 %collective-permute-start.10 = (f32[2,2,2,4,32,128]{5,4,3,2,1,0:T(8,128)S(1)}, f32[2,2,2,4,32,128]{5,4,3,2,1,0:T(8,128)S(1)}, u32[]{:S(2)}, u32[]{:S(2)}) collective-permute-start(f32[2,2,2,4,32,128]{5,4,3,2,1,0:T(8,128)S(1)} %collective-permute-done.9.refs_3_), channel_id=1, source_target_pairs={{0,8},{8,0},{16,24},{24,16},{32,40},{40,32},{48,56},{56,48},{64,72... | collective-permute-start | bytes 1572872 | tf_op jit(solution)/shard_map/ppermute | solution.py:402
  86.7 2.8 %collective-permute-done.7.refs_2_ = f32[2,2,2,4,32,128]{5,4,3,2,1,0:T(8,128)S(1)} collective-permute-done((f32[2,2,2,4,32,128]{5,4,3,2,1,0:T(8,128)S(1)}, f32[2,2,2,4,32,128]{5,4,3,2,1,0:T(8,128)S(1)}, u32[]{:S(2)}, u32[]{:S(2)}) %collective-permute-start.7) | collective-permute-done | bytes 524320 | tf_op jit(solution)/shard_map/ppermute | solution.py:345
  89.5 2.8 %collective-permute-start.8 = (f32[2,2,2,4,32,128]{5,4,3,2,1,0:T(8,128)S(1)}, f32[2,2,2,4,32,128]{5,4,3,2,1,0:T(8,128)S(1)}, u32[]{:S(2)}, u32[]{:S(2)}) collective-permute-start(f32[2,2,2,4,32,128]{5,4,3,2,1,0:T(8,128)S(1)} %collective-permute-done.7.refs_2_), channel_id=1, source_target_pairs={{0,8},{8,0},{16,24},{24,16},{32,40},{40,32},{48,56},{56,48},{64,72... | collective-permute-start | bytes 1572872 | tf_op jit(solution)/shard_map/ppermute | solution.py:402
  92.3 0.0 collective-permute-done.5.refs_1_
  92.3 1.9 %collective-permute-start.6 = (f32[2,2,2,4,32,128]{5,4,3,2,1,0:T(8,128)S(1)}, f32[2,2,2,4,32,128]{5,4,3,2,1,0:T(8,128)S(1)}, u32[]{:S(2)}, u32[]{:S(2)}) collective-permute-start(f32[2,2,2,4,32,128]{5,4,3,2,1,0:T(8,128)S(1)} %collective-permute-done.5.refs_1_), channel_id=1, source_target_pairs={{0,8},{8,0},{16,24},{24,16},{32,40},{40,32},{48,56},{56,48},{64,72... | collective-permute-start | bytes 1572872 | tf_op jit(solution)/shard_map/ppermute | solution.py:402
  94.2 1.3 %place.2.refs_4_ = f32[4,8,4,2,32,128]{5,4,3,2,1,0:T(8,128)} custom-call(s32[1]{0:T(128)} %bitcast.wide.spot, f32[2,2,2,4,32,128]{5,4,3,2,1,0:T(8,128)S(1)} %bitcast.11, f32[2,2,2,4,32,128]{5,4,3,2,1,0:T(8,128)S(1)} %collective-permute-done.5.refs_1_, f32[2,2,2,4,32,128]{5,4,3,2,1,0:T(8,128)S(1)} %collective-permute-done.7.refs_2_, ...), custom_call_target="tpu_custom_call" | custom-call | bytes 4194304 | tf_op jit(solution)/shard_map/place/pallas_call | solution.py:373
  95.5 0.0 collective-permute-done.4.refs_0_
  95.6 0.0 collective-permute-done.10.refs_3_
  95.6 0.0 collective-permute-done.8.refs_2_
  95.6 0.5 collective-permute-done.6.refs_1_
  96.1 1.3 %place.3 = f32[4,8,4,2,32,128]{5,4,3,2,1,0:T(8,128)} custom-call(s32[1]{0:T(128)} %bitcast.wide.spot, f32[2,2,2,4,32,128]{5,4,3,2,1,0:T(8,128)S(1)} %collective-permute-done.4.refs_0_, f32[2,2,2,4,32,128]{5,4,3,2,1,0:T(8,128)S(1)} %collective-permute-done.6.refs_1_, ...), custom_call_target="tpu_custom_call", output_to_operand_aliasing={{}: (5, {})} | custom-call | bytes 4194304 | tf_op jit(solution)/shard_map/place/pallas_call | solution.py:373
Async XLA Ops:
  1.6 17.0 %copy-start = (s32[32,128]{1,0:T(8,128)}, s32[32,128]{1,0:T(8,128)S(1)}, u32[]{:S(2)}) copy-start(s32[32,128]{1,0:T(8,128)S(1)} %get-tuple-element.17.back) | copy-start | bytes 49156
  1.7 17.0 %collective-permute-start = (f32[2,1,32,1024]{3,2,1,0:T(8,128)S(1)}, f32[2,1,32,1024]{3,2,1,0:T(8,128)S(1)}, u32[]{:S(2)}, u32[]{:S(2)}) collective-permute-start(f32[2,1,32,1024]{3,2,1,0:T(8,128)S(1)} %get-tuple-element.19), channel_id=1, source_target_pairs={{0,1},{1,0},{2,3},{3,2},{4,5},{5,4},{6,7},{7,6},{8,9},{9,8},{10,11... | collective-permute-start | bytes 786440 | tf_op jit(solution)/shard_map/ppermute | solution.py:389
  5.7 13.0 %collective-permute-start.1 = (f32[2,1,32,1024]{3,2,1,0:T(8,128)S(1)}, f32[2,1,32,1024]{3,2,1,0:T(8,128)S(1)}, u32[]{:S(2)}, u32[]{:S(2)}) collective-permute-start(f32[2,1,32,1024]{3,2,1,0:T(8,128)S(1)} %get-tuple-element.20), channel_id=1, source_target_pairs={{1,2},{2,1},{3,4},{4,3},{5,6},{6,5},{9,10},{10,9},{11,12},{12,11},... | collective-permute-start | bytes 786440 | tf_op jit(solution)/shard_map/ppermute | solution.py:389
  6.4 12.1 %collective-permute-start.2 = (f32[2,8,1,1024]{3,2,1,0:T(1,128)S(1)}, f32[2,8,1,1024]{3,2,1,0:T(1,128)S(1)}, u32[]{:S(2)}, u32[]{:S(2)}) collective-permute-start(f32[2,8,1,1024]{3,2,1,0:T(1,128)S(1)} %get-tuple-element.21), channel_id=1, source_target_pairs={{0,8},{8,0},{16,24},{24,16},{32,40},{40,32},{48,56},{56,48},{64,72... | collective-permute-start | bytes 196616 | tf_op jit(solution)/shard_map/ppermute | solution.py:389
  13.1 5.6 %collective-permute-start.3 = (f32[2,8,1,1024]{3,2,1,0:T(1,128)S(1)}, f32[2,8,1,1024]{3,2,1,0:T(1,128)S(1)}, u32[]{:S(2)}, u32[]{:S(2)}) collective-permute-start(f32[2,8,1,1024]{3,2,1,0:T(1,128)S(1)} %get-tuple-element.22), channel_id=1, source_target_pairs={{8,16},{16,8},{24,32},{32,24},{40,48},{48,40},{56,64},{64,56},{72,... | collective-permute-start | bytes 196616 | tf_op jit(solution)/shard_map/ppermute | solution.py:389
  67.7 17.1 %collective-permute-start.9 = (f32[2,2,2,4,32,128]{5,4,3,2,1,0:T(8,128)S(1)}, f32[2,2,2,4,32,128]{5,4,3,2,1,0:T(8,128)S(1)}, u32[]{:S(2)}, u32[]{:S(2)}) collective-permute-start(f32[2,2,2,4,32,128]{5,4,3,2,1,0:T(8,128)S(1)} %bitcast.7), channel_id=1, source_target_pairs={{0,32},{8,136},{16,48},{24,152},{32,0},{40,168},{48,16},{56,184},{... | collective-permute-start | bytes 1572872 | tf_op jit(solution)/shard_map/ppermute | solution.py:345
  74.2 15.3 %collective-permute-start.7 = (f32[2,2,2,4,32,128]{5,4,3,2,1,0:T(8,128)S(1)}, f32[2,2,2,4,32,128]{5,4,3,2,1,0:T(8,128)S(1)}, u32[]{:S(2)}, u32[]{:S(2)}) collective-permute-start(f32[2,2,2,4,32,128]{5,4,3,2,1,0:T(8,128)S(1)} %bitcast.8), channel_id=1, source_target_pairs={{0,48},{8,456},{16,32},{24,472},{32,16},{40,488},{48,0},{56,504},{... | collective-permute-start | bytes 1572872 | tf_op jit(solution)/shard_map/ppermute | solution.py:345
  77.9 14.4 %collective-permute-start.5 = (f32[2,2,2,4,32,128]{5,4,3,2,1,0:T(8,128)S(1)}, f32[2,2,2,4,32,128]{5,4,3,2,1,0:T(8,128)S(1)}, u32[]{:S(2)}, u32[]{:S(2)}) collective-permute-start(f32[2,2,2,4,32,128]{5,4,3,2,1,0:T(8,128)S(1)} %bitcast.9), channel_id=1, source_target_pairs={{0,16},{8,72},{16,0},{24,88},{32,48},{40,104},{48,32},{56,120},{64... | collective-permute-start | bytes 1572872 | tf_op jit(solution)/shard_map/ppermute | solution.py:345
  79.9 15.7 %collective-permute-start.4 = (f32[2,2,2,4,32,128]{5,4,3,2,1,0:T(8,128)S(1)}, f32[2,2,2,4,32,128]{5,4,3,2,1,0:T(8,128)S(1)}, u32[]{:S(2)}, u32[]{:S(2)}) collective-permute-start(f32[2,2,2,4,32,128]{5,4,3,2,1,0:T(8,128)S(1)} %bitcast.10), channel_id=1, source_target_pairs={{0,8},{8,0},{16,24},{24,16},{32,40},{40,32},{48,56},{56,48},{64,72... | collective-permute-start | bytes 1572872 | tf_op jit(solution)/shard_map/ppermute | solution.py:402
  84.8 10.8 %collective-permute-start.10 = (f32[2,2,2,4,32,128]{5,4,3,2,1,0:T(8,128)S(1)}, f32[2,2,2,4,32,128]{5,4,3,2,1,0:T(8,128)S(1)}, u32[]{:S(2)}, u32[]{:S(2)}) collective-permute-start(f32[2,2,2,4,32,128]{5,4,3,2,1,0:T(8,128)S(1)} %collective-permute-done.9.refs_3_), channel_id=1, source_target_pairs={{0,8},{8,0},{16,24},{24,16},{32,40},{40,32},{48,56},{56,48},{64,72... | collective-permute-start | bytes 1572872 | tf_op jit(solution)/shard_map/ppermute | solution.py:402
  89.5 6.1 %collective-permute-start.8 = (f32[2,2,2,4,32,128]{5,4,3,2,1,0:T(8,128)S(1)}, f32[2,2,2,4,32,128]{5,4,3,2,1,0:T(8,128)S(1)}, u32[]{:S(2)}, u32[]{:S(2)}) collective-permute-start(f32[2,2,2,4,32,128]{5,4,3,2,1,0:T(8,128)S(1)} %collective-permute-done.7.refs_2_), channel_id=1, source_target_pairs={{0,8},{8,0},{16,24},{24,16},{32,40},{40,32},{48,56},{56,48},{64,72... | collective-permute-start | bytes 1572872 | tf_op jit(solution)/shard_map/ppermute | solution.py:402
  92.3 3.8 %collective-permute-start.6 = (f32[2,2,2,4,32,128]{5,4,3,2,1,0:T(8,128)S(1)}, f32[2,2,2,4,32,128]{5,4,3,2,1,0:T(8,128)S(1)}, u32[]{:S(2)}, u32[]{:S(2)}) collective-permute-start(f32[2,2,2,4,32,128]{5,4,3,2,1,0:T(8,128)S(1)} %collective-permute-done.5.refs_1_), channel_id=1, source_target_pairs={{0,8},{8,0},{16,24},{24,16},{32,40},{40,32},{48,56},{56,48},{64,72... | collective-permute-start | bytes 1572872 | tf_op jit(solution)/shard_map/ppermute | solution.py:402

commit v8 on v7

--- a/solution.py
+++ b/solution.py
@@ -321,8 +321,8 @@
 
 
 DOUBLINGS = (
-    pairs(lambda z, x, core: (z ^ 4, x, core)),
-    pairs(lambda z, x, core: (z, x ^ 2, core) if core else (z ^ 2, x, core)),
+    pairs(lambda z, x, core: (z ^ 4, x, core) if core else (z ^ 2, x, core)),
+    pairs(lambda z, x, core: (z, x ^ 2, core) if core else (z ^ 4, x, core)),
     pairs(lambda z, x, core: (z, x ^ 1, core) if core else (z ^ 1, x, core)),
 )
 
@@ -357,7 +357,7 @@
         for third in range(2):
             for second in range(2):
                 for first in range(2):
-                    z_now = jnp.where(core == 0, 4 * first + 2 * second + third, 4 * first + z_from)
+                    z_now = jnp.where(core == 0, 2 * first + 4 * second + third, 4 * first + z_from)
                     x_now = jnp.where(core == 0, x_from, 2 * second + third)
                     target = out.at[:, z_now, x_now, core]
                     copies.append(pltpu.make_async_copy(pieces[piece].at[third, second, first], target, sem))

time: 97.9 us -> 97.4 us (level)
  waiting for transfers between devices: 3.45 us -> 2.29 us
    ppermute x3, waiting for transfers between devices: 2.76 us -> 1.6 us  [gather(): return [block] + [lax.ppermute(block, 'wide', move) for move in MOVES]]
where the time goes in v8:
time: 97.4 us; the launch traced here: 96.9 us
  blocking collectives  45.7 us (47%)
  starting transfers between devices  37.7 us (39%)
  Pallas kernels  11 us (11%)
  waiting for transfers between devices  2.29 us (2%)
    all_to_all x1, blocking collectives, on_device(): partial = lax.all_to_all(partial, 'narrow', 0, 0)  23.4 us
    all_gather x3, blocking collectives, gather(): block = lax.all_gather(block, 'wide', axis_index_groups=groups)  22.3 us
    ppermute x3, starting transfers between devices, gather(): return [block] + [lax.ppermute(block, 'wide', move) for move in MOVES]  12.3 us
    ppermute x4, starting transfers between devices, on_device(): other = [lax.ppermute(piece, 'wide', SWAP) for piece in own]  12.1 us
    ppermute x2, starting transfers between devices, change(): lax.ppermute(inner, axis, [(i, i ^ 1) for i in range(count)])  10.7 us
    pallas_call x1, Pallas kernels, march_inner(): pl.pallas_call(inner_kernel, out_shape=[pltpu.VMEM((2, depth, cols, rows)...  3.49 us
    pallas_call x2, Pallas kernels, place(): pl.pallas_call(functools.partial(place_kernel, swapped), in_specs=[SMEM]...  2.61 us
    ppermute x2, starting transfers between devices, change(): lax.ppermute(outer, axis, route)  2.6 us
  transfers between devices with their start and end apart: 11, of which 3 were waited for; matrix products, arithmetic and copies ran while one was open for 0% of the time, Pallas kernels for 5%

profile of v8, /device:TPU:1, one launch (start us, length us, event | category | flops | bytes accessed | tf_op | source)
XLA Modules:
  0.0 96.9 jit_solution(11429444355196294355)
XLA Ops:
  0.0 1.6 %load.1 = (f32[2,8,32,1024]{3,2,1,0:T(8,128)S(1)}, f32[2,8,1,1024]{3,2,1,0:T(1,128)S(1)}, f32[2,8,1,1024]{3,2,1,0:T(1,128)S(1)}, f32[2,1,32,1024]{3,2,1,0:T(8,12...) custom-call(s32[1]{0:T(128)} %bitcast.wide.spot, ...), custom_call_target="tpu_custom_call" | custom-call | tf_op jit(solution)/shard_map/load/pallas_call | solution.py:230
  1.6 0.0 copy-start
  1.7 4.0 %collective-permute-start = (f32[2,1,32,1024]{3,2,1,0:T(8,128)S(1)}, f32[2,1,32,1024]{3,2,1,0:T(8,128)S(1)}, u32[]{:S(2)}, u32[]{:S(2)}) collective-permute-start(f32[2,1,32,1024]{3,2,1,0:T(8,128)S(1)} %get-tuple-element.19), channel_id=1, source_target_pairs={{0,1},{1,0},{2,3},{3,2},{4,5},{5,4},{6,7},{7,6},{8,9},{9,8},{10,11... | collective-permute-start | bytes 786440 | tf_op jit(solution)/shard_map/ppermute | solution.py:389
  5.7 0.7 collective-permute-start.1
  6.4 6.7 %collective-permute-start.2 = (f32[2,8,1,1024]{3,2,1,0:T(1,128)S(1)}, f32[2,8,1,1024]{3,2,1,0:T(1,128)S(1)}, u32[]{:S(2)}, u32[]{:S(2)}) collective-permute-start(f32[2,8,1,1024]{3,2,1,0:T(1,128)S(1)} %get-tuple-element.21), channel_id=1, source_target_pairs={{0,8},{8,0},{16,24},{24,16},{32,40},{40,32},{48,56},{56,48},{64,72... | collective-permute-start | bytes 196616 | tf_op jit(solution)/shard_map/ppermute | solution.py:389
  13.1 1.9 %collective-permute-start.3 = (f32[2,8,1,1024]{3,2,1,0:T(1,128)S(1)}, f32[2,8,1,1024]{3,2,1,0:T(1,128)S(1)}, u32[]{:S(2)}, u32[]{:S(2)}) collective-permute-start(f32[2,8,1,1024]{3,2,1,0:T(1,128)S(1)} %get-tuple-element.22), channel_id=1, source_target_pairs={{8,16},{16,8},{24,32},{32,24},{40,48},{48,40},{56,64},{64,56},{72,... | collective-permute-start | bytes 196616 | tf_op jit(solution)/shard_map/ppermute | solution.py:389
  15.0 3.5 %march_inner.1 = (s32[2,8,32,1024]{3,2,1,0:T(8,128)S(1)}, f32[2,8,32,1024]{3,2,1,0:T(8,128)S(1)}, f32[8,4,16,128]{3,2,1,0:T(8,128)S(1)}) custom-call(s32[2,8,32,1024]{3,2,1,0:T(8,128)} %bins.1, f32[2,8,32,1024]{3,2,1,0:T(8,128)S(1)} %get-tuple-element.15.cells, s32[2,2,2,8,128]{4,3,2,1,0:T(8,128)S(1)} %get-tuple-element.16.tab, ...), custom_call_target="tpu_custom_call" | custom-call | flops 52428800 | bytes 8388608 | tf_op jit(solution)/shard_map/march_inner/pallas_call | solution.py:257
  18.5 0.0 collective-permute-done.2.xin
  18.5 0.2 collective-permute-done.3.xout
  18.6 0.0 collective-permute-done.zin
  18.6 0.0 collective-permute-done.1.zout
  18.7 0.0 copy-done
  18.7 2.5 %march_outer.1 = f32[8,4,32,128]{3,2,1,0:T(8,128)S(1)} custom-call(s32[1]{0:T(128)} %bitcast.wide.spot, s32[1]{0:T(128)} %bitcast.1.narrow, f32[2,8,32,1024]{3,2,1,0:T(8,128)S(1)} %get-tuple-element.15.cells, f32[2,8,32,1024]{3,2,1,0:T(8,128)S(1)} %get-tuple-element.18.slopes, f32[2,1,32,1024]{3,2,1,0:T(8,128)S(1)} %collective-permute-done.zin, ...), custom_call_target="tpu_custom_call" | custom-call | tf_op jit(solution)/shard_map/march_outer/pallas_call | solution.py:275
  21.2 23.4 %all_to_all.5.parts = f32[8,4,32,128]{3,2,1,0:T(8,128)S(1)} all-to-all(f32[8,4,32,128]{3,2,1,0:T(8,128)S(1)} %march_outer.1), channel_id=1, replica_groups=mesh['wide'=64,'narrow'=8] {'narrow'}, dimensions={0} | all-to-all | bytes 1048576 | tf_op jit(solution)/shard_map/all_to_all | solution.py:400
  44.5 0.8 join.1
  45.3 7.7 %all-gather = f32[8,32,128]{2,1,0:T(8,128)S(1)} all-gather(f32[4,32,128]{2,1,0:T(8,128)S(1)} %join.1), channel_id=2, replica_groups={{0,128},{8,264},{16,144},{24,280},{32,160},{40,296},{48,176},{56,312},{..., dimensions={0}, use_global_device_ids=true | all-gather | bytes 196608 | tf_op jit(solution)/shard_map/all_gather | solution.py:344
  53.0 8.0 %all-gather.1 = f32[4,4,32,128]{3,2,1,0:T(8,128)S(1)} all-gather(f32[2,4,32,128]{3,2,1,0:T(8,128)S(1)} %bitcast.13), channel_id=3, replica_groups={{0,256},{8,40},{16,272},{24,56},{32,288},{48,304},{64,320},{72,104},{80..., dimensions={0}, use_global_device_ids=true | all-gather | bytes 393216 | tf_op jit(solution)/shard_map/all_gather | solution.py:344
  61.0 6.6 %all-gather.2 = f32[4,2,4,32,128]{4,3,2,1,0:T(8,128)S(1)} all-gather(f32[2,2,4,32,128]{4,3,2,1,0:T(8,128)S(1)} %bitcast.12), channel_id=4, replica_groups={{0,64},{8,24},{16,80},{32,96},{40,56},{48,112},{72,88},{104,120},{128,1..., dimensions={0}, use_global_device_ids=true | all-gather | bytes 786432 | tf_op jit(solution)/shard_map/all_gather | solution.py:344
  67.6 4.7 %collective-permute-start.9 = (f32[2,2,2,4,32,128]{5,4,3,2,1,0:T(8,128)S(1)}, f32[2,2,2,4,32,128]{5,4,3,2,1,0:T(8,128)S(1)}, u32[]{:S(2)}, u32[]{:S(2)}) collective-permute-start(f32[2,2,2,4,32,128]{5,4,3,2,1,0:T(8,128)S(1)} %bitcast.7), channel_id=1, source_target_pairs={{0,32},{8,136},{16,48},{24,152},{32,0},{40,168},{48,16},{56,184},{... | collective-permute-start | bytes 1572872 | tf_op jit(solution)/shard_map/ppermute | solution.py:345
  72.4 5.0 %collective-permute-start.7 = (f32[2,2,2,4,32,128]{5,4,3,2,1,0:T(8,128)S(1)}, f32[2,2,2,4,32,128]{5,4,3,2,1,0:T(8,128)S(1)}, u32[]{:S(2)}, u32[]{:S(2)}) collective-permute-start(f32[2,2,2,4,32,128]{5,4,3,2,1,0:T(8,128)S(1)} %bitcast.8), channel_id=1, source_target_pairs={{0,48},{8,456},{16,32},{24,472},{32,16},{40,488},{48,0},{56,504},{... | collective-permute-start | bytes 1572872 | tf_op jit(solution)/shard_map/ppermute | solution.py:345
  77.4 2.6 %collective-permute-start.5 = (f32[2,2,2,4,32,128]{5,4,3,2,1,0:T(8,128)S(1)}, f32[2,2,2,4,32,128]{5,4,3,2,1,0:T(8,128)S(1)}, u32[]{:S(2)}, u32[]{:S(2)}) collective-permute-start(f32[2,2,2,4,32,128]{5,4,3,2,1,0:T(8,128)S(1)} %bitcast.9), channel_id=1, source_target_pairs={{0,16},{8,72},{16,0},{24,88},{32,48},{40,104},{48,32},{56,120},{64... | collective-permute-start | bytes 1572872 | tf_op jit(solution)/shard_map/ppermute | solution.py:345
  80.0 3.6 %collective-permute-start.4 = (f32[2,2,2,4,32,128]{5,4,3,2,1,0:T(8,128)S(1)}, f32[2,2,2,4,32,128]{5,4,3,2,1,0:T(8,128)S(1)}, u32[]{:S(2)}, u32[]{:S(2)}) collective-permute-start(f32[2,2,2,4,32,128]{5,4,3,2,1,0:T(8,128)S(1)} %bitcast.10), channel_id=1, source_target_pairs={{0,8},{8,0},{16,24},{24,16},{32,40},{40,32},{48,56},{56,48},{64,72... | collective-permute-start | bytes 1572872 | tf_op jit(solution)/shard_map/ppermute | solution.py:402
  83.6 0.0 collective-permute-done.9.refs_3_
  83.6 2.7 %collective-permute-start.10 = (f32[2,2,2,4,32,128]{5,4,3,2,1,0:T(8,128)S(1)}, f32[2,2,2,4,32,128]{5,4,3,2,1,0:T(8,128)S(1)}, u32[]{:S(2)}, u32[]{:S(2)}) collective-permute-start(f32[2,2,2,4,32,128]{5,4,3,2,1,0:T(8,128)S(1)} %collective-permute-done.9.refs_3_), channel_id=1, source_target_pairs={{0,8},{8,0},{16,24},{24,16},{32,40},{40,32},{48,56},{56,48},{64,72... | collective-permute-start | bytes 1572872 | tf_op jit(solution)/shard_map/ppermute | solution.py:402
  86.3 1.6 %collective-permute-done.7.refs_2_ = f32[2,2,2,4,32,128]{5,4,3,2,1,0:T(8,128)S(1)} collective-permute-done((f32[2,2,2,4,32,128]{5,4,3,2,1,0:T(8,128)S(1)}, f32[2,2,2,4,32,128]{5,4,3,2,1,0:T(8,128)S(1)}, u32[]{:S(2)}, u32[]{:S(2)}) %collective-permute-start.7) | collective-permute-done | bytes 524320 | tf_op jit(solution)/shard_map/ppermute | solution.py:345
  87.9 3.9 %collective-permute-start.8 = (f32[2,2,2,4,32,128]{5,4,3,2,1,0:T(8,128)S(1)}, f32[2,2,2,4,32,128]{5,4,3,2,1,0:T(8,128)S(1)}, u32[]{:S(2)}, u32[]{:S(2)}) collective-permute-start(f32[2,2,2,4,32,128]{5,4,3,2,1,0:T(8,128)S(1)} %collective-permute-done.7.refs_2_), channel_id=1, source_target_pairs={{0,8},{8,0},{16,24},{24,16},{32,40},{40,32},{48,56},{56,48},{64,72... | collective-permute-start | bytes 1572872 | tf_op jit(solution)/shard_map/ppermute | solution.py:402
  91.8 0.0 collective-permute-done.5.refs_1_
  91.8 1.9 %collective-permute-start.6 = (f32[2,2,2,4,32,128]{5,4,3,2,1,0:T(8,128)S(1)}, f32[2,2,2,4,32,128]{5,4,3,2,1,0:T(8,128)S(1)}, u32[]{:S(2)}, u32[]{:S(2)}) collective-permute-start(f32[2,2,2,4,32,128]{5,4,3,2,1,0:T(8,128)S(1)} %collective-permute-done.5.refs_1_), channel_id=1, source_target_pairs={{0,8},{8,0},{16,24},{24,16},{32,40},{40,32},{48,56},{56,48},{64,72... | collective-permute-start | bytes 1572872 | tf_op jit(solution)/shard_map/ppermute | solution.py:402
  93.7 1.3 %place.2.refs_4_ = f32[4,8,4,2,32,128]{5,4,3,2,1,0:T(8,128)} custom-call(s32[1]{0:T(128)} %bitcast.wide.spot, f32[2,2,2,4,32,128]{5,4,3,2,1,0:T(8,128)S(1)} %bitcast.11, f32[2,2,2,4,32,128]{5,4,3,2,1,0:T(8,128)S(1)} %collective-permute-done.5.refs_1_, f32[2,2,2,4,32,128]{5,4,3,2,1,0:T(8,128)S(1)} %collective-permute-done.7.refs_2_, ...), custom_call_target="tpu_custom_call" | custom-call | bytes 4194304 | tf_op jit(solution)/shard_map/place/pallas_call | solution.py:373
  95.0 0.0 collective-permute-done.4.refs_0_
  95.0 0.0 collective-permute-done.10.refs_3_
  95.1 0.0 collective-permute-done.8.refs_2_
  95.1 0.5 collective-permute-done.6.refs_1_
  95.6 1.3 %place.3 = f32[4,8,4,2,32,128]{5,4,3,2,1,0:T(8,128)} custom-call(s32[1]{0:T(128)} %bitcast.wide.spot, f32[2,2,2,4,32,128]{5,4,3,2,1,0:T(8,128)S(1)} %collective-permute-done.4.refs_0_, f32[2,2,2,4,32,128]{5,4,3,2,1,0:T(8,128)S(1)} %collective-permute-done.6.refs_1_, ...), custom_call_target="tpu_custom_call", output_to_operand_aliasing={{}: (5, {})} | custom-call | bytes 4194304 | tf_op jit(solution)/shard_map/place/pallas_call | solution.py:373
Async XLA Ops:
  1.6 17.0 %copy-start = (s32[32,128]{1,0:T(8,128)}, s32[32,128]{1,0:T(8,128)S(1)}, u32[]{:S(2)}) copy-start(s32[32,128]{1,0:T(8,128)S(1)} %get-tuple-element.17.back) | copy-start | bytes 49156
  1.7 17.0 %collective-permute-start = (f32[2,1,32,1024]{3,2,1,0:T(8,128)S(1)}, f32[2,1,32,1024]{3,2,1,0:T(8,128)S(1)}, u32[]{:S(2)}, u32[]{:S(2)}) collective-permute-start(f32[2,1,32,1024]{3,2,1,0:T(8,128)S(1)} %get-tuple-element.19), channel_id=1, source_target_pairs={{0,1},{1,0},{2,3},{3,2},{4,5},{5,4},{6,7},{7,6},{8,9},{9,8},{10,11... | collective-permute-start | bytes 786440 | tf_op jit(solution)/shard_map/ppermute | solution.py:389
  5.7 13.0 %collective-permute-start.1 = (f32[2,1,32,1024]{3,2,1,0:T(8,128)S(1)}, f32[2,1,32,1024]{3,2,1,0:T(8,128)S(1)}, u32[]{:S(2)}, u32[]{:S(2)}) collective-permute-start(f32[2,1,32,1024]{3,2,1,0:T(8,128)S(1)} %get-tuple-element.20), channel_id=1, source_target_pairs={{1,2},{2,1},{3,4},{4,3},{5,6},{6,5},{9,10},{10,9},{11,12},{12,11},... | collective-permute-start | bytes 786440 | tf_op jit(solution)/shard_map/ppermute | solution.py:389
  6.4 12.1 %collective-permute-start.2 = (f32[2,8,1,1024]{3,2,1,0:T(1,128)S(1)}, f32[2,8,1,1024]{3,2,1,0:T(1,128)S(1)}, u32[]{:S(2)}, u32[]{:S(2)}) collective-permute-start(f32[2,8,1,1024]{3,2,1,0:T(1,128)S(1)} %get-tuple-element.21), channel_id=1, source_target_pairs={{0,8},{8,0},{16,24},{24,16},{32,40},{40,32},{48,56},{56,48},{64,72... | collective-permute-start | bytes 196616 | tf_op jit(solution)/shard_map/ppermute | solution.py:389
  13.1 5.6 %collective-permute-start.3 = (f32[2,8,1,1024]{3,2,1,0:T(1,128)S(1)}, f32[2,8,1,1024]{3,2,1,0:T(1,128)S(1)}, u32[]{:S(2)}, u32[]{:S(2)}) collective-permute-start(f32[2,8,1,1024]{3,2,1,0:T(1,128)S(1)} %get-tuple-element.22), channel_id=1, source_target_pairs={{8,16},{16,8},{24,32},{32,24},{40,48},{48,40},{56,64},{64,56},{72,... | collective-permute-start | bytes 196616 | tf_op jit(solution)/shard_map/ppermute | solution.py:389
  67.6 16.0 %collective-permute-start.9 = (f32[2,2,2,4,32,128]{5,4,3,2,1,0:T(8,128)S(1)}, f32[2,2,2,4,32,128]{5,4,3,2,1,0:T(8,128)S(1)}, u32[]{:S(2)}, u32[]{:S(2)}) collective-permute-start(f32[2,2,2,4,32,128]{5,4,3,2,1,0:T(8,128)S(1)} %bitcast.7), channel_id=1, source_target_pairs={{0,32},{8,136},{16,48},{24,152},{32,0},{40,168},{48,16},{56,184},{... | collective-permute-start | bytes 1572872 | tf_op jit(solution)/shard_map/ppermute | solution.py:345
  72.4 15.5 %collective-permute-start.7 = (f32[2,2,2,4,32,128]{5,4,3,2,1,0:T(8,128)S(1)}, f32[2,2,2,4,32,128]{5,4,3,2,1,0:T(8,128)S(1)}, u32[]{:S(2)}, u32[]{:S(2)}) collective-permute-start(f32[2,2,2,4,32,128]{5,4,3,2,1,0:T(8,128)S(1)} %bitcast.8), channel_id=1, source_target_pairs={{0,48},{8,456},{16,32},{24,472},{32,16},{40,488},{48,0},{56,504},{... | collective-permute-start | bytes 1572872 | tf_op jit(solution)/shard_map/ppermute | solution.py:345
  77.4 14.4 %collective-permute-start.5 = (f32[2,2,2,4,32,128]{5,4,3,2,1,0:T(8,128)S(1)}, f32[2,2,2,4,32,128]{5,4,3,2,1,0:T(8,128)S(1)}, u32[]{:S(2)}, u32[]{:S(2)}) collective-permute-start(f32[2,2,2,4,32,128]{5,4,3,2,1,0:T(8,128)S(1)} %bitcast.9), channel_id=1, source_target_pairs={{0,16},{8,72},{16,0},{24,88},{32,48},{40,104},{48,32},{56,120},{64... | collective-permute-start | bytes 1572872 | tf_op jit(solution)/shard_map/ppermute | solution.py:345
  80.0 15.1 %collective-permute-start.4 = (f32[2,2,2,4,32,128]{5,4,3,2,1,0:T(8,128)S(1)}, f32[2,2,2,4,32,128]{5,4,3,2,1,0:T(8,128)S(1)}, u32[]{:S(2)}, u32[]{:S(2)}) collective-permute-start(f32[2,2,2,4,32,128]{5,4,3,2,1,0:T(8,128)S(1)} %bitcast.10), channel_id=1, source_target_pairs={{0,8},{8,0},{16,24},{24,16},{32,40},{40,32},{48,56},{56,48},{64,72... | collective-permute-start | bytes 1572872 | tf_op jit(solution)/shard_map/ppermute | solution.py:402
  83.6 11.5 %collective-permute-start.10 = (f32[2,2,2,4,32,128]{5,4,3,2,1,0:T(8,128)S(1)}, f32[2,2,2,4,32,128]{5,4,3,2,1,0:T(8,128)S(1)}, u32[]{:S(2)}, u32[]{:S(2)}) collective-permute-start(f32[2,2,2,4,32,128]{5,4,3,2,1,0:T(8,128)S(1)} %collective-permute-done.9.refs_3_), channel_id=1, source_target_pairs={{0,8},{8,0},{16,24},{24,16},{32,40},{40,32},{48,56},{56,48},{64,72... | collective-permute-start | bytes 1572872 | tf_op jit(solution)/shard_map/ppermute | solution.py:402
  87.9 7.2 %collective-permute-start.8 = (f32[2,2,2,4,32,128]{5,4,3,2,1,0:T(8,128)S(1)}, f32[2,2,2,4,32,128]{5,4,3,2,1,0:T(8,128)S(1)}, u32[]{:S(2)}, u32[]{:S(2)}) collective-permute-start(f32[2,2,2,4,32,128]{5,4,3,2,1,0:T(8,128)S(1)} %collective-permute-done.7.refs_2_), channel_id=1, source_target_pairs={{0,8},{8,0},{16,24},{24,16},{32,40},{40,32},{48,56},{56,48},{64,72... | collective-permute-start | bytes 1572872 | tf_op jit(solution)/shard_map/ppermute | solution.py:402
  91.8 3.8 %collective-permute-start.6 = (f32[2,2,2,4,32,128]{5,4,3,2,1,0:T(8,128)S(1)}, f32[2,2,2,4,32,128]{5,4,3,2,1,0:T(8,128)S(1)}, u32[]{:S(2)}, u32[]{:S(2)}) collective-permute-start(f32[2,2,2,4,32,128]{5,4,3,2,1,0:T(8,128)S(1)} %collective-permute-done.5.refs_1_), channel_id=1, source_target_pairs={{0,8},{8,0},{16,24},{24,16},{32,40},{40,32},{48,56},{56,48},{64,72... | collective-permute-start | bytes 1572872 | tf_op jit(solution)/shard_map/ppermute | solution.py:402

commit v9 on v8

--- a/solution.py
+++ b/solution.py
@@ -304,7 +304,6 @@
 
 
 Z, X, CORES = 8, 4, 2
-PIECES = 4
 
 
 def device(z, x, core):
@@ -339,48 +338,53 @@
 SWAP = everywhere(lambda z, x, core: (z, x, 1 - core))
 
 
-def gather(block):
-    for groups in DOUBLINGS:
-        block = lax.all_gather(block, "wide", axis_index_groups=groups)
-    return [block] + [lax.ppermute(block, "wide", move) for move in MOVES]
-
-
-def place_kernel(swapped, spot, *refs):
-    pieces, out, sem = refs[:PIECES], refs[-2], refs[-1]
+def place_kernel(plan, spot, *refs):
+    pieces, out, sem = refs[: len(plan)], refs[-2], refs[-1]
     wide = spot[0]
-    core = (wide + swapped) % CORES
     x, z = wide // CORES % X, wide // (CORES * X)
     copies = []
-    for piece in range(PIECES):
-        steps = (0, 1 - 2 * (z % 2), 2 * (z % 2) - 1, 2), (0, 1 - 2 * (x % 2), 2 * (x % 2) - 1, 2)
-        z_from, x_from = (z + Z + steps[0][piece]) % (Z // 2), (x + X + steps[1][piece]) % X
+    for ref, (piece, swapped) in zip(pieces, plan):
+        core = (wide + swapped) % CORES
+        z_from, x_from = (place + (0, 1 - 2 * (place % 2), 2 * (place % 2) - 1, 2)[piece] for place in (z + Z, x + X))
+        z_from, x_from = z_from % (Z // 2), x_from % X
         for third in range(2):
             for second in range(2):
                 for first in range(2):
                     z_now = jnp.where(core == 0, 2 * first + 4 * second + third, 4 * first + z_from)
                     x_now = jnp.where(core == 0, x_from, 2 * second + third)
                     target = out.at[:, z_now, x_now, core]
-                    copies.append(pltpu.make_async_copy(pieces[piece].at[third, second, first], target, sem))
+                    copies.append(pltpu.make_async_copy(ref.at[third, second, first], target, sem))
     for copy in copies:
         copy.start()
     for copy in copies:
         copy.wait()
 
 
-def place(pieces, spot, swapped, frame=None):
+def place(plan, pieces, spot, frame=None):
     channels, cols, rows = pieces[0].shape[3:]
     kept = [] if frame is None else [frame]
     return pl.pallas_call(
-        functools.partial(place_kernel, swapped),
-        in_specs=[SMEM] + [VMEM] * PIECES + [ANY] * len(kept),
+        functools.partial(place_kernel, plan),
+        in_specs=[SMEM] + [VMEM] * len(pieces) + [ANY] * len(kept),
         out_specs=ANY,
         out_shape=jax.ShapeDtypeStruct((channels, Z, X, CORES, cols, rows), jnp.float32),
         scratch_shapes=[pltpu.SemaphoreType.DMA],
-        input_output_aliases={1 + PIECES: 0} if kept else {},
+        input_output_aliases={1 + len(pieces): 0} if kept else {},
         compiler_params=pltpu.CompilerParams(vmem_limit_bytes=2**20),
         cost_estimate=pl.CostEstimate(flops=0, bytes_accessed=4 * 2**20, transcendentals=0),
         name="place",
     )(spot, *(pltpu.with_memory_space_constraint(piece, pltpu.VMEM) for piece in pieces), *kept)
+
+
+def gather(block, wide):
+    for groups in DOUBLINGS:
+        block = lax.all_gather(block, "wide", axis_index_groups=groups)
+    pieces = [block] + [lax.ppermute(block, "wide", move) for move in MOVES]
+    swapped = [lax.ppermute(piece, "wide", SWAP) for piece in pieces]
+    early, late = (0, 3), (1, 2)
+    plan = tuple((piece, 0) for piece in range(4)) + tuple((piece, 1) for piece in early)
+    frame = place(plan, pieces + [swapped[piece] for piece in early], wide)
+    return place(tuple((piece, 1) for piece in late), [swapped[piece] for piece in late], wide, frame)
 
 
 def change(inner, outer, axis):
@@ -398,9 +402,7 @@
     picks, slopes, mid = march_inner(field_bins, cells, tab, back)
     partial = march_outer(wide, narrow, cells, slopes, zin, zout, xin, xout, picks, mid, tab, back)
     partial = lax.all_to_all(partial, "narrow", 0, 0)
-    own = gather(join(partial, back))
-    other = [lax.ppermute(piece, "wide", SWAP) for piece in own]
-    frame = place(other, wide, 1, place(own, wide, 0))
+    frame = gather(join(partial, back), wide)
     return frame.reshape(frame.shape[0], -1, frame.shape[-1])
 
 

time: 97.4 us -> 97.1 us (level)
  no operation moved by 1% of the time
where the time goes in v9:
time: 97.1 us; the launch traced here: 96.5 us
  blocking collectives  45.7 us (47%)
  starting transfers between devices  37.7 us (39%)
  Pallas kernels  11 us (11%)
  waiting for transfers between devices  1.95 us (2%)
    all_to_all x1, blocking collectives, on_device(): partial = lax.all_to_all(partial, 'narrow', 0, 0)  23.4 us
    all_gather x3, blocking collectives, gather(): block = lax.all_gather(block, 'wide', axis_index_groups=groups)  22.3 us
    ppermute x3, starting transfers between devices, gather(): pieces = [block] + [lax.ppermute(block, 'wide', move) for move in MOVES]  12.3 us
    ppermute x4, starting transfers between devices, gather(): swapped = [lax.ppermute(piece, 'wide', SWAP) for piece in pieces]  12.1 us
    ppermute x2, starting transfers between devices, change(): lax.ppermute(inner, axis, [(i, i ^ 1) for i in range(count)])  10.7 us
    pallas_call x1, Pallas kernels, march_inner(): pl.pallas_call(inner_kernel, out_shape=[pltpu.VMEM((2, depth, cols, rows)...  3.49 us
    pallas_call x2, Pallas kernels, place(): pl.pallas_call(functools.partial(place_kernel, plan), in_specs=[SMEM] + [...  2.61 us
    ppermute x2, starting transfers between devices, change(): lax.ppermute(outer, axis, route)  2.6 us
  transfers between devices with their start and end apart: 11, of which 3 were waited for; matrix products, arithmetic and copies ran while one was open for 0% of the time, Pallas kernels for 5%

profile of v9, /device:TPU:1, one launch (start us, length us, event | category | flops | bytes accessed | tf_op | source)
XLA Modules:
  0.0 96.5 jit_solution(8403562935545029080)
XLA Ops:
  0.0 1.6 %load.1 = (f32[2,8,32,1024]{3,2,1,0:T(8,128)S(1)}, f32[2,8,1,1024]{3,2,1,0:T(1,128)S(1)}, f32[2,8,1,1024]{3,2,1,0:T(1,128)S(1)}, f32[2,1,32,1024]{3,2,1,0:T(8,12...) custom-call(s32[1]{0:T(128)} %bitcast.wide.spot, ...), custom_call_target="tpu_custom_call" | custom-call | tf_op jit(solution)/shard_map/load/pallas_call | solution.py:230
  1.6 0.0 copy-start
  1.7 4.0 %collective-permute-start = (f32[2,1,32,1024]{3,2,1,0:T(8,128)S(1)}, f32[2,1,32,1024]{3,2,1,0:T(8,128)S(1)}, u32[]{:S(2)}, u32[]{:S(2)}) collective-permute-start(f32[2,1,32,1024]{3,2,1,0:T(8,128)S(1)} %get-tuple-element.19), channel_id=1, source_target_pairs={{0,1},{1,0},{2,3},{3,2},{4,5},{5,4},{6,7},{7,6},{8,9},{9,8},{10,11... | collective-permute-start | bytes 786440 | tf_op jit(solution)/shard_map/ppermute | solution.py:393
  5.7 0.7 collective-permute-start.1
  6.4 6.7 %collective-permute-start.2 = (f32[2,8,1,1024]{3,2,1,0:T(1,128)S(1)}, f32[2,8,1,1024]{3,2,1,0:T(1,128)S(1)}, u32[]{:S(2)}, u32[]{:S(2)}) collective-permute-start(f32[2,8,1,1024]{3,2,1,0:T(1,128)S(1)} %get-tuple-element.21), channel_id=1, source_target_pairs={{0,8},{8,0},{16,24},{24,16},{32,40},{40,32},{48,56},{56,48},{64,72... | collective-permute-start | bytes 196616 | tf_op jit(solution)/shard_map/ppermute | solution.py:393
  13.1 1.9 %collective-permute-start.3 = (f32[2,8,1,1024]{3,2,1,0:T(1,128)S(1)}, f32[2,8,1,1024]{3,2,1,0:T(1,128)S(1)}, u32[]{:S(2)}, u32[]{:S(2)}) collective-permute-start(f32[2,8,1,1024]{3,2,1,0:T(1,128)S(1)} %get-tuple-element.22), channel_id=1, source_target_pairs={{8,16},{16,8},{24,32},{32,24},{40,48},{48,40},{56,64},{64,56},{72,... | collective-permute-start | bytes 196616 | tf_op jit(solution)/shard_map/ppermute | solution.py:393
  15.0 3.5 %march_inner.1 = (s32[2,8,32,1024]{3,2,1,0:T(8,128)S(1)}, f32[2,8,32,1024]{3,2,1,0:T(8,128)S(1)}, f32[8,4,16,128]{3,2,1,0:T(8,128)S(1)}) custom-call(s32[2,8,32,1024]{3,2,1,0:T(8,128)} %bins.1, f32[2,8,32,1024]{3,2,1,0:T(8,128)S(1)} %get-tuple-element.15.cells, s32[2,2,2,8,128]{4,3,2,1,0:T(8,128)S(1)} %get-tuple-element.16.tab, ...), custom_call_target="tpu_custom_call" | custom-call | flops 52428800 | bytes 8388608 | tf_op jit(solution)/shard_map/march_inner/pallas_call | solution.py:257
  18.5 0.0 collective-permute-done.2.xin
  18.5 0.2 collective-permute-done.3.xout
  18.6 0.0 collective-permute-done.zin
  18.6 0.0 collective-permute-done.1.zout
  18.7 0.0 copy-done
  18.7 2.5 %march_outer.1 = f32[8,4,32,128]{3,2,1,0:T(8,128)S(1)} custom-call(s32[1]{0:T(128)} %bitcast.wide.spot, s32[1]{0:T(128)} %bitcast.1.narrow, f32[2,8,32,1024]{3,2,1,0:T(8,128)S(1)} %get-tuple-element.15.cells, f32[2,8,32,1024]{3,2,1,0:T(8,128)S(1)} %get-tuple-element.18.slopes, f32[2,1,32,1024]{3,2,1,0:T(8,128)S(1)} %collective-permute-done.zin, ...), custom_call_target="tpu_custom_call" | custom-call | tf_op jit(solution)/shard_map/march_outer/pallas_call | solution.py:275
  21.2 23.4 %all_to_all.5.parts = f32[8,4,32,128]{3,2,1,0:T(8,128)S(1)} all-to-all(f32[8,4,32,128]{3,2,1,0:T(8,128)S(1)} %march_outer.1), channel_id=1, replica_groups=mesh['wide'=64,'narrow'=8] {'narrow'}, dimensions={0} | all-to-all | bytes 1048576 | tf_op jit(solution)/shard_map/all_to_all | solution.py:404
  44.5 0.8 join.1
  45.3 7.7 %all-gather = f32[8,32,128]{2,1,0:T(8,128)S(1)} all-gather(f32[4,32,128]{2,1,0:T(8,128)S(1)} %join.1), channel_id=2, replica_groups={{0,128},{8,264},{16,144},{24,280},{32,160},{40,296},{48,176},{56,312},{..., dimensions={0}, use_global_device_ids=true | all-gather | bytes 196608 | tf_op jit(solution)/shard_map/all_gather | solution.py:381
  53.0 8.0 %all-gather.1 = f32[4,4,32,128]{3,2,1,0:T(8,128)S(1)} all-gather(f32[2,4,32,128]{3,2,1,0:T(8,128)S(1)} %bitcast.13), channel_id=3, replica_groups={{0,256},{8,40},{16,272},{24,56},{32,288},{48,304},{64,320},{72,104},{80..., dimensions={0}, use_global_device_ids=true | all-gather | bytes 393216 | tf_op jit(solution)/shard_map/all_gather | solution.py:381
  61.0 6.6 %all-gather.2 = f32[4,2,4,32,128]{4,3,2,1,0:T(8,128)S(1)} all-gather(f32[2,2,4,32,128]{4,3,2,1,0:T(8,128)S(1)} %bitcast.12), channel_id=4, replica_groups={{0,64},{8,24},{16,80},{32,96},{40,56},{48,112},{72,88},{104,120},{128,1..., dimensions={0}, use_global_device_ids=true | all-gather | bytes 786432 | tf_op jit(solution)/shard_map/all_gather | solution.py:381
  67.6 4.7 %collective-permute-start.8 = (f32[2,2,2,4,32,128]{5,4,3,2,1,0:T(8,128)S(1)}, f32[2,2,2,4,32,128]{5,4,3,2,1,0:T(8,128)S(1)}, u32[]{:S(2)}, u32[]{:S(2)}) collective-permute-start(f32[2,2,2,4,32,128]{5,4,3,2,1,0:T(8,128)S(1)} %bitcast.7), channel_id=1, source_target_pairs={{0,32},{8,136},{16,48},{24,152},{32,0},{40,168},{48,16},{56,184},{... | collective-permute-start | bytes 1572872 | tf_op jit(solution)/shard_map/ppermute | solution.py:382
  72.4 5.0 %collective-permute-start.6 = (f32[2,2,2,4,32,128]{5,4,3,2,1,0:T(8,128)S(1)}, f32[2,2,2,4,32,128]{5,4,3,2,1,0:T(8,128)S(1)}, u32[]{:S(2)}, u32[]{:S(2)}) collective-permute-start(f32[2,2,2,4,32,128]{5,4,3,2,1,0:T(8,128)S(1)} %bitcast.8), channel_id=1, source_target_pairs={{0,48},{8,456},{16,32},{24,472},{32,16},{40,488},{48,0},{56,504},{... | collective-permute-start | bytes 1572872 | tf_op jit(solution)/shard_map/ppermute | solution.py:382
  77.4 2.6 %collective-permute-start.4 = (f32[2,2,2,4,32,128]{5,4,3,2,1,0:T(8,128)S(1)}, f32[2,2,2,4,32,128]{5,4,3,2,1,0:T(8,128)S(1)}, u32[]{:S(2)}, u32[]{:S(2)}) collective-permute-start(f32[2,2,2,4,32,128]{5,4,3,2,1,0:T(8,128)S(1)} %bitcast.9), channel_id=1, source_target_pairs={{0,16},{8,72},{16,0},{24,88},{32,48},{40,104},{48,32},{56,120},{64... | collective-permute-start | bytes 1572872 | tf_op jit(solution)/shard_map/ppermute | solution.py:382
  80.0 3.6 %collective-permute-start.9 = (f32[2,2,2,4,32,128]{5,4,3,2,1,0:T(8,128)S(1)}, f32[2,2,2,4,32,128]{5,4,3,2,1,0:T(8,128)S(1)}, u32[]{:S(2)}, u32[]{:S(2)}) collective-permute-start(f32[2,2,2,4,32,128]{5,4,3,2,1,0:T(8,128)S(1)} %bitcast.10), channel_id=1, source_target_pairs={{0,8},{8,0},{16,24},{24,16},{32,40},{40,32},{48,56},{56,48},{64,72... | collective-permute-start | bytes 1572872 | tf_op jit(solution)/shard_map/ppermute | solution.py:383
  83.6 0.0 collective-permute-done.8.refs_3_
  83.6 2.7 %collective-permute-start.10 = (f32[2,2,2,4,32,128]{5,4,3,2,1,0:T(8,128)S(1)}, f32[2,2,2,4,32,128]{5,4,3,2,1,0:T(8,128)S(1)}, u32[]{:S(2)}, u32[]{:S(2)}) collective-permute-start(f32[2,2,2,4,32,128]{5,4,3,2,1,0:T(8,128)S(1)} %collective-permute-done.8.refs_3_), channel_id=1, source_target_pairs={{0,8},{8,0},{16,24},{24,16},{32,40},{40,32},{48,56},{56,48},{64,72... | collective-permute-start | bytes 1572872 | tf_op jit(solution)/shard_map/ppermute | solution.py:383
  86.3 1.6 %collective-permute-done.6.refs_2_ = f32[2,2,2,4,32,128]{5,4,3,2,1,0:T(8,128)S(1)} collective-permute-done((f32[2,2,2,4,32,128]{5,4,3,2,1,0:T(8,128)S(1)}, f32[2,2,2,4,32,128]{5,4,3,2,1,0:T(8,128)S(1)}, u32[]{:S(2)}, u32[]{:S(2)}) %collective-permute-start.6) | collective-permute-done | bytes 524320 | tf_op jit(solution)/shard_map/ppermute | solution.py:382
  87.9 3.9 %collective-permute-start.7 = (f32[2,2,2,4,32,128]{5,4,3,2,1,0:T(8,128)S(1)}, f32[2,2,2,4,32,128]{5,4,3,2,1,0:T(8,128)S(1)}, u32[]{:S(2)}, u32[]{:S(2)}) collective-permute-start(f32[2,2,2,4,32,128]{5,4,3,2,1,0:T(8,128)S(1)} %collective-permute-done.6.refs_2_), channel_id=1, source_target_pairs={{0,8},{8,0},{16,24},{24,16},{32,40},{40,32},{48,56},{56,48},{64,72... | collective-permute-start | bytes 1572872 | tf_op jit(solution)/shard_map/ppermute | solution.py:383
  91.8 0.0 collective-permute-done.4.refs_1_
  91.8 1.9 %collective-permute-start.5 = (f32[2,2,2,4,32,128]{5,4,3,2,1,0:T(8,128)S(1)}, f32[2,2,2,4,32,128]{5,4,3,2,1,0:T(8,128)S(1)}, u32[]{:S(2)}, u32[]{:S(2)}) collective-permute-start(f32[2,2,2,4,32,128]{5,4,3,2,1,0:T(8,128)S(1)} %collective-permute-done.4.refs_1_), channel_id=1, source_target_pairs={{0,8},{8,0},{16,24},{24,16},{32,40},{40,32},{48,56},{56,48},{64,72... | collective-permute-start | bytes 1572872 | tf_op jit(solution)/shard_map/ppermute | solution.py:383
  93.7 0.0 collective-permute-done.9.refs_4_
  93.7 0.0 collective-permute-done.10.refs_5_
  93.7 1.7 %place.2.refs_2_ = f32[4,8,4,2,32,128]{5,4,3,2,1,0:T(8,128)} custom-call(s32[1]{0:T(128)} %bitcast.wide.spot, f32[2,2,2,4,32,128]{5,4,3,2,1,0:T(8,128)S(1)} %bitcast.11, f32[2,2,2,4,32,128]{5,4,3,2,1,0:T(8,128)S(1)} %collective-permute-done.4.refs_1_, f32[2,2,2,4,32,128]{5,4,3,2,1,0:T(8,128)S(1)} %collective-permute-done.6.refs_2_, ...), custom_call_target="tpu_custom_call" | custom-call | bytes 4194304 | tf_op jit(solution)/shard_map/place/pallas_call | solution.py:366
  95.4 0.0 collective-permute-done.7.refs_1_
  95.4 0.2 collective-permute-done.5.refs_0_
  95.6 1.0 place.3
Async XLA Ops:
  1.6 17.0 %copy-start = (s32[32,128]{1,0:T(8,128)}, s32[32,128]{1,0:T(8,128)S(1)}, u32[]{:S(2)}) copy-start(s32[32,128]{1,0:T(8,128)S(1)} %get-tuple-element.17.back) | copy-start | bytes 49156
  1.7 17.0 %collective-permute-start = (f32[2,1,32,1024]{3,2,1,0:T(8,128)S(1)}, f32[2,1,32,1024]{3,2,1,0:T(8,128)S(1)}, u32[]{:S(2)}, u32[]{:S(2)}) collective-permute-start(f32[2,1,32,1024]{3,2,1,0:T(8,128)S(1)} %get-tuple-element.19), channel_id=1, source_target_pairs={{0,1},{1,0},{2,3},{3,2},{4,5},{5,4},{6,7},{7,6},{8,9},{9,8},{10,11... | collective-permute-start | bytes 786440 | tf_op jit(solution)/shard_map/ppermute | solution.py:393
  5.7 13.0 %collective-permute-start.1 = (f32[2,1,32,1024]{3,2,1,0:T(8,128)S(1)}, f32[2,1,32,1024]{3,2,1,0:T(8,128)S(1)}, u32[]{:S(2)}, u32[]{:S(2)}) collective-permute-start(f32[2,1,32,1024]{3,2,1,0:T(8,128)S(1)} %get-tuple-element.20), channel_id=1, source_target_pairs={{1,2},{2,1},{3,4},{4,3},{5,6},{6,5},{9,10},{10,9},{11,12},{12,11},... | collective-permute-start | bytes 786440 | tf_op jit(solution)/shard_map/ppermute | solution.py:393
  6.4 12.1 %collective-permute-start.2 = (f32[2,8,1,1024]{3,2,1,0:T(1,128)S(1)}, f32[2,8,1,1024]{3,2,1,0:T(1,128)S(1)}, u32[]{:S(2)}, u32[]{:S(2)}) collective-permute-start(f32[2,8,1,1024]{3,2,1,0:T(1,128)S(1)} %get-tuple-element.21), channel_id=1, source_target_pairs={{0,8},{8,0},{16,24},{24,16},{32,40},{40,32},{48,56},{56,48},{64,72... | collective-permute-start | bytes 196616 | tf_op jit(solution)/shard_map/ppermute | solution.py:393
  13.1 5.6 %collective-permute-start.3 = (f32[2,8,1,1024]{3,2,1,0:T(1,128)S(1)}, f32[2,8,1,1024]{3,2,1,0:T(1,128)S(1)}, u32[]{:S(2)}, u32[]{:S(2)}) collective-permute-start(f32[2,8,1,1024]{3,2,1,0:T(1,128)S(1)} %get-tuple-element.22), channel_id=1, source_target_pairs={{8,16},{16,8},{24,32},{32,24},{40,48},{48,40},{56,64},{64,56},{72,... | collective-permute-start | bytes 196616 | tf_op jit(solution)/shard_map/ppermute | solution.py:393
  67.6 16.0 %collective-permute-start.8 = (f32[2,2,2,4,32,128]{5,4,3,2,1,0:T(8,128)S(1)}, f32[2,2,2,4,32,128]{5,4,3,2,1,0:T(8,128)S(1)}, u32[]{:S(2)}, u32[]{:S(2)}) collective-permute-start(f32[2,2,2,4,32,128]{5,4,3,2,1,0:T(8,128)S(1)} %bitcast.7), channel_id=1, source_target_pairs={{0,32},{8,136},{16,48},{24,152},{32,0},{40,168},{48,16},{56,184},{... | collective-permute-start | bytes 1572872 | tf_op jit(solution)/shard_map/ppermute | solution.py:382
  72.4 15.5 %collective-permute-start.6 = (f32[2,2,2,4,32,128]{5,4,3,2,1,0:T(8,128)S(1)}, f32[2,2,2,4,32,128]{5,4,3,2,1,0:T(8,128)S(1)}, u32[]{:S(2)}, u32[]{:S(2)}) collective-permute-start(f32[2,2,2,4,32,128]{5,4,3,2,1,0:T(8,128)S(1)} %bitcast.8), channel_id=1, source_target_pairs={{0,48},{8,456},{16,32},{24,472},{32,16},{40,488},{48,0},{56,504},{... | collective-permute-start | bytes 1572872 | tf_op jit(solution)/shard_map/ppermute | solution.py:382
  77.4 14.4 %collective-permute-start.4 = (f32[2,2,2,4,32,128]{5,4,3,2,1,0:T(8,128)S(1)}, f32[2,2,2,4,32,128]{5,4,3,2,1,0:T(8,128)S(1)}, u32[]{:S(2)}, u32[]{:S(2)}) collective-permute-start(f32[2,2,2,4,32,128]{5,4,3,2,1,0:T(8,128)S(1)} %bitcast.9), channel_id=1, source_target_pairs={{0,16},{8,72},{16,0},{24,88},{32,48},{40,104},{48,32},{56,120},{64... | collective-permute-start | bytes 1572872 | tf_op jit(solution)/shard_map/ppermute | solution.py:382
  80.0 13.8 %collective-permute-start.9 = (f32[2,2,2,4,32,128]{5,4,3,2,1,0:T(8,128)S(1)}, f32[2,2,2,4,32,128]{5,4,3,2,1,0:T(8,128)S(1)}, u32[]{:S(2)}, u32[]{:S(2)}) collective-permute-start(f32[2,2,2,4,32,128]{5,4,3,2,1,0:T(8,128)S(1)} %bitcast.10), channel_id=1, source_target_pairs={{0,8},{8,0},{16,24},{24,16},{32,40},{40,32},{48,56},{56,48},{64,72... | collective-permute-start | bytes 1572872 | tf_op jit(solution)/shard_map/ppermute | solution.py:383
  83.6 10.1 %collective-permute-start.10 = (f32[2,2,2,4,32,128]{5,4,3,2,1,0:T(8,128)S(1)}, f32[2,2,2,4,32,128]{5,4,3,2,1,0:T(8,128)S(1)}, u32[]{:S(2)}, u32[]{:S(2)}) collective-permute-start(f32[2,2,2,4,32,128]{5,4,3,2,1,0:T(8,128)S(1)} %collective-permute-done.8.refs_3_), channel_id=1, source_target_pairs={{0,8},{8,0},{16,24},{24,16},{32,40},{40,32},{48,56},{56,48},{64,72... | collective-permute-start | bytes 1572872 | tf_op jit(solution)/shard_map/ppermute | solution.py:383
  87.9 7.5 %collective-permute-start.7 = (f32[2,2,2,4,32,128]{5,4,3,2,1,0:T(8,128)S(1)}, f32[2,2,2,4,32,128]{5,4,3,2,1,0:T(8,128)S(1)}, u32[]{:S(2)}, u32[]{:S(2)}) collective-permute-start(f32[2,2,2,4,32,128]{5,4,3,2,1,0:T(8,128)S(1)} %collective-permute-done.6.refs_2_), channel_id=1, source_target_pairs={{0,8},{8,0},{16,24},{24,16},{32,40},{40,32},{48,56},{56,48},{64,72... | collective-permute-start | bytes 1572872 | tf_op jit(solution)/shard_map/ppermute | solution.py:383
  91.8 3.8 %collective-permute-start.5 = (f32[2,2,2,4,32,128]{5,4,3,2,1,0:T(8,128)S(1)}, f32[2,2,2,4,32,128]{5,4,3,2,1,0:T(8,128)S(1)}, u32[]{:S(2)}, u32[]{:S(2)}) collective-permute-start(f32[2,2,2,4,32,128]{5,4,3,2,1,0:T(8,128)S(1)} %collective-permute-done.4.refs_1_), channel_id=1, source_target_pairs={{0,8},{8,0},{16,24},{24,16},{32,40},{40,32},{48,56},{56,48},{64,72... | collective-permute-start | bytes 1572872 | tf_op jit(solution)/shard_map/ppermute | solution.py:383
